TPU v7x, 512 devices: a whole 4x8x8 slice. The times are simulated.
512 devices in a mesh: leaf: 64 (over y, x, z_lo), row: 8 (over z_hi, core).
Axes of the slice: x: 4, y: 8, z: 8 (z_hi: 4, z_lo: 2; z = z_hi * 2 + z_lo), core: 2. Of those that a mesh axis runs over, the one named last changes fastest.
Arguments:
- coupling: bfloat16 [64, 4096, 4096], P('leaf', 'row'), may hold values from -0.0390625 to 0.0390625
- rhs: bfloat16 [64, 4096, 128], P('leaf', 'row'), may hold values from -6 to 6
- left_factors: bfloat16 [64, 4096, 384], P('leaf', 'row'), may hold values from -6 to 6
- right_factors: bfloat16 [64, 4096, 384], P('leaf', 'row'), may hold values from -0.0014648438 to 0.0014648438
Outputs:
- solution: bfloat16 [64, 4096, 128], P('leaf', 'row')
All inputs are finite; a program needn't handle non-finite values.
Results may differ from a plain program's by a relative error of at most 0.001.
Values may be sent and summed in bfloat16 or wider, within the bound.
No kernel may reach another device: no remote copies, remote signals or barrier semaphores. Data moves between devices by JAX's collectives and lax.ppermute only.
A program may use at most 64 MiB of HBM per device.

v0:
```python
import jax
import jax.numpy as jnp
from jax import lax
from jax.sharding import PartitionSpec as P

R = 128
B = 128
LEVELS = 3


def swapped(value, axis, bit):
    return lax.ppermute(value, axis, [(i, i ^ 1 << bit) for i in range(lax.axis_size(axis))])


def node_pair(values, level):
    for bit in range(level):
        values = values + swapped(values, "leaf", bit)
    return (values, swapped(values, "leaf", level))


def solve_dense(system, right):
    highest_precision = lax.Precision.HIGHEST
    normal_matrix = jnp.dot(system.T, system, precision=highest_precision)
    lower = jnp.linalg.cholesky(normal_matrix)
    return jax.scipy.linalg.cho_solve(
        (lower, True), jnp.dot(system.T, right, precision=highest_precision)
    )


def lead_first(values):
    return jnp.concatenate([values[:, B : B + R], values[:, :B], values[:, B + R :]], axis=1)


def drop_lead(values):
    return jnp.concatenate([values[:, :B], values[:, B + R :]], axis=1)


def node_coef(own, other):
    highest_precision = lax.Precision.HIGHEST
    identity = jnp.eye(R, dtype=jnp.float32)
    system = identity - jnp.dot(other[:, :R], own[:, :R], precision=highest_precision)
    right = other[:, R:] - jnp.dot(other[:, :R], own[:, R:], precision=highest_precision)
    return solve_dense(system, right)


def local(coupling, rhs, left_factors, right_factors):
    highest_precision = lax.Precision.HIGHEST
    block = coupling[0]
    local_columns = jnp.concatenate([rhs[0], left_factors[0]], axis=1)
    remaining_blocks = local_columns.astype(jnp.float32) + jnp.dot(
        block,
        lax.all_gather(local_columns, "row", axis=0, tiled=True),
        preferred_element_type=jnp.float32,
    )
    for level in range(LEVELS):
        leading_block = remaining_blocks[:, B : B + R]
        other_blocks = drop_lead(remaining_blocks)
        cholesky_factor = right_factors[0, :, level * R : (level + 1) * R].astype(jnp.float32)
        joined_pieces = lead_first(remaining_blocks)
        partial_value_sum = lax.dot_general(
            cholesky_factor, joined_pieces, (((0,), (0,)), ((), ())), precision=highest_precision
        )
        total = lax.psum(partial_value_sum, "row")
        own, other = node_pair(total, level)
        coef = node_coef(own, other)
        remaining_blocks = other_blocks - jnp.dot(leading_block, coef, precision=highest_precision)
    return remaining_blocks[None].astype(jnp.bfloat16)


def solution(mesh):
    in_specs = (
        P("leaf", "row", None),
        P("leaf", "row", None),
        P("leaf", "row", None),
        P("leaf", "row", None),
    )
    out_specs = P("leaf", "row", None)
    return jax.shard_map(local, mesh=mesh, in_specs=in_specs, out_specs=out_specs, check_vma=False)
```

profile of v0, /device:TPU:6, one launch (start us, length us, event | category | flops | bytes accessed | tf_op | source)
XLA Modules:
  0.0 444.7 jit_solution(15830671054009944002)
XLA Ops:
  9.6 59.0 %all-gather.2.cloned.1.call-done = bf16[4096,512]{0,1:T(8,128)(2,1)} async-done(((bf16[512,512]{0,1:T(8,128)(2,1)}), bf16[4096,512]{0,1:T(8,128)(2,1)}) %all-gather.2.cloned.1.call-update) | async-done | bytes 4194320 | tf_op jit(solution)/shard_map/all_gather | solution.py:52
  68.7 5.8 %fusion.5 = f32[512,512]{0,1:T(8,128)S(1)} fusion(bf16[4096,512]{0,1:T(8,128)(2,1)} %all-gather.2.cloned.1.call-done, bf16[1,512,4096]{2,1,0:T(8,128)(2,1)} %param.5, bf16[512,384]{0,1:T(8,128)(2,1)S(1)} %bitcast.83, bf16[512,128]{0,1:T(8,128)(2,1)S(1)} %bitcast.85), kind=kOutput, calls=%fused_computation.3 | convolution fusion | flops 2148794368 | bytes 9961472 | tf_op jit(solution)/shard_map/dot_general | solution.py:50
  74.6 1.3 convolution_bitcast_fusion
  76.0 78.7 %all-reduce.4.cloned.1.call-done = f32[128,512]{0,1:T(8,128)} async-done(((f32[128,512]{0,1:T(8,128)}), f32[128,512]{0,1:T(8,128)}) %all-reduce.4.cloned.1.call-update) | async-done | bytes 262160 | tf_op jit(solution)/shard_map/psum | solution.py:63
  154.7 2.8 collective-permute-start
  157.5 6.2 %collective-permute-done = f32[128,512]{0,1:T(8,128)S(1)} collective-permute-done((f32[128,512]{0,1:T(8,128)}, f32[128,512]{0,1:T(8,128)S(1)}, u32[]{:S(2)}, u32[]{:S(2)}) %collective-permute-start) | collective-permute-done | bytes 262176 | tf_op jit(solution)/shard_map/ppermute | solution.py:12
  165.2 11.7 %cholesky.59 = f32[128,128]{1,0:T(8,128)S(1)} custom-call(f32[128,128]{1,0:T(8,128)S(1)} %fusion.58), custom_call_target="Cholesky" | custom-call | tf_op jit(solution)/shard_map/jit(cholesky)/cholesky | solution.py:24
  178.3 9.8 %custom-call.23 = f32[1,128,128]{1,2,0:T(8,128)S(1)} custom-call(f32[1,128,128]{2,1,0:T(8,128)S(1)} %fusion.35), custom_call_target="InvertDiagBlocksLowerTriangular" | custom-call | tf_op jit(solution)/shard_map/jit(_cho_solve)/triangular_solve | solution.py:25
  192.6 76.8 %all-reduce.6.cloned.1.call-done = f32[128,384]{0,1:T(8,128)} async-done(((f32[128,384]{0,1:T(8,128)}), f32[128,384]{0,1:T(8,128)}) %all-reduce.6.cloned.1.call-update) | async-done | bytes 196624 | tf_op jit(solution)/shard_map/psum | solution.py:63
  269.4 2.7 collective-permute-start.1
  272.1 5.1 %collective-permute-done.1 = f32[128,384]{0,1:T(8,128)S(1)} collective-permute-done((f32[128,384]{0,1:T(8,128)}, f32[128,384]{0,1:T(8,128)S(1)}, u32[]{:S(2)}, u32[]{:S(2)}) %collective-permute-start.1) | collective-permute-done | bytes 196640 | tf_op jit(solution)/shard_map/ppermute | solution.py:12
  278.1 3.0 collective-permute-start.2
  281.1 4.6 %collective-permute-done.2 = f32[128,384]{0,1:T(8,128)S(1)} collective-permute-done((f32[128,384]{0,1:T(8,128)S(1)}, f32[128,384]{0,1:T(8,128)S(1)}, u32[]{:S(2)}, u32[]{:S(2)}) %collective-permute-start.2) | collective-permute-done | bytes 196640 | tf_op jit(solution)/shard_map/ppermute | solution.py:12
  286.4 11.7 %cholesky.70 = f32[128,128]{1,0:T(8,128)S(1)} custom-call(f32[128,128]{1,0:T(8,128)S(1)} %fusion.53), custom_call_target="Cholesky" | custom-call | tf_op jit(solution)/shard_map/jit(cholesky)/cholesky | solution.py:24
  299.4 9.8 %custom-call.24 = f32[1,128,128]{1,2,0:T(8,128)S(1)} custom-call(f32[1,128,128]{2,1,0:T(8,128)S(1)} %fusion.36), custom_call_target="InvertDiagBlocksLowerTriangular" | custom-call | tf_op jit(solution)/shard_map/jit(_cho_solve)/triangular_solve | solution.py:25
  312.1 77.0 %all-reduce.8.cloned.1.call-done = f32[128,256]{0,1:T(8,128)} async-done(((f32[128,256]{0,1:T(8,128)}), f32[128,256]{0,1:T(8,128)}) %all-reduce.8.cloned.1.call-update) | async-done | bytes 131088 | tf_op jit(solution)/shard_map/psum | solution.py:63
  389.1 2.6 collective-permute-start.3
  391.8 4.4 collective-permute-done.3
  397.1 2.8 collective-permute-start.4
  399.9 4.1 collective-permute-done.4
  404.0 3.6 collective-permute-start.5
  407.6 4.7 %collective-permute-done.5 = f32[128,256]{0,1:T(8,128)S(1)} collective-permute-done((f32[128,256]{0,1:T(8,128)S(1)}, f32[128,256]{0,1:T(8,128)S(1)}, u32[]{:S(2)}, u32[]{:S(2)}) %collective-permute-start.5) | collective-permute-done | bytes 131104 | tf_op jit(solution)/shard_map/ppermute | solution.py:12
  413.1 11.7 %cholesky.81 = f32[128,128]{1,0:T(8,128)S(1)} custom-call(f32[128,128]{1,0:T(8,128)S(1)} %fusion.48), custom_call_target="Cholesky" | custom-call | tf_op jit(solution)/shard_map/jit(cholesky)/cholesky | solution.py:24
  426.1 9.8 %custom-call.25 = f32[1,128,128]{1,2,0:T(8,128)S(1)} custom-call(f32[1,128,128]{2,1,0:T(8,128)S(1)} %fusion.37), custom_call_target="InvertDiagBlocksLowerTriangular" | custom-call | tf_op jit(solution)/shard_map/jit(_cho_solve)/triangular_solve | solution.py:25
  (59 shorter events, 21.4 us)
Async XLA Ops:
  6.5 62.1 %all-gather.2.cloned.1.call-start = ((), (), s32[]{:S(2)}) async-start(), calls=%async_computation | async-start | bytes 4718592 | tf_op jit(solution)/shard_map/all_gather | solution.py:52
  9.6 65.0 %copy-start = (bf16[1,512,384]{2,1,0:T(8,128)(2,1)S(1)}, bf16[1,512,384]{2,1,0:T(8,128)(2,1)}, u32[]{:S(2)}) copy-start(bf16[1,512,384]{2,1,0:T(8,128)(2,1)} %param.8) | copy-start | bytes 1179652
  9.6 145.1 %all-reduce.4.cloned.1.call-start = ((), (), s32[]{:S(2)}) async-start(), calls=%async_computation.1 | async-start | bytes 524288 | tf_op jit(solution)/shard_map/psum | solution.py:63
  75.9 193.4 %all-reduce.6.cloned.1.call-start = ((), (), s32[]{:S(2)}) async-start(), calls=%async_computation.2 | async-start | bytes 393216 | tf_op jit(solution)/shard_map/psum | solution.py:63
  154.7 9.0 %collective-permute-start = (f32[128,512]{0,1:T(8,128)}, f32[128,512]{0,1:T(8,128)S(1)}, u32[]{:S(2)}, u32[]{:S(2)}) collective-permute-start(f32[128,512]{0,1:T(8,128)} %all-reduce.4.cloned.1.call-done), channel_id=1, source_target_pairs={{0,8},{8,0},{16,24},{24,16},{32,40},{40,32},{48,56},{56,48},{64,72... | collective-permute-start | bytes 786440 | tf_op jit(solution)/shard_map/ppermute | solution.py:12
  192.5 196.6 %all-reduce.8.cloned.1.call-start = ((), (), s32[]{:S(2)}) async-start(), calls=%async_computation.3 | async-start | bytes 262144 | tf_op jit(solution)/shard_map/psum | solution.py:63
  269.4 7.8 %collective-permute-start.1 = (f32[128,384]{0,1:T(8,128)}, f32[128,384]{0,1:T(8,128)S(1)}, u32[]{:S(2)}, u32[]{:S(2)}) collective-permute-start(f32[128,384]{0,1:T(8,128)} %all-reduce.6.cloned.1.call-done), channel_id=1, source_target_pairs={{0,8},{8,0},{16,24},{24,16},{32,40},{40,32},{48,56},{56,48},{64,72... | collective-permute-start | bytes 589832 | tf_op jit(solution)/shard_map/ppermute | solution.py:12
  278.1 7.6 %collective-permute-start.2 = (f32[128,384]{0,1:T(8,128)S(1)}, f32[128,384]{0,1:T(8,128)S(1)}, u32[]{:S(2)}, u32[]{:S(2)}) collective-permute-start(f32[128,384]{0,1:T(8,128)S(1)} %add.44), channel_id=1, source_target_pairs={{0,16},{8,24},{16,0},{24,8},{32,48},{40,56},{48,32},{56,40},{64,80... | collective-permute-start | bytes 589832 | tf_op jit(solution)/shard_map/ppermute | solution.py:12
  389.1 7.1 %collective-permute-start.3 = (f32[128,256]{0,1:T(8,128)}, f32[128,256]{0,1:T(8,128)S(1)}, u32[]{:S(2)}, u32[]{:S(2)}) collective-permute-start(f32[128,256]{0,1:T(8,128)} %all-reduce.8.cloned.1.call-done), channel_id=1, source_target_pairs={{0,8},{8,0},{16,24},{24,16},{32,40},{40,32},{48,56},{56,48},{64,72... | collective-permute-start | bytes 393224 | tf_op jit(solution)/shard_map/ppermute | solution.py:12
  397.1 6.9 %collective-permute-start.4 = (f32[128,256]{0,1:T(8,128)S(1)}, f32[128,256]{0,1:T(8,128)S(1)}, u32[]{:S(2)}, u32[]{:S(2)}) collective-permute-start(f32[128,256]{0,1:T(8,128)S(1)} %add.45), channel_id=1, source_target_pairs={{0,16},{8,24},{16,0},{24,8},{32,48},{40,56},{48,32},{56,40},{64,80... | collective-permute-start | bytes 393224 | tf_op jit(solution)/shard_map/ppermute | solution.py:12
  404.0 8.4 %collective-permute-start.5 = (f32[128,256]{0,1:T(8,128)S(1)}, f32[128,256]{0,1:T(8,128)S(1)}, u32[]{:S(2)}, u32[]{:S(2)}) collective-permute-start(f32[128,256]{0,1:T(8,128)S(1)} %add.46), channel_id=1, source_target_pairs={{0,32},{8,40},{16,48},{24,56},{32,0},{40,8},{48,16},{56,24},{64,96... | collective-permute-start | bytes 393224 | tf_op jit(solution)/shard_map/ppermute | solution.py:12
Sparse Core Ops, SparseCore 0:
  9.7 58.9 all-gather.1
  76.1 78.6 all-reduce.3
  192.7 76.6 all-reduce.5
  312.3 76.8 all-reduce.7
where the time goes:
time: 445 us
  waiting for transfers between devices  321 us (72%)
  other arithmetic  71.3 us (16%)
  matrix products  18.2 us (4%)
  starting transfers between devices  17.6 us (4%)
  between operations  13.5 us (3%)
    psum x3, waiting for transfers between devices, local(): total = lax.psum(partial_value_sum, 'row')  233 us
    all_gather x1, waiting for transfers between devices, local(): lax.all_gather(local_columns, 'row', axis=0, tiled=True)  59 us
    another operation x9, other arithmetic, solve_dense(): lower = jnp.linalg.cholesky(normal_matrix)  37.2 us
    another operation x6, other arithmetic, solve_dense(): jax.scipy.linalg.cho_solve((lower, True), jnp.dot(system.T, right, precis...  31.4 us
    ppermute x6, waiting for transfers between devices, swapped(): lax.ppermute(value, axis, [(i, i ^ 1 << bit) for i in range(lax.axis_size...  29.1 us
    ppermute x6, starting transfers between devices, swapped(): lax.ppermute(value, axis, [(i, i ^ 1 << bit) for i in range(lax.axis_size...  17.5 us
  transfers between devices with their start and end apart: 10, of which 10 were waited for; matrix products, arithmetic and copies ran while one was open for 0% of the time, Pallas kernels for 0%

commit v1 on v0

v1 whole, which is shorter than its diff:
```python
import jax
import jax.numpy as jnp
from jax import lax
from jax.experimental import pallas as pl
from jax.experimental.pallas import tpu as pltpu
from jax.sharding import PartitionSpec as P

R = 128
F32 = jnp.float32
BF16 = jnp.bfloat16
VMEM_BYTES = 48 * 1024 * 1024


def dot(a, b):
    return jnp.dot(a, b, precision=lax.Precision.HIGHEST, preferred_element_type=F32)


def solve(s, right, c_ref, p_ref):
    c = right + dot(s, right)
    p = dot(s, s)
    for _ in range(2):
        c = c + dot(p, c)
        p = dot(p, p)
    c_ref[...] = c
    p_ref[...] = p
    left = jnp.sum(p * p)
    good = jnp.logical_and(left < 0.25, jnp.sum(s * s) < 64.0)

    @pl.when(good)
    def _():
        def more(_):
            q = p_ref[...]
            c_ref[...] = c_ref[...] + dot(q, c_ref[...])
            q = dot(q, q)
            p_ref[...] = q
            return jnp.sum(q * q)

        lax.while_loop(lambda size: size > 1e-15, more, left)

    @pl.when(jnp.logical_not(good))
    def _():
        eye = (lax.broadcasted_iota(jnp.int32, (R, R), 0) == lax.broadcasted_iota(jnp.int32, (R, R), 1)).astype(F32)
        a = eye - s
        one = jnp.max(jnp.sum(jnp.abs(a), axis=0))
        most = jnp.max(jnp.sum(jnp.abs(a), axis=1))
        p_ref[...] = (a / one).T / most

        def again(state):
            step, old, new = state
            still = jnp.logical_or(new > 0.01, new < 0.25 * old)
            return jnp.logical_and(step < 200, jnp.logical_and(new > 1e-12, still))

        def newton(state):
            x = p_ref[...]
            res = eye - dot(a, x)
            p_ref[...] = x + dot(x, res)
            return (state[0] + 1, state[2], jnp.sum(res * res))

        lax.while_loop(again, newton, (jnp.int32(0), jnp.float32(1e30), jnp.float32(1e29)))
        x = p_ref[...]
        c_ref[...] = dot(x, right)
        for _ in range(2):
            c_ref[...] = c_ref[...] + dot(x, right - dot(a, c_ref[...]))


def apply_kernel(where_ref, block_ref, cols_ref, own_ref, v_ref, y_ref, keep_ref, send_ref, gram_ref):
    k = pl.program_id(0)

    @pl.when(k == 0)
    def _():
        y_ref[...] = own_ref[...].astype(F32)

    y_ref[...] += jnp.dot(block_ref[...], cols_ref[...], preferred_element_type=F32)

    @pl.when(k == pl.num_programs(0) - 1)
    def _():
        core = where_ref[0]
        rest = y_ref[...]
        total = None
        for _ in range(3):
            piece = rest.astype(BF16)
            rest = rest - piece.astype(F32)
            term = lax.dot_general(v_ref[...], piece, (((0,), (0,)), ((), ())), preferred_element_type=F32)
            total = term if total is None else total + term
        gram_ref[...] = total.reshape(gram_ref.shape)
        keep_ref[...] = gram_ref[core]
        send_ref[...] = gram_ref[1 - core]


def apply_leaf(where, block, gathered, own, v):
    m, width = own.shape
    steps = block.shape[1] // m
    half = v.shape[1] // 2
    return pl.pallas_call(
        apply_kernel,
        grid_spec=pltpu.PrefetchScalarGridSpec(
            num_scalar_prefetch=1,
            grid=(steps,),
            in_specs=[
                pl.BlockSpec((m, m), lambda k, w: (0, k)),
                pl.BlockSpec((m, width), lambda k, w: (k, 0)),
                pl.BlockSpec((m, width), lambda k, w: (0, 0)),
                pl.BlockSpec(v.shape, lambda k, w: (0, 0)),
            ],
            out_specs=[
                pl.BlockSpec((m, width), lambda k, w: (0, 0)),
                pl.BlockSpec((half, width), lambda k, w: (0, 0)),
                pl.BlockSpec((half, width), lambda k, w: (0, 0)),
            ],
            scratch_shapes=[pltpu.VMEM((2, half, width), F32)],
        ),
        out_shape=[
            jax.ShapeDtypeStruct((m, width), F32),
            jax.ShapeDtypeStruct((half, width), F32),
            jax.ShapeDtypeStruct((half, width), F32),
        ],
        compiler_params=pltpu.CompilerParams(vmem_limit_bytes=VMEM_BYTES),
    )(where, block, gathered, own, v)


def first_level(where_ref, own_ref, other_ref, coef_ref, half_ref, full_ref, p_ref):
    core, leaf = where_ref[0], where_ref[1]
    full_ref[core] = own_ref[...]
    full_ref[1 - core] = other_ref[...]
    a, b = leaf, 1 - leaf
    lead = full_ref[0, a, :R, :]
    product = dot(full_ref[0, b, :R, :R], lead)
    right = full_ref[0, b, :R, R:] - product[:, R:]
    solve(product[:, :R], right, coef_ref, p_ref)
    coef = coef_ref[...]
    coef_b = lead[:, R:] - dot(lead[:, :R], coef)

    def update(node, c):
        rows = full_ref[core, node, 64:, :] if False else None
        return rows

    @pl.when(core == 0)
    def _():
        total = None
        for node, c in ((a, coef), (b, coef_b)):
            rows = jnp.concatenate([full_ref[0, node, R:, :], full_ref[1, node, :64, :]], axis=0)
            term = rows[:, R:] - dot(rows[:, :R], c)
            total = term if total is None else total + term
        half_ref[...] = total

    @pl.when(core == 1)
    def _():
        total = None
        for node, c in ((a, coef), (b, coef_b)):
            rows = full_ref[1, node, 64:, :]
            term = rows[:, R:] - dot(rows[:, :R], c)
            total = term if total is None else total + term
        half_ref[...] = total


def last_levels(where_ref, own_ref, other_ref, coef_ref, y_ref, out_ref, full_ref, c_ref, d_ref, p_ref):
    core, node = where_ref[0], where_ref[2]
    full_ref[core] = own_ref[...]
    full_ref[1 - core] = other_ref[...]

    sums = []
    for index, (a, b) in enumerate(((node, node ^ 1), (node ^ 2, node ^ 3))):
        lead = full_ref[0, a]
        product = dot(full_ref[0, b, :, :R], lead)
        right = full_ref[0, b, :, R:] - product[:, R:]
        solve(product[:, :R], right, c_ref.at[index], p_ref)
        coef_a = c_ref[index]
        coef_b = lead[:, R:] - dot(lead[:, :R], coef_a)
        total = None
        for place, c in ((a, coef_a), (b, coef_b)):
            rows = full_ref[1, place]
            term = rows[:, R:] - dot(rows[:, :R], c)
            total = term if total is None else total + term
        sums.append(total)
    own, other = sums
    product = dot(other[:, :R], own)
    solve(product[:, :R], other[:, R:] - product[:, R:], d_ref, p_ref)
    x2 = d_ref[...]
    c1 = c_ref[0]
    c0 = coef_ref[...]
    x1 = c1[:, R:] - dot(c1[:, :R], x2)
    x0 = c0[:, 2 * R :] - dot(c0[:, :R], x1) - dot(c0[:, R : 2 * R], x2)
    x = jnp.concatenate([x0, x1, x2], axis=0)
    out_ref[...] = (y_ref[:, 3 * R :] - dot(y_ref[:, : 3 * R], x)).astype(BF16)


def whole(kernel, outs, scratch, operands):
    smem = pl.BlockSpec(memory_space=pltpu.SMEM)
    vmem = pl.BlockSpec(memory_space=pltpu.VMEM)
    return pl.pallas_call(
        kernel,
        in_specs=[smem] + [vmem] * (len(operands) - 1),
        out_specs=[vmem] * len(outs) if len(outs) > 1 else vmem,
        out_shape=outs if len(outs) > 1 else outs[0],
        scratch_shapes=scratch,
        compiler_params=pltpu.CompilerParams(vmem_limit_bytes=VMEM_BYTES),
    )(*operands)


def local(coupling, rhs, left_factors, right_factors):
    leaves, rows = lax.axis_size("leaf"), lax.axis_size("row")
    leaf, row = lax.axis_index("leaf"), lax.axis_index("row")
    where = jnp.stack([row % 2, leaf % 2, leaf // 2 % 4]).astype(jnp.int32)
    swap = [(i, i ^ 1) for i in range(rows)]
    own = jnp.concatenate([left_factors[0], rhs[0]], axis=1)
    gathered = lax.all_gather(own, "row", axis=0, tiled=True)
    y, keep, send = apply_leaf(where, coupling[0], gathered, own, right_factors[0])
    half, width = keep.shape
    keep = keep + lax.ppermute(send, "row", swap)
    quarter = half // 4
    same_core = [list(range(c, rows, 2)) for c in range(2)]
    pieces = lax.all_to_all(keep.reshape(4, quarter, width), "row", 0, 0, tiled=True, axis_index_groups=same_core)
    piece = jnp.sum(pieces, axis=0)
    column = [
        [(2 * g + low) * rows + 2 * high + c for low in range(2) for high in range(rows // 2)]
        for g in range(leaves // 2)
        for c in range(2)
    ]
    mine = lax.all_gather(piece, ("leaf", "row"), axis=0, tiled=True, axis_index_groups=column)
    mine = mine.reshape(2, half, width)
    others = lax.ppermute(mine, "row", swap)
    coef, part = whole(
        first_level,
        [jax.ShapeDtypeStruct((R, 3 * R), F32), jax.ShapeDtypeStruct((R, 3 * R), F32)],
        [pltpu.VMEM((2, 2, half, width), F32), pltpu.VMEM((R, R), F32)],
        (where, mine, others),
    )
    window = [[8 * g + 2 * n + low for n in range(4)] for g in range(leaves // 8) for low in range(2)]
    nodes = lax.all_gather(part, "leaf", axis=0, axis_index_groups=window)
    others = lax.ppermute(nodes, "row", swap)
    out = whole(
        last_levels,
        [jax.ShapeDtypeStruct((y.shape[0], R), BF16)],
        [
            pltpu.VMEM((2, 4, R, 3 * R), F32),
            pltpu.VMEM((2, R, 2 * R), F32),
            pltpu.VMEM((R, R), F32),
            pltpu.VMEM((R, R), F32),
        ],
        (where, nodes, others, coef, y),
    )
    return out[None]


def solution(mesh):
    spec = P("leaf", "row", None)
    return jax.shard_map(local, mesh=mesh, in_specs=(spec,) * 4, out_specs=spec, check_vma=False)
```

time: 445 us -> 176 us (0.40)
  waiting for transfers between devices: 321 us -> 65.9 us
  other arithmetic: 71.3 us -> 2.08 us
  blocking collectives: 0 us -> 64.2 us
  Pallas kernels: 0 us -> 20.7 us
  matrix products: 18.2 us -> 0 us
  starting transfers between devices: 17.6 us -> 5.98 us
    psum x3 -> x0, waiting for transfers between devices: 233 us -> none  [local(): total = lax.psum(partial_value_sum, 'row')]
    another operation x15 -> x1, other arithmetic: 68.6 us -> 0.08 us  [local(): where = jnp.stack([row % 2, leaf % 2, leaf // 2 % 4]).astype(jnp.int32)]
    all_gather x0 -> x2, blocking collectives: none -> 44.6 us  [the longest x1 30.4 us: local(): lax.all_gather(piece, ('leaf', 'row'), axis=0, tiled=True, axis_index_gro...]
    ppermute x6 -> x3, waiting for transfers between devices: 29.1 us -> 5.95 us  [the longest x1 2.25 us: local(): others = lax.ppermute(nodes, 'row', swap)]
    pallas_call x0 -> x3, Pallas kernels: none -> 20.7 us  [the longest x2 11.9 us: whole(): pl.pallas_call(kernel, in_specs=[smem] + [vmem] * (len(operands) - 1), ou...]
    all_to_all x0 -> x1, blocking collectives: none -> 19.6 us  [local(): lax.all_to_all(keep.reshape(4, quarter, width), 'row', 0, 0, tiled=True,...]
    dot_general x19 -> x0, matrix products: 16.4 us -> none  [the longest x1 5.82 us: local(): jnp.dot(block, lax.all_gather(local_columns, 'row', axis=0, tiled=True),...]
    ppermute x6 -> x3, starting transfers between devices: 17.5 us -> 5.98 us  [the longest x1 2.16 us: local(): keep = keep + lax.ppermute(send, 'row', swap)]
  transfers between devices with their start and end apart: 10 -> 4, of which waited for: 10 -> 4; matrix products, arithmetic and copies ran while one was open for 0% -> 0% of each run, Pallas kernels for 0% -> 0%
where the time goes in v1:
time: 176 us; the launch traced here: 174 us
  waiting for transfers between devices  65.9 us (37%)
  blocking collectives  64.2 us (36%)
  Pallas kernels  20.7 us (12%)
  between operations  13.5 us (8%)
  starting transfers between devices  5.98 us (3%)
  other arithmetic  2.08 us (1%)
  local copies, waits for them, and re-layouts  2.04 us (1%)
    all_gather x1, waiting for transfers between devices, local(): gathered = lax.all_gather(own, 'row', axis=0, tiled=True)  59.9 us
    all_gather x1, blocking collectives, local(): lax.all_gather(piece, ('leaf', 'row'), axis=0, tiled=True, axis_index_gro...  30.4 us
    all_to_all x1, blocking collectives, local(): lax.all_to_all(keep.reshape(4, quarter, width), 'row', 0, 0, tiled=True,...  19.6 us
    all_gather x1, blocking collectives, local(): nodes = lax.all_gather(part, 'leaf', axis=0, axis_index_groups=window)  14.2 us
    pallas_call x2, Pallas kernels, whole(): pl.pallas_call(kernel, in_specs=[smem] + [vmem] * (len(operands) - 1), ou...  11.9 us
    pallas_call x1, Pallas kernels, apply_leaf(): pl.pallas_call(apply_kernel, grid_spec=pltpu.PrefetchScalarGridSpec(num_s...  8.82 us
  transfers between devices with their start and end apart: 4, of which 4 were waited for; matrix products, arithmetic and copies ran while one was open for 0% of the time, Pallas kernels for 0%

profile of v1, /device:TPU:6, one launch (start us, length us, event | category | flops | bytes accessed | tf_op | source)
XLA Modules:
  0.0 174.4 jit_solution(15145249032930114992)
XLA Ops:
  6.5 0.0 all-gather.3.cloned.1.call-start
  6.5 1.9 %pad_maximum_fusion.own_ref = bf16[512,512]{1,0:T(8,128)(2,1)} fusion(bf16[512,128]{1,0:T(8,128)(2,1)} %bitcast.19, bf16[512,384]{1,0:T(8,128)(2,1)} %bitcast.18), kind=kLoop, calls=%fused_computation | loop fusion | flops 1048576 | bytes 1048576 | tf_op jit(solution)/shard_map/concatenate | solution.py:205
  8.5 0.0 all-gather.3.cloned.1.call-update
  8.5 0.1 pad_add_fusion.where_ref
  8.6 59.9 %all-gather.3.cloned.1.call-done.cols_ref = bf16[4096,512]{1,0:T(8,128)(2,1)} async-done(((bf16[512,512]{1,0:T(8,128)(2,1)}), bf16[4096,512]{1,0:T(8,128)(2,1)}) %all-gather.3.cloned.1.call-update) | async-done | bytes 4194320 | tf_op jit(solution)/shard_map/all_gather | solution.py:206
  68.5 0.0 copy-start
  68.5 1.0 copy-done
  69.5 0.0 copy-start.1
  69.5 1.0 copy-done.1
  70.5 8.8 %shard_map.46 = (f32[512,512]{1,0:T(8,128)S(1)}, f32[192,512]{1,0:T(8,128)S(1)}, f32[192,512]{1,0:T(8,128)S(1)}) custom-call(s32[3]{0:T(128)S(1)} %pad_add_fusion.where_ref, bf16[512,4096]{1,0:T(8,128)(2,1)} %bitcast.16, bf16[4096,512]{1,0:T(8,128)(2,1)} %all-gather.3.cloned.1.call-done.cols_ref, bf16[512,512]{1,0:T(8,128)(2,1)S(1)} %copy-done, ...), custom_call_target="tpu_custom_call" | custom-call | tf_op jit(solution)/shard_map/pallas_call | solution.py:94
  79.3 2.2 %collective-permute-start = (f32[192,512]{1,0:T(8,128)S(1)}, f32[192,512]{1,0:T(8,128)S(1)}, u32[]{:S(2)}, u32[]{:S(2)}) collective-permute-start(f32[192,512]{1,0:T(8,128)S(1)} %get-tuple-element.11), channel_id=1, source_target_pairs={{0,1},{1,0},{2,3},{3,2},{4,5},{5,4},{6,7},{7,6},{8,9},{9,8},{10,11... | collective-permute-start | bytes 1179656 | tf_op jit(solution)/shard_map/ppermute | solution.py:209
  81.5 1.5 collective-permute-done
  83.0 0.1 add.17
  83.0 19.6 %all_to_all.5 = f32[4,48,512]{2,1,0:T(8,128)S(1)} all-to-all(f32[4,48,512]{2,1,0:T(8,128)S(1)} %bitcast.17), channel_id=1, replica_groups={{0,2,4,6},{1,3,5,7},{8,10,12,14},{9,11,13,15},{16,18,20,22},{17,19,21,2..., dimensions={0} | all-to-all | bytes 786432 | tf_op jit(solution)/shard_map/all_to_all | solution.py:212
  102.6 30.4 %all_gather.13 = f32[384,512]{1,0:T(8,128)S(1)} all-gather(f32[48,512]{1,0:T(8,128)S(1)} %reduce_sum.9), channel_id=1, replica_groups={{0,2,4,6,8,10,12,14},{1,3,5,7,9,11,13,15},{16,18,20,22,24,26,28,30},{17..., dimensions={0}, use_global_device_ids=true | all-gather | bytes 884736 | tf_op jit(solution)/shard_map/all_gather | solution.py:219
  133.0 1.9 %collective-permute-start.1 = (f32[2,192,512]{2,1,0:T(8,128)S(1)}, f32[2,192,512]{2,1,0:T(8,128)S(1)}, u32[]{:S(2)}, u32[]{:S(2)}) collective-permute-start(f32[2,192,512]{2,1,0:T(8,128)S(1)} %bitcast.11), channel_id=1, source_target_pairs={{0,1},{1,0},{2,3},{3,2},{4,5},{5,4},{6,7},{7,6},{8,9},{9,8},{10,11... | collective-permute-start | bytes 2359304 | tf_op jit(solution)/shard_map/ppermute | solution.py:221
  135.0 2.3 %collective-permute-done.1.other_ref = f32[2,192,512]{2,1,0:T(8,128)S(1)} collective-permute-done((f32[2,192,512]{2,1,0:T(8,128)S(1)}, f32[2,192,512]{2,1,0:T(8,128)S(1)}, u32[]{:S(2)}, u32[]{:S(2)}) %collective-permute-start.1) | collective-permute-done | bytes 786464 | tf_op jit(solution)/shard_map/ppermute | solution.py:221
  137.2 2.9 %shard_map.47 = (f32[128,384]{1,0:T(8,128)S(1)}, f32[128,384]{1,0:T(8,128)S(1)}) custom-call(s32[3]{0:T(128)S(1)} %pad_add_fusion.where_ref, f32[2,192,512]{2,1,0:T(8,128)S(1)} %bitcast.12, f32[2,192,512]{2,1,0:T(8,128)S(1)} %collective-permute-done.1.other_ref), custom_call_target="tpu_custom_call" | custom-call | tf_op jit(solution)/shard_map/pallas_call | solution.py:190
  140.1 14.2 %all-gather = f32[512,384]{1,0:T(8,128)S(1)} all-gather(f32[128,384]{1,0:T(8,128)S(1)} %get-tuple-element.12), channel_id=2, replica_groups={{0,16,32,48},{8,24,40,56},{64,80,96,112},{72,88,104,120},{128,144,160,1..., dimensions={0}, use_global_device_ids=true | all-gather | bytes 983040 | tf_op jit(solution)/shard_map/all_gather | solution.py:229
  154.4 1.9 %collective-permute-start.2 = (f32[4,128,384]{2,1,0:T(8,128)S(1)}, f32[4,128,384]{2,1,0:T(8,128)S(1)}, u32[]{:S(2)}, u32[]{:S(2)}) collective-permute-start(f32[4,128,384]{2,1,0:T(8,128)S(1)} %bitcast.13), channel_id=1, source_target_pairs={{0,1},{1,0},{2,3},{3,2},{4,5},{5,4},{6,7},{7,6},{8,9},{9,8},{10,11... | collective-permute-start | bytes 2359304 | tf_op jit(solution)/shard_map/ppermute | solution.py:230
  156.3 2.3 %collective-permute-done.2.other_ref = f32[4,128,384]{2,1,0:T(8,128)S(1)} collective-permute-done((f32[4,128,384]{2,1,0:T(8,128)S(1)}, f32[4,128,384]{2,1,0:T(8,128)S(1)}, u32[]{:S(2)}, u32[]{:S(2)}) %collective-permute-start.2) | collective-permute-done | bytes 786464 | tf_op jit(solution)/shard_map/ppermute | solution.py:230
  158.6 9.0 %shard_map.48 = bf16[512,128]{1,0:T(8,128)(2,1)} custom-call(s32[3]{0:T(128)S(1)} %pad_add_fusion.where_ref, f32[4,128,384]{2,1,0:T(8,128)S(1)} %bitcast.14, f32[4,128,384]{2,1,0:T(8,128)S(1)} %collective-permute-done.2.other_ref, f32[128,384]{1,0:T(8,128)S(1)} %get-tuple-element.13.coef_ref, f32[512,512]{1,0:T(8,128)S(1)} %get-tuple-element.14.y_ref), custom_call_target="tpu_custom_call" | custom-call | tf_op jit(solution)/shard_map/pallas_call | solution.py:190
  (1 shorter events, 0.0 us)
Async XLA Ops:
  6.5 61.9 %all-gather.3.cloned.1.call-start = ((), (), s32[]{:S(2)}) async-start(), calls=%async_computation.1 | async-start | bytes 4718592 | tf_op jit(solution)/shard_map/all_gather | solution.py:206
  68.5 1.0 copy-start
  69.5 1.0 copy-start.1
  79.3 3.6 %collective-permute-start = (f32[192,512]{1,0:T(8,128)S(1)}, f32[192,512]{1,0:T(8,128)S(1)}, u32[]{:S(2)}, u32[]{:S(2)}) collective-permute-start(f32[192,512]{1,0:T(8,128)S(1)} %get-tuple-element.11), channel_id=1, source_target_pairs={{0,1},{1,0},{2,3},{3,2},{4,5},{5,4},{6,7},{7,6},{8,9},{9,8},{10,11... | collective-permute-start | bytes 1179656 | tf_op jit(solution)/shard_map/ppermute | solution.py:209
  133.0 4.2 %collective-permute-start.1 = (f32[2,192,512]{2,1,0:T(8,128)S(1)}, f32[2,192,512]{2,1,0:T(8,128)S(1)}, u32[]{:S(2)}, u32[]{:S(2)}) collective-permute-start(f32[2,192,512]{2,1,0:T(8,128)S(1)} %bitcast.11), channel_id=1, source_target_pairs={{0,1},{1,0},{2,3},{3,2},{4,5},{5,4},{6,7},{7,6},{8,9},{9,8},{10,11... | collective-permute-start | bytes 2359304 | tf_op jit(solution)/shard_map/ppermute | solution.py:221
  154.4 4.2 %collective-permute-start.2 = (f32[4,128,384]{2,1,0:T(8,128)S(1)}, f32[4,128,384]{2,1,0:T(8,128)S(1)}, u32[]{:S(2)}, u32[]{:S(2)}) collective-permute-start(f32[4,128,384]{2,1,0:T(8,128)S(1)} %bitcast.13), channel_id=1, source_target_pairs={{0,1},{1,0},{2,3},{3,2},{4,5},{5,4},{6,7},{7,6},{8,9},{9,8},{10,11... | collective-permute-start | bytes 2359304 | tf_op jit(solution)/shard_map/ppermute | solution.py:230
Sparse Core Ops, SparseCore 0:
  9.5 58.9 all-gather.2

commit v2 on v1

v2 whole, which is shorter than its diff:
```python
import functools

import jax
import jax.numpy as jnp
from jax import lax
from jax.experimental import pallas as pl
from jax.experimental.pallas import tpu as pltpu
from jax.sharding import PartitionSpec as P

R = 128
BLOCK = 512
F32 = jnp.float32
BF16 = jnp.bfloat16
VMEM_BYTES = 48 * 1024 * 1024


def dot(a, b):
    return jnp.dot(a, b, precision=lax.Precision.HIGHEST, preferred_element_type=F32)


def invert(s, right, c_ref, p_ref):
    eye = (lax.broadcasted_iota(jnp.int32, (R, R), 0) == lax.broadcasted_iota(jnp.int32, (R, R), 1)).astype(F32)
    a = eye - s
    one = jnp.max(jnp.sum(jnp.abs(a), axis=0))
    most = jnp.max(jnp.sum(jnp.abs(a), axis=1))
    p_ref[...] = (a / one).T / most

    def again(state):
        step, old, new = state
        still = jnp.logical_or(new > 0.01, new < 0.25 * old)
        return jnp.logical_and(step < 200, jnp.logical_and(new > 1e-12, still))

    def newton(state):
        x = p_ref[...]
        res = eye - dot(a, x)
        p_ref[...] = x + dot(x, res)
        return (state[0] + 1, state[2], jnp.sum(res * res))

    lax.while_loop(again, newton, (jnp.int32(0), jnp.float32(1e30), jnp.float32(1e29)))
    x = p_ref[...]
    c_ref[...] = dot(x, right)
    for _ in range(2):
        c_ref[...] = c_ref[...] + dot(x, right - dot(a, c_ref[...]))


def solve(systems):
    left = jnp.float32(0)
    grown = jnp.float32(0)
    for s, right, c_ref, p_ref in systems:
        c = right + dot(s, right)
        p = dot(s, s)
        for _ in range(2):
            c = c + dot(p, c)
            p = dot(p, p)
        c_ref[...] = c
        p_ref[...] = p
        left = jnp.maximum(left, jnp.sum(p * p))
        grown = jnp.maximum(grown, jnp.sum(s * s))
    good = jnp.logical_and(left < 0.25, grown < 64.0)

    @pl.when(good)
    def _():
        def more(_):
            size = jnp.float32(0)
            for _, _, c_ref, p_ref in systems:
                q = p_ref[...]
                c_ref[...] = c_ref[...] + dot(q, c_ref[...])
                q = dot(q, q)
                p_ref[...] = q
                size = jnp.maximum(size, jnp.sum(q * q))
            return size

        lax.while_loop(lambda size: size > 1e-15, more, left)

    @pl.when(jnp.logical_not(good))
    def _():
        for system in systems:
            invert(*system)


def column(row):
    return pl.ds(pl.multiple_of(row * BLOCK, BLOCK), BLOCK)


def term(block_ref, row, cols_ref):
    return jnp.dot(block_ref[:, column(row)], cols_ref[...], preferred_element_type=F32)


def start_kernel(where_ref, block_ref, own_ref, y_ref):
    y_ref[...] = own_ref[...].astype(F32) + term(block_ref, where_ref[3], own_ref)


def more_kernel(rows, where_ref, block_ref, *refs):
    *cols_refs, before_ref, y_ref = refs
    y_ref[...] = before_ref[...] + term(block_ref, where_ref[rows[0]], cols_refs[0])
    for row, cols_ref in zip(rows[1:], cols_refs[1:]):
        y_ref[...] += term(block_ref, where_ref[row], cols_ref)


def far_kernel(where_ref, block_ref, far_ref, next_near_ref, swapped_ref, before_ref, v_ref, y_ref, keep_ref, send_ref, gram_ref):
    core = where_ref[0]
    y_ref[...] = before_ref[...] + term(block_ref, where_ref[9], far_ref)
    y_ref[...] += term(block_ref, where_ref[8], next_near_ref)
    y_ref[...] += term(block_ref, where_ref[10], swapped_ref)
    rest = y_ref[...]
    total = None
    for _ in range(2):
        piece = rest.astype(BF16)
        rest = rest - piece.astype(F32)
        part = lax.dot_general(v_ref[...], piece, (((0,), (0,)), ((), ())), preferred_element_type=F32)
        total = part if total is None else total + part
    gram_ref[...] = total.reshape(gram_ref.shape)
    keep_ref[...] = gram_ref[core]
    send_ref[...] = gram_ref[1 - core]


def first_level(where_ref, own_ref, other_ref, coef_ref, half_ref, full_ref, p_ref):
    core, leaf = where_ref[0], where_ref[1]
    full_ref[core] = own_ref[...]
    full_ref[1 - core] = other_ref[...]
    a, b = leaf, 1 - leaf
    lead = full_ref[0, a, :R, :]
    product = dot(full_ref[0, b, :R, :R], lead)
    right = full_ref[0, b, :R, R:] - product[:, R:]
    solve([(product[:, :R], right, coef_ref, p_ref)])
    coef = coef_ref[...]
    coef_b = lead[:, R:] - dot(lead[:, :R], coef)

    @pl.when(core == 0)
    def _():
        total = None
        for node, c in ((a, coef), (b, coef_b)):
            rows = jnp.concatenate([full_ref[0, node, R:, :], full_ref[1, node, :64, :]], axis=0)
            term = rows[:, R:] - dot(rows[:, :R], c)
            total = term if total is None else total + term
        half_ref[...] = total

    @pl.when(core == 1)
    def _():
        total = None
        for node, c in ((a, coef), (b, coef_b)):
            rows = full_ref[1, node, 64:, :]
            term = rows[:, R:] - dot(rows[:, :R], c)
            total = term if total is None else total + term
        half_ref[...] = total


def last_levels(where_ref, own_ref, other_ref, coef_ref, y_ref, out_ref, full_ref, c_ref, d_ref, p_ref):
    core, node = where_ref[0], where_ref[2]
    full_ref[core] = own_ref[...]
    full_ref[1 - core] = other_ref[...]

    pairs = ((node, node ^ 1), (node ^ 2, node ^ 3))
    systems = []
    for index, (a, b) in enumerate(pairs):
        product = dot(full_ref[0, b, :, :R], full_ref[0, a])
        right = full_ref[0, b, :, R:] - product[:, R:]
        systems.append((product[:, :R], right, c_ref.at[index], p_ref.at[index]))
    solve(systems)
    sums = []
    for index, (a, b) in enumerate(pairs):
        coef_a = c_ref[index]
        coef_b = full_ref[0, a, :, R:] - dot(full_ref[0, a, :, :R], coef_a)
        total = None
        for place, c in ((a, coef_a), (b, coef_b)):
            part = full_ref[1, place, :, R:] - dot(full_ref[1, place, :, :R], c)
            total = part if total is None else total + part
        sums.append(total)
    own, other = sums
    product = dot(other[:, :R], own)
    solve([(product[:, :R], other[:, R:] - product[:, R:], d_ref, p_ref.at[0])])
    x2 = d_ref[...]
    c1 = c_ref[0]
    c0 = coef_ref[...]
    x1 = c1[:, R:] - dot(c1[:, :R], x2)
    x0 = c0[:, 2 * R :] - dot(c0[:, :R], x1) - dot(c0[:, R : 2 * R], x2)
    x = jnp.concatenate([x0, x1, x2], axis=0)
    out_ref[...] = (y_ref[:, 3 * R :] - dot(y_ref[:, : 3 * R], x)).astype(BF16)


def whole(kernel, outs, scratch, operands):
    smem = pl.BlockSpec(memory_space=pltpu.SMEM)
    vmem = pl.BlockSpec(memory_space=pltpu.VMEM)
    return pl.pallas_call(
        kernel,
        in_specs=[smem] + [vmem] * (len(operands) - 1),
        out_specs=[vmem] * len(outs) if len(outs) > 1 else vmem,
        out_shape=outs if len(outs) > 1 else outs[0],
        scratch_shapes=scratch,
        cost_estimate=pl.CostEstimate(flops=10**9, bytes_accessed=10**7, transcendentals=0),
        compiler_params=pltpu.CompilerParams(vmem_limit_bytes=VMEM_BYTES),
    )(*operands)


def local(coupling, rhs, left_factors, right_factors):
    leaves, rows = lax.axis_size("leaf"), lax.axis_size("row")
    leaf, row = lax.axis_index("leaf"), lax.axis_index("row")
    core, high, ring = row % 2, row // 2, rows // 2
    behind = (high + 2 * core - 1) % ring * 2
    ahead = (high - 2 * core + 1) % ring * 2
    far = (high + 2) % ring * 2
    where = [core, leaf % 2, leaf // 2 % 4, row, row ^ 1]
    where += [behind + core, behind + 1 - core, ahead + 1 - core, ahead + core, far + core, far + 1 - core]
    where = jnp.stack(where).astype(jnp.int32)
    swap = [(i, i ^ 1) for i in range(rows)]
    onward = [(i, (i + 2 - 4 * (i % 2)) % rows) for i in range(rows)]

    def move(value, way):
        return lax.ppermute(value, "row", way)

    block, v = coupling[0], right_factors[0]
    own = jnp.concatenate([left_factors[0], rhs[0]], axis=1)
    width, half = own.shape[1], v.shape[1] // 2
    y_shape = jax.ShapeDtypeStruct((BLOCK, width), F32)
    g_shape = jax.ShapeDtypeStruct((half, width), F32)

    def more(rows, cols, before):
        return whole(functools.partial(more_kernel, rows), [y_shape], [], (where, block, *cols, before))

    near = move(own, onward)
    own_s = move(own, swap)
    next_near = move(own_s, onward)
    y = whole(start_kernel, [y_shape], [], (where, block, own))
    far = move(near, onward)
    near_s = move(near, swap)
    y = more((4, 5), (own_s, near), y)
    y = more((6, 7), (next_near, near_s), y)
    far, next_near, y = lax.optimization_barrier((far, next_near, y))
    y, keep, send = whole(
        far_kernel,
        [y_shape, g_shape, g_shape],
        [pltpu.VMEM((2, half, width), F32)],
        (where, block, far, move(next_near, swap), move(far, swap), y, v),
    )
    keep = keep + move(send, swap)
    quarter = half // 4
    same_core = [list(range(c, rows, 2)) for c in range(2)]
    pieces = lax.all_to_all(keep.reshape(4, quarter, width), "row", 0, 0, tiled=True, axis_index_groups=same_core)
    piece = jnp.sum(pieces, axis=0)
    sibling = lax.ppermute(piece, "leaf", [(i, i ^ 1) for i in range(leaves)])
    low = leaf % 2
    both = jnp.stack([jnp.where(low == 0, piece, sibling), jnp.where(low == 0, sibling, piece)])
    mine = lax.all_gather(both, "row", axis=1, tiled=True, axis_index_groups=same_core)
    mine = mine.reshape(2, half, width)
    others = lax.ppermute(mine, "row", swap)
    coef, part = whole(
        first_level,
        [jax.ShapeDtypeStruct((R, 3 * R), F32), jax.ShapeDtypeStruct((R, 3 * R), F32)],
        [pltpu.VMEM((2, 2, half, width), F32), pltpu.VMEM((R, R), F32)],
        (where, mine, others),
    )
    window = [[8 * g + 2 * n + low for n in range(4)] for g in range(leaves // 8) for low in range(2)]
    nodes = lax.all_gather(part, "leaf", axis=0, axis_index_groups=window)
    others = lax.ppermute(nodes, "row", swap)
    out = whole(
        last_levels,
        [jax.ShapeDtypeStruct((y.shape[0], R), BF16)],
        [
            pltpu.VMEM((2, 4, R, 3 * R), F32),
            pltpu.VMEM((2, R, 2 * R), F32),
            pltpu.VMEM((R, R), F32),
            pltpu.VMEM((2, R, R), F32),
        ],
        (where, nodes, others, coef, y),
    )
    return out[None]


def solution(mesh):
    spec = P("leaf", "row", None)
    return jax.shard_map(local, mesh=mesh, in_specs=(spec,) * 4, out_specs=spec, check_vma=False)
```

time: 176 us -> 140 us (0.80)
  waiting for transfers between devices: 65.9 us -> 20.7 us
  starting transfers between devices: 5.98 us -> 41.5 us
  between operations: 13.5 us -> 0.31 us
  blocking collectives: 64.2 us -> 51.6 us
    all_gather x1 -> x0, waiting for transfers between devices: 59.9 us -> none  [local(): gathered = lax.all_gather(own, 'row', axis=0, tiled=True)]
    ppermute x1 -> x9, starting transfers between devices: 2.16 us -> 37.6 us  [the longest x8 34.7 us: move(): return lax.ppermute(value, 'row', way)]
    ppermute x1 -> x9, waiting for transfers between devices: 1.45 us -> 16.2 us  [the longest x8 12.6 us: move(): return lax.ppermute(value, 'row', way)]
    all_gather x1, blocking collectives: 30.4 us -> 17.3 us  [local(): lax.all_gather(both, 'row', axis=1, tiled=True, axis_index_groups=same_core)]
    pallas_call x2 -> x6, Pallas kernels: 11.9 us -> 20.9 us  [whole(): pl.pallas_call(kernel, in_specs=[smem] + [vmem] * (len(operands) - 1), ou...]
    pallas_call x1 -> x0, Pallas kernels: 8.82 us -> none  [apply_leaf(): pl.pallas_call(apply_kernel, grid_spec=pltpu.PrefetchScalarGridSpec(num_s...]
  transfers between devices with their start and end apart: 4 -> 11, of which waited for: 4 -> 7; matrix products, arithmetic and copies ran while one was open for 0% -> 0% of each run, Pallas kernels for 0% -> 5%
where the time goes in v2:
time: 140 us; the launch traced here: 138 us
  blocking collectives  51.6 us (37%)
  starting transfers between devices  41.5 us (30%)
  Pallas kernels  20.9 us (15%)
  waiting for transfers between devices  20.7 us (15%)
  local copies, waits for them, and re-layouts  2.28 us (2%)
    ppermute x8, starting transfers between devices, move(): return lax.ppermute(value, 'row', way)  34.7 us
    pallas_call x6, Pallas kernels, whole(): pl.pallas_call(kernel, in_specs=[smem] + [vmem] * (len(operands) - 1), ou...  20.9 us
    all_to_all x1, blocking collectives, local(): lax.all_to_all(keep.reshape(4, quarter, width), 'row', 0, 0, tiled=True,...  20 us
    all_gather x1, blocking collectives, local(): lax.all_gather(both, 'row', axis=1, tiled=True, axis_index_groups=same_core)  17.3 us
    all_gather x1, blocking collectives, local(): nodes = lax.all_gather(part, 'leaf', axis=0, axis_index_groups=window)  14.3 us
    ppermute x8, waiting for transfers between devices, move(): return lax.ppermute(value, 'row', way)  12.6 us
    ppermute x1, waiting for transfers between devices, local(): sibling = lax.ppermute(piece, 'leaf', [(i, i ^ 1) for i in range(leaves)])  3.6 us
    ppermute x1, starting transfers between devices, local(): sibling = lax.ppermute(piece, 'leaf', [(i, i ^ 1) for i in range(leaves)])  2.9 us
  transfers between devices with their start and end apart: 11, of which 7 were waited for; matrix products, arithmetic and copies ran while one was open for 0% of the time, Pallas kernels for 5%

profile of v2, /device:TPU:6, one launch (start us, length us, event | category | flops | bytes accessed | tf_op | source)
XLA Modules:
  0.0 138.4 jit_solution(14378493240566316959)
XLA Ops:
  1.1 1.9 %collective-permute-start.2 = (bf16[512,512]{1,0:T(8,128)(2,1)S(1)}, bf16[512,512]{1,0:T(8,128)(2,1)S(1)}, u32[]{:S(2)}, u32[]{:S(2)}) collective-permute-start(bf16[512,512]{1,0:T(8,128)(2,1)S(1)} %pad_maximum_fusion.own_ref), channel_id=1, source_target_pairs={{0,1},{1,0},{2,3},{3,2},{4,5},{5,4},{6,7},{7,6},{8,9},{9,8},{10,11... | collective-permute-start | bytes 1572872 | tf_op jit(solution)/shard_map/ppermute | solution.py:209
  3.0 6.1 %collective-permute-start = (bf16[512,512]{1,0:T(8,128)(2,1)S(1)}, bf16[512,512]{1,0:T(8,128)(2,1)S(1)}, u32[]{:S(2)}, u32[]{:S(2)}) collective-permute-start(bf16[512,512]{1,0:T(8,128)(2,1)S(1)} %pad_maximum_fusion.own_ref), channel_id=1, source_target_pairs={{0,2},{1,7},{2,4},{3,1},{4,6},{5,3},{6,0},{7,5},{8,10},{9,15},{10,... | collective-permute-start | bytes 1572872 | tf_op jit(solution)/shard_map/ppermute | solution.py:209
  9.2 7.3 %collective-permute-start.3 = (bf16[512,512]{1,0:T(8,128)(2,1)S(1)}, bf16[512,512]{1,0:T(8,128)(2,1)S(1)}, u32[]{:S(2)}, u32[]{:S(2)}) collective-permute-start(bf16[512,512]{1,0:T(8,128)(2,1)S(1)} %collective-permute-done.2.refs_0_), channel_id=1, source_target_pairs={{0,2},{1,7},{2,4},{3,1},{4,6},{5,3},{6,0},{7,5},{8,10},{9,15},{10,... | collective-permute-start | bytes 1572872 | tf_op jit(solution)/shard_map/ppermute | solution.py:209
  16.5 4.8 %collective-permute-done.refs_1_ = bf16[512,512]{1,0:T(8,128)(2,1)S(1)} collective-permute-done((bf16[512,512]{1,0:T(8,128)(2,1)S(1)}, bf16[512,512]{1,0:T(8,128)(2,1)S(1)}, u32[]{:S(2)}, u32[]{:S(2)}) %collective-permute-start) | collective-permute-done | bytes 524320 | tf_op jit(solution)/shard_map/ppermute | solution.py:209
  21.3 6.0 %collective-permute-start.4 = (bf16[512,512]{1,0:T(8,128)(2,1)S(1)}, bf16[512,512]{1,0:T(8,128)(2,1)S(1)}, u32[]{:S(2)}, u32[]{:S(2)}) collective-permute-start(bf16[512,512]{1,0:T(8,128)(2,1)S(1)} %collective-permute-done.refs_1_), channel_id=1, source_target_pairs={{0,1},{1,0},{2,3},{3,2},{4,5},{5,4},{6,7},{7,6},{8,9},{9,8},{10,11... | collective-permute-start | bytes 1572872 | tf_op jit(solution)/shard_map/ppermute | solution.py:209
  27.3 3.6 %collective-permute-start.1 = (bf16[512,512]{1,0:T(8,128)(2,1)S(1)}, bf16[512,512]{1,0:T(8,128)(2,1)S(1)}, u32[]{:S(2)}, u32[]{:S(2)}) collective-permute-start(bf16[512,512]{1,0:T(8,128)(2,1)S(1)} %collective-permute-done.refs_1_), channel_id=1, source_target_pairs={{0,2},{1,7},{2,4},{3,1},{4,6},{5,3},{6,0},{7,5},{8,10},{9,15},{10,... | collective-permute-start | bytes 1572872 | tf_op jit(solution)/shard_map/ppermute | solution.py:209
  31.1 2.2 %copy-done = bf16[1,512,4096]{2,1,0:T(8,128)(2,1)S(1)} copy-done((bf16[1,512,4096]{2,1,0:T(8,128)(2,1)S(1)}, bf16[1,512,4096]{2,1,0:T(8,128)(2,1)}, u32[]{:S(2)}) %copy-start) | copy-done | bytes 4194328
  34.3 2.9 %shard_map.47.refs_2_ = f32[512,512]{1,0:T(8,128)S(1)} custom-call(s32[11]{0:T(128)S(1)} %stack.56.where_ref, bf16[512,4096]{1,0:T(8,128)(2,1)} %bitcast.22, bf16[512,512]{1,0:T(8,128)(2,1)S(1)} %collective-permute-done.2.refs_0_, bf16[512,512]{1,0:T(8,128)(2,1)S(1)} %collective-permute-done.refs_1_, f32[512,512]{1,0:T(8,128)S(1)} %shard_map.46.refs_2_), custom_call_target="tpu_custom_call" | custom-call | flops 1000000000 | bytes 10000000 | tf_op jit(solution)/shard_map/pallas_call | solution.py:184
  37.2 2.9 %shard_map.48.before_ref = f32[512,512]{1,0:T(8,128)S(1)} custom-call(s32[11]{0:T(128)S(1)} %stack.56.where_ref, bf16[512,4096]{1,0:T(8,128)(2,1)} %bitcast.23, bf16[512,512]{1,0:T(8,128)(2,1)S(1)} %collective-permute-done.3.refs_0_, bf16[512,512]{1,0:T(8,128)(2,1)S(1)} %collective-permute-done.4.refs_1_, f32[512,512]{1,0:T(8,128)S(1)} %shard_map.47.refs_2_), custom_call_target="tpu_custom_call" | custom-call | flops 1000000000 | bytes 10000000 | tf_op jit(solution)/shard_map/pallas_call | solution.py:184
  40.2 4.3 %collective-permute-done.1.far_ref = bf16[512,512]{1,0:T(8,128)(2,1)S(1)} collective-permute-done((bf16[512,512]{1,0:T(8,128)(2,1)S(1)}, bf16[512,512]{1,0:T(8,128)(2,1)S(1)}, u32[]{:S(2)}, u32[]{:S(2)}) %collective-permute-start.1) | collective-permute-done | bytes 524320 | tf_op jit(solution)/shard_map/ppermute | solution.py:209
  44.5 5.9 %collective-permute-start.5 = (bf16[512,512]{1,0:T(8,128)(2,1)S(1)}, bf16[512,512]{1,0:T(8,128)(2,1)S(1)}, u32[]{:S(2)}, u32[]{:S(2)}) collective-permute-start(bf16[512,512]{1,0:T(8,128)(2,1)S(1)} %collective-permute-done.3.refs_0_), channel_id=1, source_target_pairs={{0,1},{1,0},{2,3},{3,2},{4,5},{5,4},{6,7},{7,6},{8,9},{9,8},{10,11... | collective-permute-start | bytes 1572872 | tf_op jit(solution)/shard_map/ppermute | solution.py:209
  50.4 1.9 %collective-permute-start.6 = (bf16[512,512]{1,0:T(8,128)(2,1)S(1)}, bf16[512,512]{1,0:T(8,128)(2,1)S(1)}, u32[]{:S(2)}, u32[]{:S(2)}) collective-permute-start(bf16[512,512]{1,0:T(8,128)(2,1)S(1)} %collective-permute-done.1.far_ref), channel_id=1, source_target_pairs={{0,1},{1,0},{2,3},{3,2},{4,5},{5,4},{6,7},{7,6},{8,9},{9,8},{10,11... | collective-permute-start | bytes 1572872 | tf_op jit(solution)/shard_map/ppermute | solution.py:209
  54.2 3.7 %shard_map.49 = (f32[512,512]{1,0:T(8,128)S(1)}, f32[192,512]{1,0:T(8,128)S(1)}, f32[192,512]{1,0:T(8,128)S(1)}) custom-call(s32[11]{0:T(128)S(1)} %stack.56.where_ref, bf16[512,4096]{1,0:T(8,128)(2,1)} %bitcast.24, bf16[512,512]{1,0:T(8,128)(2,1)S(1)} %collective-permute-done.1.far_ref, bf16[512,512]{1,0:T(8,128)(2,1)S(1)} %collective-permute-done.5.next_near_ref, ...), custom_call_target="tpu_custom_call" | custom-call | flops 1000000000 | bytes 10000000 | tf_op jit(solution)/shard_map/pallas_call | solution.py:184
  57.9 2.0 %collective-permute-start.7 = (f32[192,512]{1,0:T(8,128)S(1)}, f32[192,512]{1,0:T(8,128)S(1)}, u32[]{:S(2)}, u32[]{:S(2)}) collective-permute-start(f32[192,512]{1,0:T(8,128)S(1)} %get-tuple-element.17), channel_id=1, source_target_pairs={{0,1},{1,0},{2,3},{3,2},{4,5},{5,4},{6,7},{7,6},{8,9},{9,8},{10,11... | collective-permute-start | bytes 1179656 | tf_op jit(solution)/shard_map/ppermute | solution.py:209
  61.6 20.0 %all_to_all.5 = f32[4,48,512]{2,1,0:T(8,128)S(1)} all-to-all(f32[4,48,512]{2,1,0:T(8,128)S(1)} %bitcast.29), channel_id=1, replica_groups={{0,2,4,6},{1,3,5,7},{8,10,12,14},{9,11,13,15},{16,18,20,22},{17,19,21,2..., dimensions={0} | all-to-all | bytes 786432 | tf_op jit(solution)/shard_map/all_to_all | solution.py:238
  81.6 2.9 %collective-permute-start.8 = (f32[48,512]{1,0:T(8,128)S(1)}, f32[48,512]{1,0:T(8,128)S(1)}, u32[]{:S(2)}, u32[]{:S(2)}) collective-permute-start(f32[48,512]{1,0:T(8,128)S(1)} %reduce_sum.9), channel_id=1, source_target_pairs={{0,8},{8,0},{16,24},{24,16},{32,40},{40,32},{48,56},{56,48},{64,72... | collective-permute-start | bytes 294920 | tf_op jit(solution)/shard_map/ppermute | solution.py:240
  84.5 3.6 %collective-permute-done.8 = f32[48,512]{1,0:T(8,128)S(1)} collective-permute-done((f32[48,512]{1,0:T(8,128)S(1)}, f32[48,512]{1,0:T(8,128)S(1)}, u32[]{:S(2)}, u32[]{:S(2)}) %collective-permute-start.8) | collective-permute-done | bytes 98336 | tf_op jit(solution)/shard_map/ppermute | solution.py:240
  88.1 17.3 %all_gather.9.own_ref = f32[2,192,512]{2,1,0:T(8,128)S(1)} all-gather(f32[2,48,512]{2,1,0:T(8,128)S(1)} %pad_maximum_fusion.1), channel_id=1, replica_groups={{0,2,4,6},{1,3,5,7},{8,10,12,14},{9,11,13,15},{16,18,20,22},{17,19,21,2..., dimensions={1}, use_global_device_ids=true | all-gather | bytes 983040 | tf_op jit(solution)/shard_map/all_gather | solution.py:243
  105.4 1.9 %collective-permute-start.9 = (f32[2,192,512]{2,1,0:T(8,128)S(1)}, f32[2,192,512]{2,1,0:T(8,128)S(1)}, u32[]{:S(2)}, u32[]{:S(2)}) collective-permute-start(f32[2,192,512]{2,1,0:T(8,128)S(1)} %all_gather.9.own_ref), channel_id=1, source_target_pairs={{0,1},{1,0},{2,3},{3,2},{4,5},{5,4},{6,7},{7,6},{8,9},{9,8},{10,11... | collective-permute-start | bytes 2359304 | tf_op jit(solution)/shard_map/ppermute | solution.py:245
  107.4 2.3 %collective-permute-done.9.other_ref = f32[2,192,512]{2,1,0:T(8,128)S(1)} collective-permute-done((f32[2,192,512]{2,1,0:T(8,128)S(1)}, f32[2,192,512]{2,1,0:T(8,128)S(1)}, u32[]{:S(2)}, u32[]{:S(2)}) %collective-permute-start.9) | collective-permute-done | bytes 786464 | tf_op jit(solution)/shard_map/ppermute | solution.py:245
  109.6 2.9 %shard_map.50 = (f32[128,384]{1,0:T(8,128)S(1)}, f32[128,384]{1,0:T(8,128)S(1)}) custom-call(s32[11]{0:T(128)S(1)} %stack.56.where_ref, f32[2,192,512]{2,1,0:T(8,128)S(1)} %all_gather.9.own_ref, f32[2,192,512]{2,1,0:T(8,128)S(1)} %collective-permute-done.9.other_ref), custom_call_target="tpu_custom_call" | custom-call | flops 1000000000 | bytes 10000000 | tf_op jit(solution)/shard_map/pallas_call | solution.py:184
  112.5 14.3 %all-gather = f32[512,384]{1,0:T(8,128)S(1)} all-gather(f32[128,384]{1,0:T(8,128)S(1)} %get-tuple-element.18), channel_id=2, replica_groups={{0,16,32,48},{8,24,40,56},{64,80,96,112},{72,88,104,120},{128,144,160,1..., dimensions={0}, use_global_device_ids=true | all-gather | bytes 983040 | tf_op jit(solution)/shard_map/all_gather | solution.py:253
  128.7 2.3 %collective-permute-done.10.other_ref = f32[4,128,384]{2,1,0:T(8,128)S(1)} collective-permute-done((f32[4,128,384]{2,1,0:T(8,128)S(1)}, f32[4,128,384]{2,1,0:T(8,128)S(1)}, u32[]{:S(2)}, u32[]{:S(2)}) %collective-permute-start.10) | collective-permute-done | bytes 786464 | tf_op jit(solution)/shard_map/ppermute | solution.py:254
  131.0 7.4 %shard_map.51 = bf16[512,128]{1,0:T(8,128)(2,1)} custom-call(s32[11]{0:T(128)S(1)} %stack.56.where_ref, f32[4,128,384]{2,1,0:T(8,128)S(1)} %bitcast.27, f32[4,128,384]{2,1,0:T(8,128)S(1)} %collective-permute-done.10.other_ref, f32[128,384]{1,0:T(8,128)S(1)} %get-tuple-element.19.coef_ref, f32[512,512]{1,0:T(8,128)S(1)} %get-tuple-element.20.y_ref), custom_call_target="tpu_custom_call" | custom-call | flops 1000000000 | bytes 10000000 | tf_op jit(solution)/shard_map/pallas_call | solution.py:184
  (17 shorter events, 7.7 us)
Async XLA Ops:
  1.1 8.0 %collective-permute-start.2 = (bf16[512,512]{1,0:T(8,128)(2,1)S(1)}, bf16[512,512]{1,0:T(8,128)(2,1)S(1)}, u32[]{:S(2)}, u32[]{:S(2)}) collective-permute-start(bf16[512,512]{1,0:T(8,128)(2,1)S(1)} %pad_maximum_fusion.own_ref), channel_id=1, source_target_pairs={{0,1},{1,0},{2,3},{3,2},{4,5},{5,4},{6,7},{7,6},{8,9},{9,8},{10,11... | collective-permute-start | bytes 1572872 | tf_op jit(solution)/shard_map/ppermute | solution.py:209
  3.0 18.2 %collective-permute-start = (bf16[512,512]{1,0:T(8,128)(2,1)S(1)}, bf16[512,512]{1,0:T(8,128)(2,1)S(1)}, u32[]{:S(2)}, u32[]{:S(2)}) collective-permute-start(bf16[512,512]{1,0:T(8,128)(2,1)S(1)} %pad_maximum_fusion.own_ref), channel_id=1, source_target_pairs={{0,2},{1,7},{2,4},{3,1},{4,6},{5,3},{6,0},{7,5},{8,10},{9,15},{10,... | collective-permute-start | bytes 1572872 | tf_op jit(solution)/shard_map/ppermute | solution.py:209
  9.2 28.0 %collective-permute-start.3 = (bf16[512,512]{1,0:T(8,128)(2,1)S(1)}, bf16[512,512]{1,0:T(8,128)(2,1)S(1)}, u32[]{:S(2)}, u32[]{:S(2)}) collective-permute-start(bf16[512,512]{1,0:T(8,128)(2,1)S(1)} %collective-permute-done.2.refs_0_), channel_id=1, source_target_pairs={{0,2},{1,7},{2,4},{3,1},{4,6},{5,3},{6,0},{7,5},{8,10},{9,15},{10,... | collective-permute-start | bytes 1572872 | tf_op jit(solution)/shard_map/ppermute | solution.py:209
  21.3 15.9 %collective-permute-start.4 = (bf16[512,512]{1,0:T(8,128)(2,1)S(1)}, bf16[512,512]{1,0:T(8,128)(2,1)S(1)}, u32[]{:S(2)}, u32[]{:S(2)}) collective-permute-start(bf16[512,512]{1,0:T(8,128)(2,1)S(1)} %collective-permute-done.refs_1_), channel_id=1, source_target_pairs={{0,1},{1,0},{2,3},{3,2},{4,5},{5,4},{6,7},{7,6},{8,9},{9,8},{10,11... | collective-permute-start | bytes 1572872 | tf_op jit(solution)/shard_map/ppermute | solution.py:209
  27.3 17.2 %collective-permute-start.1 = (bf16[512,512]{1,0:T(8,128)(2,1)S(1)}, bf16[512,512]{1,0:T(8,128)(2,1)S(1)}, u32[]{:S(2)}, u32[]{:S(2)}) collective-permute-start(bf16[512,512]{1,0:T(8,128)(2,1)S(1)} %collective-permute-done.refs_1_), channel_id=1, source_target_pairs={{0,2},{1,7},{2,4},{3,1},{4,6},{5,3},{6,0},{7,5},{8,10},{9,15},{10,... | collective-permute-start | bytes 1572872 | tf_op jit(solution)/shard_map/ppermute | solution.py:209
  31.1 2.2 %copy-start = (bf16[1,512,4096]{2,1,0:T(8,128)(2,1)S(1)}, bf16[1,512,4096]{2,1,0:T(8,128)(2,1)}, u32[]{:S(2)}) copy-start(bf16[1,512,4096]{2,1,0:T(8,128)(2,1)} %param.4) | copy-start | bytes 12582916
  37.2 17.0 %copy-start.1 = (bf16[1,512,384]{2,1,0:T(8,128)(2,1)S(1)}, bf16[1,512,384]{2,1,0:T(8,128)(2,1)}, u32[]{:S(2)}) copy-start(bf16[1,512,384]{2,1,0:T(8,128)(2,1)} %param.7) | copy-start | bytes 1179652
  44.5 7.8 %collective-permute-start.5 = (bf16[512,512]{1,0:T(8,128)(2,1)S(1)}, bf16[512,512]{1,0:T(8,128)(2,1)S(1)}, u32[]{:S(2)}, u32[]{:S(2)}) collective-permute-start(bf16[512,512]{1,0:T(8,128)(2,1)S(1)} %collective-permute-done.3.refs_0_), channel_id=1, source_target_pairs={{0,1},{1,0},{2,3},{3,2},{4,5},{5,4},{6,7},{7,6},{8,9},{9,8},{10,11... | collective-permute-start | bytes 1572872 | tf_op jit(solution)/shard_map/ppermute | solution.py:209
  50.4 3.8 %collective-permute-start.6 = (bf16[512,512]{1,0:T(8,128)(2,1)S(1)}, bf16[512,512]{1,0:T(8,128)(2,1)S(1)}, u32[]{:S(2)}, u32[]{:S(2)}) collective-permute-start(bf16[512,512]{1,0:T(8,128)(2,1)S(1)} %collective-permute-done.1.far_ref), channel_id=1, source_target_pairs={{0,1},{1,0},{2,3},{3,2},{4,5},{5,4},{6,7},{7,6},{8,9},{9,8},{10,11... | collective-permute-start | bytes 1572872 | tf_op jit(solution)/shard_map/ppermute | solution.py:209
  57.9 3.6 %collective-permute-start.7 = (f32[192,512]{1,0:T(8,128)S(1)}, f32[192,512]{1,0:T(8,128)S(1)}, u32[]{:S(2)}, u32[]{:S(2)}) collective-permute-start(f32[192,512]{1,0:T(8,128)S(1)} %get-tuple-element.17), channel_id=1, source_target_pairs={{0,1},{1,0},{2,3},{3,2},{4,5},{5,4},{6,7},{7,6},{8,9},{9,8},{10,11... | collective-permute-start | bytes 1179656 | tf_op jit(solution)/shard_map/ppermute | solution.py:209
  81.6 6.5 %collective-permute-start.8 = (f32[48,512]{1,0:T(8,128)S(1)}, f32[48,512]{1,0:T(8,128)S(1)}, u32[]{:S(2)}, u32[]{:S(2)}) collective-permute-start(f32[48,512]{1,0:T(8,128)S(1)} %reduce_sum.9), channel_id=1, source_target_pairs={{0,8},{8,0},{16,24},{24,16},{32,40},{40,32},{48,56},{56,48},{64,72... | collective-permute-start | bytes 294920 | tf_op jit(solution)/shard_map/ppermute | solution.py:240
  105.4 4.2 %collective-permute-start.9 = (f32[2,192,512]{2,1,0:T(8,128)S(1)}, f32[2,192,512]{2,1,0:T(8,128)S(1)}, u32[]{:S(2)}, u32[]{:S(2)}) collective-permute-start(f32[2,192,512]{2,1,0:T(8,128)S(1)} %all_gather.9.own_ref), channel_id=1, source_target_pairs={{0,1},{1,0},{2,3},{3,2},{4,5},{5,4},{6,7},{7,6},{8,9},{9,8},{10,11... | collective-permute-start | bytes 2359304 | tf_op jit(solution)/shard_map/ppermute | solution.py:245
  126.8 4.2 %collective-permute-start.10 = (f32[4,128,384]{2,1,0:T(8,128)S(1)}, f32[4,128,384]{2,1,0:T(8,128)S(1)}, u32[]{:S(2)}, u32[]{:S(2)}) collective-permute-start(f32[4,128,384]{2,1,0:T(8,128)S(1)} %bitcast.26), channel_id=1, source_target_pairs={{0,1},{1,0},{2,3},{3,2},{4,5},{5,4},{6,7},{7,6},{8,9},{9,8},{10,11... | collective-permute-start | bytes 2359304 | tf_op jit(solution)/shard_map/ppermute | solution.py:254

commit v3 on v2

--- a/solution.py
+++ b/solution.py
@@ -70,7 +70,7 @@
                 size = jnp.maximum(size, jnp.sum(q * q))
             return size
 
-        lax.while_loop(lambda size: size > 1e-15, more, left)
+        lax.while_loop(lambda size: size > 1e-13, more, left)
 
     @pl.when(jnp.logical_not(good))
     def _():
@@ -97,11 +97,10 @@
         y_ref[...] += term(block_ref, where_ref[row], cols_ref)
 
 
-def far_kernel(where_ref, block_ref, far_ref, next_near_ref, swapped_ref, before_ref, v_ref, y_ref, keep_ref, send_ref, gram_ref):
+def far_kernel(where_ref, block_ref, next_near_ref, far_ref, before_ref, v_ref, y_ref, keep_ref, send_ref, gram_ref):
     core = where_ref[0]
-    y_ref[...] = before_ref[...] + term(block_ref, where_ref[9], far_ref)
-    y_ref[...] += term(block_ref, where_ref[8], next_near_ref)
-    y_ref[...] += term(block_ref, where_ref[10], swapped_ref)
+    y_ref[...] = before_ref[...] + term(block_ref, where_ref[8], next_near_ref)
+    y_ref[...] += term(block_ref, where_ref[10], far_ref)
     rest = y_ref[...]
     total = None
     for _ in range(2):
@@ -109,61 +108,51 @@
         rest = rest - piece.astype(F32)
         part = lax.dot_general(v_ref[...], piece, (((0,), (0,)), ((), ())), preferred_element_type=F32)
         total = part if total is None else total + part
-    gram_ref[...] = total.reshape(gram_ref.shape)
-    keep_ref[...] = gram_ref[core]
-    send_ref[...] = gram_ref[1 - core]
-
-
-def first_level(where_ref, own_ref, other_ref, coef_ref, half_ref, full_ref, p_ref):
-    core, leaf = where_ref[0], where_ref[1]
-    full_ref[core] = own_ref[...]
-    full_ref[1 - core] = other_ref[...]
-    a, b = leaf, 1 - leaf
-    lead = full_ref[0, a, :R, :]
-    product = dot(full_ref[0, b, :R, :R], lead)
-    right = full_ref[0, b, :R, R:] - product[:, R:]
-    solve([(product[:, :R], right, coef_ref, p_ref)])
+    gram_ref[...] = total
+    for part_ref, c in ((keep_ref, core), (send_ref, 1 - core)):
+        part_ref[: R // 2, :] = gram_ref[pl.ds(pl.multiple_of(c * (R // 2), R // 2), R // 2), :]
+        part_ref[R // 2 :, :] = gram_ref[pl.ds(pl.multiple_of(R + c * R, R), R), :]
+
+
+def first_level(own_ref, pair_ref, coef_ref, half_ref, p_ref):
+    lead, sibling = (jnp.concatenate([pair_ref[0, node], pair_ref[1, node]], axis=0) for node in range(2))
+    product = dot(sibling[:, :R], lead)
+    solve([(product[:, :R], sibling[:, R:] - product[:, R:], coef_ref, p_ref)])
     coef = coef_ref[...]
     coef_b = lead[:, R:] - dot(lead[:, :R], coef)
-
-    @pl.when(core == 0)
-    def _():
-        total = None
-        for node, c in ((a, coef), (b, coef_b)):
-            rows = jnp.concatenate([full_ref[0, node, R:, :], full_ref[1, node, :64, :]], axis=0)
-            term = rows[:, R:] - dot(rows[:, :R], c)
-            total = term if total is None else total + term
-        half_ref[...] = total
-
-    @pl.when(core == 1)
-    def _():
-        total = None
-        for node, c in ((a, coef), (b, coef_b)):
-            rows = full_ref[1, node, 64:, :]
-            term = rows[:, R:] - dot(rows[:, :R], c)
-            total = term if total is None else total + term
-        half_ref[...] = total
-
-
-def last_levels(where_ref, own_ref, other_ref, coef_ref, y_ref, out_ref, full_ref, c_ref, d_ref, p_ref):
-    core, node = where_ref[0], where_ref[2]
-    full_ref[core] = own_ref[...]
-    full_ref[1 - core] = other_ref[...]
-
+    total = None
+    for node, c in ((0, coef), (1, coef_b)):
+        part = own_ref[node, R // 2 :, R:] - dot(own_ref[node, R // 2 :, :R], c)
+        total = part if total is None else total + part
+    half_ref[...] = total
+
+
+def last_levels(where_ref, own_ref, other_ref, *refs):
+    @pl.when(where_ref[0] == 0)
+    def _():
+        last_body(where_ref, own_ref, other_ref, *refs)
+
+    @pl.when(where_ref[0] == 1)
+    def _():
+        last_body(where_ref, other_ref, own_ref, *refs)
+
+
+def last_body(where_ref, v1_ref, v2_ref, coef_ref, y_ref, out_ref, c_ref, d_ref, p_ref):
+    node = where_ref[2]
     pairs = ((node, node ^ 1), (node ^ 2, node ^ 3))
     systems = []
     for index, (a, b) in enumerate(pairs):
-        product = dot(full_ref[0, b, :, :R], full_ref[0, a])
-        right = full_ref[0, b, :, R:] - product[:, R:]
+        product = dot(v1_ref[b, :, :R], v1_ref[a])
+        right = v1_ref[b, :, R:] - product[:, R:]
         systems.append((product[:, :R], right, c_ref.at[index], p_ref.at[index]))
     solve(systems)
     sums = []
     for index, (a, b) in enumerate(pairs):
         coef_a = c_ref[index]
-        coef_b = full_ref[0, a, :, R:] - dot(full_ref[0, a, :, :R], coef_a)
+        coef_b = v1_ref[a, :, R:] - dot(v1_ref[a, :, :R], coef_a)
         total = None
         for place, c in ((a, coef_a), (b, coef_b)):
-            part = full_ref[1, place, :, R:] - dot(full_ref[1, place, :, :R], c)
+            part = v2_ref[place, :, R:] - dot(v2_ref[place, :, :R], c)
             total = part if total is None else total + part
         sums.append(total)
     own, other = sums
@@ -183,7 +172,7 @@
     vmem = pl.BlockSpec(memory_space=pltpu.VMEM)
     return pl.pallas_call(
         kernel,
-        in_specs=[smem] + [vmem] * (len(operands) - 1),
+        in_specs=[smem if x.ndim == 1 else vmem for x in operands],
         out_specs=[vmem] * len(outs) if len(outs) > 1 else vmem,
         out_shape=outs if len(outs) > 1 else outs[0],
         scratch_shapes=scratch,
@@ -219,18 +208,24 @@
 
     near = move(own, onward)
     own_s = move(own, swap)
+    y = whole(start_kernel, [y_shape], [], (where, block, own))
+    y = more((4,), (own_s,), y)
+    own_s, y = lax.optimization_barrier((own_s, y))
     next_near = move(own_s, onward)
-    y = whole(start_kernel, [y_shape], [], (where, block, own))
     far = move(near, onward)
+    y = more((5,), (near,), y)
+    near, y = lax.optimization_barrier((near, y))
     near_s = move(near, swap)
-    y = more((4, 5), (own_s, near), y)
-    y = more((6, 7), (next_near, near_s), y)
-    far, next_near, y = lax.optimization_barrier((far, next_near, y))
+    y = more((6,), (next_near,), y)
+    next_near, y = lax.optimization_barrier((next_near, y))
+    next_near_s = move(next_near, swap)
+    far_s = move(far, swap)
+    y = more((7, 9), (near_s, far), y)
     y, keep, send = whole(
         far_kernel,
         [y_shape, g_shape, g_shape],
-        [pltpu.VMEM((2, half, width), F32)],
-        (where, block, far, move(next_near, swap), move(far, swap), y, v),
+        [pltpu.VMEM((2 * half, width), F32)],
+        (where, block, next_near_s, far_s, y, v),
     )
     keep = keep + move(send, swap)
     quarter = half // 4
@@ -238,25 +233,24 @@
     pieces = lax.all_to_all(keep.reshape(4, quarter, width), "row", 0, 0, tiled=True, axis_index_groups=same_core)
     piece = jnp.sum(pieces, axis=0)
     sibling = lax.ppermute(piece, "leaf", [(i, i ^ 1) for i in range(leaves)])
-    low = leaf % 2
-    both = jnp.stack([jnp.where(low == 0, piece, sibling), jnp.where(low == 0, sibling, piece)])
+    both = jnp.stack([piece, sibling])
     mine = lax.all_gather(both, "row", axis=1, tiled=True, axis_index_groups=same_core)
     mine = mine.reshape(2, half, width)
-    others = lax.ppermute(mine, "row", swap)
+    chip = [[2 * i, 2 * i + 1] for i in range(rows // 2)]
+    pair = lax.all_gather(mine[:, : R // 2], "row", axis=0, axis_index_groups=chip)
     coef, part = whole(
         first_level,
         [jax.ShapeDtypeStruct((R, 3 * R), F32), jax.ShapeDtypeStruct((R, 3 * R), F32)],
-        [pltpu.VMEM((2, 2, half, width), F32), pltpu.VMEM((R, R), F32)],
-        (where, mine, others),
+        [pltpu.VMEM((R, R), F32)],
+        (mine, pair),
     )
     window = [[8 * g + 2 * n + low for n in range(4)] for g in range(leaves // 8) for low in range(2)]
     nodes = lax.all_gather(part, "leaf", axis=0, axis_index_groups=window)
-    others = lax.ppermute(nodes, "row", swap)
+    others = move(nodes, swap)
     out = whole(
         last_levels,
         [jax.ShapeDtypeStruct((y.shape[0], R), BF16)],
         [
-            pltpu.VMEM((2, 4, R, 3 * R), F32),
             pltpu.VMEM((2, R, 2 * R), F32),
             pltpu.VMEM((R, R), F32),
             pltpu.VMEM((2, R, R), F32),

time: 140 us -> 137 us (0.979)
  waiting for transfers between devices: 20.7 us -> 10.8 us
  Pallas kernels: 20.9 us -> 25.5 us
  starting transfers between devices: 41.5 us -> 43.1 us
    ppermute x8 -> x9, starting transfers between devices: 34.7 us -> 41.2 us  [move(): return lax.ppermute(value, 'row', way)]
    ppermute x8 -> x9, waiting for transfers between devices: 12.6 us -> 6.24 us  [move(): return lax.ppermute(value, 'row', way)]
    pallas_call x6 -> x8, Pallas kernels: 20.9 us -> 25.5 us  [whole(): pl.pallas_call(kernel, in_specs=[smem if x.ndim == 1 else vmem for x in o...]
    ppermute x2 -> x0, waiting for transfers between devices: 4.5 us -> none  [the longest x1 2.25 us: local(): others = lax.ppermute(mine, 'row', swap)]
    ppermute x2 -> x0, starting transfers between devices: 3.82 us -> none  [the longest x1 1.91 us: local(): others = lax.ppermute(mine, 'row', swap)]
    all_to_all x1, blocking collectives: 20 us -> 17.5 us  [local(): lax.all_to_all(keep.reshape(4, quarter, width), 'row', 0, 0, tiled=True,...]
    all_gather x0 -> x1, blocking collectives: none -> 2.18 us  [local(): lax.all_gather(mine[:, :R // 2], 'row', axis=0, axis_index_groups=chip)]
  transfers between devices with their start and end apart: 11 -> 10, of which waited for: 7 -> 4; matrix products, arithmetic and copies ran while one was open for 0% -> 0% of each run, Pallas kernels for 5% -> 9%
where the time goes in v3:
time: 137 us; the launch traced here: 135 us
  blocking collectives  52.2 us (38%)
  starting transfers between devices  43.1 us (31%)
  Pallas kernels  25.5 us (19%)
  waiting for transfers between devices  10.8 us (8%)
  local copies, waits for them, and re-layouts  2.3 us (2%)
    ppermute x9, starting transfers between devices, move(): return lax.ppermute(value, 'row', way)  41.2 us
    pallas_call x8, Pallas kernels, whole(): pl.pallas_call(kernel, in_specs=[smem if x.ndim == 1 else vmem for x in o...  25.5 us
    all_gather x1, blocking collectives, local(): lax.all_gather(both, 'row', axis=1, tiled=True, axis_index_groups=same_core)  18.1 us
    all_to_all x1, blocking collectives, local(): lax.all_to_all(keep.reshape(4, quarter, width), 'row', 0, 0, tiled=True,...  17.5 us
    all_gather x1, blocking collectives, local(): nodes = lax.all_gather(part, 'leaf', axis=0, axis_index_groups=window)  14.3 us
    ppermute x9, waiting for transfers between devices, move(): return lax.ppermute(value, 'row', way)  6.24 us
    ppermute x1, waiting for transfers between devices, local(): sibling = lax.ppermute(piece, 'leaf', [(i, i ^ 1) for i in range(leaves)])  4.6 us
  transfers between devices with their start and end apart: 10, of which 4 were waited for; matrix products, arithmetic and copies ran while one was open for 0% of the time, Pallas kernels for 9%

profile of v3, /device:TPU:6, one launch (start us, length us, event | category | flops | bytes accessed | tf_op | source)
XLA Modules:
  0.0 135.5 jit_solution(12327308585484463419)
XLA Ops:
  1.1 1.9 %collective-permute-start = (bf16[512,512]{1,0:T(8,128)(2,1)S(1)}, bf16[512,512]{1,0:T(8,128)(2,1)S(1)}, u32[]{:S(2)}, u32[]{:S(2)}) collective-permute-start(bf16[512,512]{1,0:T(8,128)(2,1)S(1)} %pad_maximum_fusion.own_ref), channel_id=1, source_target_pairs={{0,1},{1,0},{2,3},{3,2},{4,5},{5,4},{6,7},{7,6},{8,9},{9,8},{10,11... | collective-permute-start | bytes 1572872 | tf_op jit(solution)/shard_map/ppermute | solution.py:198
  3.0 6.1 %collective-permute-start.2 = (bf16[512,512]{1,0:T(8,128)(2,1)S(1)}, bf16[512,512]{1,0:T(8,128)(2,1)S(1)}, u32[]{:S(2)}, u32[]{:S(2)}) collective-permute-start(bf16[512,512]{1,0:T(8,128)(2,1)S(1)} %pad_maximum_fusion.own_ref), channel_id=1, source_target_pairs={{0,2},{1,7},{2,4},{3,1},{4,6},{5,3},{6,0},{7,5},{8,10},{9,15},{10,... | collective-permute-start | bytes 1572872 | tf_op jit(solution)/shard_map/ppermute | solution.py:198
  9.3 2.2 %copy-done = bf16[1,512,4096]{2,1,0:T(8,128)(2,1)S(1)} copy-done((bf16[1,512,4096]{2,1,0:T(8,128)(2,1)S(1)}, bf16[1,512,4096]{2,1,0:T(8,128)(2,1)}, u32[]{:S(2)}) %copy-start) | copy-done | bytes 4194328
  12.5 2.6 %shard_map.47.refs_1_ = f32[512,512]{1,0:T(8,128)S(1)} custom-call(s32[11]{0:T(128)S(1)} %stack.56.where_ref, bf16[512,4096]{1,0:T(8,128)(2,1)} %bitcast.21, bf16[512,512]{1,0:T(8,128)(2,1)S(1)} %collective-permute-done.refs_0_, f32[512,512]{1,0:T(8,128)S(1)} %shard_map.46.refs_1_), custom_call_target="tpu_custom_call" | custom-call | flops 1000000000 | bytes 10000000 | tf_op jit(solution)/shard_map/pallas_call | solution.py:173
  15.2 7.3 %collective-permute-start.1 = (bf16[512,512]{1,0:T(8,128)(2,1)S(1)}, bf16[512,512]{1,0:T(8,128)(2,1)S(1)}, u32[]{:S(2)}, u32[]{:S(2)}) collective-permute-start(bf16[512,512]{1,0:T(8,128)(2,1)S(1)} %collective-permute-done.refs_0_), channel_id=1, source_target_pairs={{0,2},{1,7},{2,4},{3,1},{4,6},{5,3},{6,0},{7,5},{8,10},{9,15},{10,... | collective-permute-start | bytes 1572872 | tf_op jit(solution)/shard_map/ppermute | solution.py:198
  22.5 9.5 %collective-permute-start.4 = (bf16[512,512]{1,0:T(8,128)(2,1)S(1)}, bf16[512,512]{1,0:T(8,128)(2,1)S(1)}, u32[]{:S(2)}, u32[]{:S(2)}) collective-permute-start(bf16[512,512]{1,0:T(8,128)(2,1)S(1)} %collective-permute-done.2.refs_0_), channel_id=1, source_target_pairs={{0,2},{1,7},{2,4},{3,1},{4,6},{5,3},{6,0},{7,5},{8,10},{9,15},{10,... | collective-permute-start | bytes 1572872 | tf_op jit(solution)/shard_map/ppermute | solution.py:198
  32.0 2.6 %shard_map.48.refs_1_ = f32[512,512]{1,0:T(8,128)S(1)} custom-call(s32[11]{0:T(128)S(1)} %stack.56.where_ref, bf16[512,4096]{1,0:T(8,128)(2,1)} %bitcast.22, bf16[512,512]{1,0:T(8,128)(2,1)S(1)} %collective-permute-done.2.refs_0_, f32[512,512]{1,0:T(8,128)S(1)} %shard_map.47.refs_1_), custom_call_target="tpu_custom_call" | custom-call | flops 1000000000 | bytes 10000000 | tf_op jit(solution)/shard_map/pallas_call | solution.py:173
  34.6 6.6 %collective-permute-start.6 = (bf16[512,512]{1,0:T(8,128)(2,1)S(1)}, bf16[512,512]{1,0:T(8,128)(2,1)S(1)}, u32[]{:S(2)}, u32[]{:S(2)}) collective-permute-start(bf16[512,512]{1,0:T(8,128)(2,1)S(1)} %collective-permute-done.2.refs_0_), channel_id=1, source_target_pairs={{0,1},{1,0},{2,3},{3,2},{4,5},{5,4},{6,7},{7,6},{8,9},{9,8},{10,11... | collective-permute-start | bytes 1572872 | tf_op jit(solution)/shard_map/ppermute | solution.py:198
  41.2 2.6 %shard_map.49.refs_2_ = f32[512,512]{1,0:T(8,128)S(1)} custom-call(s32[11]{0:T(128)S(1)} %stack.56.where_ref, bf16[512,4096]{1,0:T(8,128)(2,1)} %bitcast.23, bf16[512,512]{1,0:T(8,128)(2,1)S(1)} %collective-permute-done.1.refs_0_, f32[512,512]{1,0:T(8,128)S(1)} %shard_map.48.refs_1_), custom_call_target="tpu_custom_call" | custom-call | flops 1000000000 | bytes 10000000 | tf_op jit(solution)/shard_map/pallas_call | solution.py:173
  43.9 3.6 %collective-permute-start.3 = (bf16[512,512]{1,0:T(8,128)(2,1)S(1)}, bf16[512,512]{1,0:T(8,128)(2,1)S(1)}, u32[]{:S(2)}, u32[]{:S(2)}) collective-permute-start(bf16[512,512]{1,0:T(8,128)(2,1)S(1)} %collective-permute-done.1.refs_0_), channel_id=1, source_target_pairs={{0,1},{1,0},{2,3},{3,2},{4,5},{5,4},{6,7},{7,6},{8,9},{9,8},{10,11... | collective-permute-start | bytes 1572872 | tf_op jit(solution)/shard_map/ppermute | solution.py:198
  47.5 2.6 %collective-permute-done.4.refs_1_ = bf16[512,512]{1,0:T(8,128)(2,1)S(1)} collective-permute-done((bf16[512,512]{1,0:T(8,128)(2,1)S(1)}, bf16[512,512]{1,0:T(8,128)(2,1)S(1)}, u32[]{:S(2)}, u32[]{:S(2)}) %collective-permute-start.4) | collective-permute-done | bytes 524320 | tf_op jit(solution)/shard_map/ppermute | solution.py:198
  50.1 1.9 %collective-permute-start.5 = (bf16[512,512]{1,0:T(8,128)(2,1)S(1)}, bf16[512,512]{1,0:T(8,128)(2,1)S(1)}, u32[]{:S(2)}, u32[]{:S(2)}) collective-permute-start(bf16[512,512]{1,0:T(8,128)(2,1)S(1)} %collective-permute-done.4.refs_1_), channel_id=1, source_target_pairs={{0,1},{1,0},{2,3},{3,2},{4,5},{5,4},{6,7},{7,6},{8,9},{9,8},{10,11... | collective-permute-start | bytes 1572872 | tf_op jit(solution)/shard_map/ppermute | solution.py:198
  52.1 2.9 %shard_map.50.before_ref = f32[512,512]{1,0:T(8,128)S(1)} custom-call(s32[11]{0:T(128)S(1)} %stack.56.where_ref, bf16[512,4096]{1,0:T(8,128)(2,1)} %bitcast.24, bf16[512,512]{1,0:T(8,128)(2,1)S(1)} %collective-permute-done.6.refs_0_, bf16[512,512]{1,0:T(8,128)(2,1)S(1)} %collective-permute-done.4.refs_1_, f32[512,512]{1,0:T(8,128)S(1)} %shard_map.49.refs_2_), custom_call_target="tpu_custom_call" | custom-call | flops 1000000000 | bytes 10000000 | tf_op jit(solution)/shard_map/pallas_call | solution.py:173
  55.0 3.5 %shard_map.51 = (f32[512,512]{1,0:T(8,128)S(1)}, f32[192,512]{1,0:T(8,128)S(1)}, f32[192,512]{1,0:T(8,128)S(1)}) custom-call(s32[11]{0:T(128)S(1)} %stack.56.where_ref, bf16[512,4096]{1,0:T(8,128)(2,1)} %bitcast.25, bf16[512,512]{1,0:T(8,128)(2,1)S(1)} %collective-permute-done.3.next_near_ref, bf16[512,512]{1,0:T(8,128)(2,1)S(1)} %collective-permute-done.5.far_ref, ...), custom_call_target="tpu_custom_call" | custom-call | flops 1000000000 | bytes 10000000 | tf_op jit(solution)/shard_map/pallas_call | solution.py:173
  58.5 2.4 %collective-permute-start.7 = (f32[192,512]{1,0:T(8,128)S(1)}, f32[192,512]{1,0:T(8,128)S(1)}, u32[]{:S(2)}, u32[]{:S(2)}) collective-permute-start(f32[192,512]{1,0:T(8,128)S(1)} %get-tuple-element.23), channel_id=1, source_target_pairs={{0,1},{1,0},{2,3},{3,2},{4,5},{5,4},{6,7},{7,6},{8,9},{9,8},{10,11... | collective-permute-start | bytes 1179656 | tf_op jit(solution)/shard_map/ppermute | solution.py:198
  62.3 17.5 %all_to_all.5 = f32[4,48,512]{2,1,0:T(8,128)S(1)} all-to-all(f32[4,48,512]{2,1,0:T(8,128)S(1)} %bitcast.31), channel_id=1, replica_groups={{0,2,4,6},{1,3,5,7},{8,10,12,14},{9,11,13,15},{16,18,20,22},{17,19,21,2..., dimensions={0} | all-to-all | bytes 786432 | tf_op jit(solution)/shard_map/all_to_all | solution.py:233
  79.8 1.9 %collective-permute-start.8 = (f32[48,512]{1,0:T(8,128)S(1)}, f32[48,512]{1,0:T(8,128)S(1)}, u32[]{:S(2)}, u32[]{:S(2)}) collective-permute-start(f32[48,512]{1,0:T(8,128)S(1)} %reduce_sum.9), channel_id=1, source_target_pairs={{0,8},{8,0},{16,24},{24,16},{32,40},{40,32},{48,56},{56,48},{64,72... | collective-permute-start | bytes 294920 | tf_op jit(solution)/shard_map/ppermute | solution.py:235
  81.8 4.6 %collective-permute-done.8 = f32[48,512]{1,0:T(8,128)S(1)} collective-permute-done((f32[48,512]{1,0:T(8,128)S(1)}, f32[48,512]{1,0:T(8,128)S(1)}, u32[]{:S(2)}, u32[]{:S(2)}) %collective-permute-start.8) | collective-permute-done | bytes 98336 | tf_op jit(solution)/shard_map/ppermute | solution.py:235
  86.4 18.1 %all_gather.15.own_ref = f32[2,192,512]{2,1,0:T(8,128)S(1)} all-gather(f32[2,48,512]{2,1,0:T(8,128)S(1)} %pad_maximum_fusion.1), channel_id=1, replica_groups={{0,2,4,6},{1,3,5,7},{8,10,12,14},{9,11,13,15},{16,18,20,22},{17,19,21,2..., dimensions={1}, use_global_device_ids=true | all-gather | bytes 983040 | tf_op jit(solution)/shard_map/all_gather | solution.py:237
  104.5 2.2 %all-gather = f32[4,64,512]{2,1,0:T(8,128)S(1)} all-gather(f32[2,64,512]{2,1,0:T(8,128)S(1)} %slice.4), channel_id=2, replica_groups={{0,1},{2,3},{4,5},{6,7},{8,9},{10,11},{12,13},{14,15},{16,17},{18,19},{..., dimensions={0}, use_global_device_ids=true | all-gather | bytes 786432 | tf_op jit(solution)/shard_map/all_gather | solution.py:240
  106.7 2.1 %shard_map.52 = (f32[128,384]{1,0:T(8,128)S(1)}, f32[128,384]{1,0:T(8,128)S(1)}) custom-call(f32[2,192,512]{2,1,0:T(8,128)S(1)} %all_gather.15.own_ref, f32[2,2,64,512]{3,2,1,0:T(8,128)S(1)} %bitcast.29), custom_call_target="tpu_custom_call" | custom-call | flops 1000000000 | bytes 10000000 | tf_op jit(solution)/shard_map/pallas_call | solution.py:173
  108.9 14.3 %all-gather.1 = f32[512,384]{1,0:T(8,128)S(1)} all-gather(f32[128,384]{1,0:T(8,128)S(1)} %get-tuple-element.24), channel_id=3, replica_groups={{0,16,32,48},{8,24,40,56},{64,80,96,112},{72,88,104,120},{128,144,160,1..., dimensions={0}, use_global_device_ids=true | all-gather | bytes 983040 | tf_op jit(solution)/shard_map/all_gather | solution.py:248
  125.1 2.3 %collective-permute-done.9.other_ref = f32[4,128,384]{2,1,0:T(8,128)S(1)} collective-permute-done((f32[4,128,384]{2,1,0:T(8,128)S(1)}, f32[4,128,384]{2,1,0:T(8,128)S(1)}, u32[]{:S(2)}, u32[]{:S(2)}) %collective-permute-start.9) | collective-permute-done | bytes 786464 | tf_op jit(solution)/shard_map/ppermute | solution.py:198
  127.4 8.1 %shard_map.53 = bf16[512,128]{1,0:T(8,128)(2,1)} custom-call(s32[11]{0:T(128)S(1)} %stack.56.where_ref, f32[4,128,384]{2,1,0:T(8,128)S(1)} %bitcast.28, f32[4,128,384]{2,1,0:T(8,128)S(1)} %collective-permute-done.9.other_ref, f32[128,384]{1,0:T(8,128)S(1)} %get-tuple-element.25.refs_0_, f32[512,512]{1,0:T(8,128)S(1)} %get-tuple-element.26.refs_1_), custom_call_target="tpu_custom_call" | custom-call | flops 1000000000 | bytes 10000000 | tf_op jit(solution)/shard_map/pallas_call | solution.py:173
  (18 shorter events, 5.6 us)
Async XLA Ops:
  1.1 11.4 %collective-permute-start = (bf16[512,512]{1,0:T(8,128)(2,1)S(1)}, bf16[512,512]{1,0:T(8,128)(2,1)S(1)}, u32[]{:S(2)}, u32[]{:S(2)}) collective-permute-start(bf16[512,512]{1,0:T(8,128)(2,1)S(1)} %pad_maximum_fusion.own_ref), channel_id=1, source_target_pairs={{0,1},{1,0},{2,3},{3,2},{4,5},{5,4},{6,7},{7,6},{8,9},{9,8},{10,11... | collective-permute-start | bytes 1572872 | tf_op jit(solution)/shard_map/ppermute | solution.py:198
  3.0 19.4 %collective-permute-start.2 = (bf16[512,512]{1,0:T(8,128)(2,1)S(1)}, bf16[512,512]{1,0:T(8,128)(2,1)S(1)}, u32[]{:S(2)}, u32[]{:S(2)}) collective-permute-start(bf16[512,512]{1,0:T(8,128)(2,1)S(1)} %pad_maximum_fusion.own_ref), channel_id=1, source_target_pairs={{0,2},{1,7},{2,4},{3,1},{4,6},{5,3},{6,0},{7,5},{8,10},{9,15},{10,... | collective-permute-start | bytes 1572872 | tf_op jit(solution)/shard_map/ppermute | solution.py:198
  9.3 2.2 %copy-start = (bf16[1,512,4096]{2,1,0:T(8,128)(2,1)S(1)}, bf16[1,512,4096]{2,1,0:T(8,128)(2,1)}, u32[]{:S(2)}) copy-start(bf16[1,512,4096]{2,1,0:T(8,128)(2,1)} %param.4) | copy-start | bytes 12582916
  15.2 26.0 %collective-permute-start.1 = (bf16[512,512]{1,0:T(8,128)(2,1)S(1)}, bf16[512,512]{1,0:T(8,128)(2,1)S(1)}, u32[]{:S(2)}, u32[]{:S(2)}) collective-permute-start(bf16[512,512]{1,0:T(8,128)(2,1)S(1)} %collective-permute-done.refs_0_), channel_id=1, source_target_pairs={{0,2},{1,7},{2,4},{3,1},{4,6},{5,3},{6,0},{7,5},{8,10},{9,15},{10,... | collective-permute-start | bytes 1572872 | tf_op jit(solution)/shard_map/ppermute | solution.py:198
  22.5 27.6 %collective-permute-start.4 = (bf16[512,512]{1,0:T(8,128)(2,1)S(1)}, bf16[512,512]{1,0:T(8,128)(2,1)S(1)}, u32[]{:S(2)}, u32[]{:S(2)}) collective-permute-start(bf16[512,512]{1,0:T(8,128)(2,1)S(1)} %collective-permute-done.2.refs_0_), channel_id=1, source_target_pairs={{0,2},{1,7},{2,4},{3,1},{4,6},{5,3},{6,0},{7,5},{8,10},{9,15},{10,... | collective-permute-start | bytes 1572872 | tf_op jit(solution)/shard_map/ppermute | solution.py:198
  34.6 17.4 %collective-permute-start.6 = (bf16[512,512]{1,0:T(8,128)(2,1)S(1)}, bf16[512,512]{1,0:T(8,128)(2,1)S(1)}, u32[]{:S(2)}, u32[]{:S(2)}) collective-permute-start(bf16[512,512]{1,0:T(8,128)(2,1)S(1)} %collective-permute-done.2.refs_0_), channel_id=1, source_target_pairs={{0,1},{1,0},{2,3},{3,2},{4,5},{5,4},{6,7},{7,6},{8,9},{9,8},{10,11... | collective-permute-start | bytes 1572872 | tf_op jit(solution)/shard_map/ppermute | solution.py:198
  43.9 11.1 %copy-start.1 = (bf16[1,512,384]{2,1,0:T(8,128)(2,1)S(1)}, bf16[1,512,384]{2,1,0:T(8,128)(2,1)}, u32[]{:S(2)}) copy-start(bf16[1,512,384]{2,1,0:T(8,128)(2,1)} %param.7) | copy-start | bytes 1179652
  43.9 11.1 %collective-permute-start.3 = (bf16[512,512]{1,0:T(8,128)(2,1)S(1)}, bf16[512,512]{1,0:T(8,128)(2,1)S(1)}, u32[]{:S(2)}, u32[]{:S(2)}) collective-permute-start(bf16[512,512]{1,0:T(8,128)(2,1)S(1)} %collective-permute-done.1.refs_0_), channel_id=1, source_target_pairs={{0,1},{1,0},{2,3},{3,2},{4,5},{5,4},{6,7},{7,6},{8,9},{9,8},{10,11... | collective-permute-start | bytes 1572872 | tf_op jit(solution)/shard_map/ppermute | solution.py:198
  50.1 4.9 %collective-permute-start.5 = (bf16[512,512]{1,0:T(8,128)(2,1)S(1)}, bf16[512,512]{1,0:T(8,128)(2,1)S(1)}, u32[]{:S(2)}, u32[]{:S(2)}) collective-permute-start(bf16[512,512]{1,0:T(8,128)(2,1)S(1)} %collective-permute-done.4.refs_1_), channel_id=1, source_target_pairs={{0,1},{1,0},{2,3},{3,2},{4,5},{5,4},{6,7},{7,6},{8,9},{9,8},{10,11... | collective-permute-start | bytes 1572872 | tf_op jit(solution)/shard_map/ppermute | solution.py:198
  58.5 3.7 %collective-permute-start.7 = (f32[192,512]{1,0:T(8,128)S(1)}, f32[192,512]{1,0:T(8,128)S(1)}, u32[]{:S(2)}, u32[]{:S(2)}) collective-permute-start(f32[192,512]{1,0:T(8,128)S(1)} %get-tuple-element.23), channel_id=1, source_target_pairs={{0,1},{1,0},{2,3},{3,2},{4,5},{5,4},{6,7},{7,6},{8,9},{9,8},{10,11... | collective-permute-start | bytes 1179656 | tf_op jit(solution)/shard_map/ppermute | solution.py:198
  79.8 6.5 %collective-permute-start.8 = (f32[48,512]{1,0:T(8,128)S(1)}, f32[48,512]{1,0:T(8,128)S(1)}, u32[]{:S(2)}, u32[]{:S(2)}) collective-permute-start(f32[48,512]{1,0:T(8,128)S(1)} %reduce_sum.9), channel_id=1, source_target_pairs={{0,8},{8,0},{16,24},{24,16},{32,40},{40,32},{48,56},{56,48},{64,72... | collective-permute-start | bytes 294920 | tf_op jit(solution)/shard_map/ppermute | solution.py:235
  123.2 4.2 %collective-permute-start.9 = (f32[4,128,384]{2,1,0:T(8,128)S(1)}, f32[4,128,384]{2,1,0:T(8,128)S(1)}, u32[]{:S(2)}, u32[]{:S(2)}) collective-permute-start(f32[4,128,384]{2,1,0:T(8,128)S(1)} %bitcast.27), channel_id=1, source_target_pairs={{0,1},{1,0},{2,3},{3,2},{4,5},{5,4},{6,7},{7,6},{8,9},{9,8},{10,11... | collective-permute-start | bytes 2359304 | tf_op jit(solution)/shard_map/ppermute | solution.py:198

commit v4 on v3

--- a/solution.py
+++ b/solution.py
@@ -11,7 +11,7 @@
 BLOCK = 512
 F32 = jnp.float32
 BF16 = jnp.bfloat16
-VMEM_BYTES = 48 * 1024 * 1024
+VMEM_BYTES = 16 * 1024 * 1024
 
 
 def dot(a, b):
@@ -82,25 +82,24 @@
     return pl.ds(pl.multiple_of(row * BLOCK, BLOCK), BLOCK)
 
 
-def term(block_ref, row, cols_ref):
-    return jnp.dot(block_ref[:, column(row)], cols_ref[...], preferred_element_type=F32)
+def terms(where_ref, block_ref, rows, cols_refs):
+    blocks = jnp.concatenate([block_ref[:, column(where_ref[row])] for row in rows], axis=1)
+    cols = jnp.concatenate([cols_ref[...] for cols_ref in cols_refs], axis=0)
+    return jnp.dot(blocks, cols, preferred_element_type=F32)
 
 
 def start_kernel(where_ref, block_ref, own_ref, y_ref):
-    y_ref[...] = own_ref[...].astype(F32) + term(block_ref, where_ref[3], own_ref)
+    y_ref[...] = own_ref[...].astype(F32) + terms(where_ref, block_ref, (3,), (own_ref,))
 
 
 def more_kernel(rows, where_ref, block_ref, *refs):
     *cols_refs, before_ref, y_ref = refs
-    y_ref[...] = before_ref[...] + term(block_ref, where_ref[rows[0]], cols_refs[0])
-    for row, cols_ref in zip(rows[1:], cols_refs[1:]):
-        y_ref[...] += term(block_ref, where_ref[row], cols_ref)
+    y_ref[...] = before_ref[...] + terms(where_ref, block_ref, rows, cols_refs)
 
 
 def far_kernel(where_ref, block_ref, next_near_ref, far_ref, before_ref, v_ref, y_ref, keep_ref, send_ref, gram_ref):
     core = where_ref[0]
-    y_ref[...] = before_ref[...] + term(block_ref, where_ref[8], next_near_ref)
-    y_ref[...] += term(block_ref, where_ref[10], far_ref)
+    y_ref[...] = before_ref[...] + terms(where_ref, block_ref, (8, 10), (next_near_ref, far_ref))
     rest = y_ref[...]
     total = None
     for _ in range(2):

time: 137 us -> 134 us (0.978)
  Pallas kernels: 25.5 us -> 16.6 us
  waiting for transfers between devices: 10.8 us -> 18 us
  starting transfers between devices: 43.1 us -> 41 us
    pallas_call x8, Pallas kernels: 25.5 us -> 16.6 us  [whole(): pl.pallas_call(kernel, in_specs=[smem if x.ndim == 1 else vmem for x in o...]
    ppermute x9, waiting for transfers between devices: 6.24 us -> 14.3 us  [move(): return lax.ppermute(value, 'row', way)]
    ppermute x9, starting transfers between devices: 41.2 us -> 38.1 us  [move(): return lax.ppermute(value, 'row', way)]
    all_to_all x1, blocking collectives: 17.5 us -> 19.2 us  [local(): lax.all_to_all(keep.reshape(4, quarter, width), 'row', 0, 0, tiled=True,...]
  transfers between devices with their start and end apart: 10 -> 10, of which waited for: 4 -> 7; matrix products, arithmetic and copies ran while one was open for 0% -> 0% of each run, Pallas kernels for 9% -> 4%
where the time goes in v4:
time: 134 us; the launch traced here: 132 us
  blocking collectives  52.6 us (39%)
  starting transfers between devices  41 us (31%)
  waiting for transfers between devices  18 us (13%)
  Pallas kernels  16.6 us (12%)
  local copies, waits for them, and re-layouts  2.3 us (2%)
    ppermute x9, starting transfers between devices, move(): return lax.ppermute(value, 'row', way)  38.1 us
    all_to_all x1, blocking collectives, local(): lax.all_to_all(keep.reshape(4, quarter, width), 'row', 0, 0, tiled=True,...  19.2 us
    all_gather x1, blocking collectives, local(): lax.all_gather(both, 'row', axis=1, tiled=True, axis_index_groups=same_core)  16.8 us
    pallas_call x8, Pallas kernels, whole(): pl.pallas_call(kernel, in_specs=[smem if x.ndim == 1 else vmem for x in o...  16.6 us
    ppermute x9, waiting for transfers between devices, move(): return lax.ppermute(value, 'row', way)  14.3 us
    all_gather x1, blocking collectives, local(): nodes = lax.all_gather(part, 'leaf', axis=0, axis_index_groups=window)  14.3 us
    ppermute x1, waiting for transfers between devices, local(): sibling = lax.ppermute(piece, 'leaf', [(i, i ^ 1) for i in range(leaves)])  3.66 us
    ppermute x1, starting transfers between devices, local(): sibling = lax.ppermute(piece, 'leaf', [(i, i ^ 1) for i in range(leaves)])  2.85 us
  transfers between devices with their start and end apart: 10, of which 7 were waited for; matrix products, arithmetic and copies ran while one was open for 0% of the time, Pallas kernels for 4%

profile of v4, /device:TPU:6, one launch (start us, length us, event | category | flops | bytes accessed | tf_op | source)
XLA Modules:
  0.0 132.0 jit_solution(9685652161038198967)
XLA Ops:
  1.1 1.9 %collective-permute-start = (bf16[512,512]{1,0:T(8,128)(2,1)S(1)}, bf16[512,512]{1,0:T(8,128)(2,1)S(1)}, u32[]{:S(2)}, u32[]{:S(2)}) collective-permute-start(bf16[512,512]{1,0:T(8,128)(2,1)S(1)} %pad_maximum_fusion.own_ref), channel_id=1, source_target_pairs={{0,1},{1,0},{2,3},{3,2},{4,5},{5,4},{6,7},{7,6},{8,9},{9,8},{10,11... | collective-permute-start | bytes 1572872 | tf_op jit(solution)/shard_map/ppermute | solution.py:197
  3.0 6.1 %collective-permute-start.2 = (bf16[512,512]{1,0:T(8,128)(2,1)S(1)}, bf16[512,512]{1,0:T(8,128)(2,1)S(1)}, u32[]{:S(2)}, u32[]{:S(2)}) collective-permute-start(bf16[512,512]{1,0:T(8,128)(2,1)S(1)} %pad_maximum_fusion.own_ref), channel_id=1, source_target_pairs={{0,2},{1,7},{2,4},{3,1},{4,6},{5,3},{6,0},{7,5},{8,10},{9,15},{10,... | collective-permute-start | bytes 1572872 | tf_op jit(solution)/shard_map/ppermute | solution.py:197
  9.3 2.2 %copy-done = bf16[1,512,4096]{2,1,0:T(8,128)(2,1)S(1)} copy-done((bf16[1,512,4096]{2,1,0:T(8,128)(2,1)S(1)}, bf16[1,512,4096]{2,1,0:T(8,128)(2,1)}, u32[]{:S(2)}) %copy-start) | copy-done | bytes 4194328
  13.5 7.3 %collective-permute-start.1 = (bf16[512,512]{1,0:T(8,128)(2,1)S(1)}, bf16[512,512]{1,0:T(8,128)(2,1)S(1)}, u32[]{:S(2)}, u32[]{:S(2)}) collective-permute-start(bf16[512,512]{1,0:T(8,128)(2,1)S(1)} %collective-permute-done.refs_0_), channel_id=1, source_target_pairs={{0,2},{1,7},{2,4},{3,1},{4,6},{5,3},{6,0},{7,5},{8,10},{9,15},{10,... | collective-permute-start | bytes 1572872 | tf_op jit(solution)/shard_map/ppermute | solution.py:197
  21.3 13.0 %collective-permute-start.4 = (bf16[512,512]{1,0:T(8,128)(2,1)S(1)}, bf16[512,512]{1,0:T(8,128)(2,1)S(1)}, u32[]{:S(2)}, u32[]{:S(2)}) collective-permute-start(bf16[512,512]{1,0:T(8,128)(2,1)S(1)} %collective-permute-done.2.refs_0_), channel_id=1, source_target_pairs={{0,2},{1,7},{2,4},{3,1},{4,6},{5,3},{6,0},{7,5},{8,10},{9,15},{10,... | collective-permute-start | bytes 1572872 | tf_op jit(solution)/shard_map/ppermute | solution.py:197
  35.3 1.9 %collective-permute-start.6 = (bf16[512,512]{1,0:T(8,128)(2,1)S(1)}, bf16[512,512]{1,0:T(8,128)(2,1)S(1)}, u32[]{:S(2)}, u32[]{:S(2)}) collective-permute-start(bf16[512,512]{1,0:T(8,128)(2,1)S(1)} %collective-permute-done.2.refs_0_), channel_id=1, source_target_pairs={{0,1},{1,0},{2,3},{3,2},{4,5},{5,4},{6,7},{7,6},{8,9},{9,8},{10,11... | collective-permute-start | bytes 1572872 | tf_op jit(solution)/shard_map/ppermute | solution.py:197
  37.2 3.2 %collective-permute-done.1.refs_0_ = bf16[512,512]{1,0:T(8,128)(2,1)S(1)} collective-permute-done((bf16[512,512]{1,0:T(8,128)(2,1)S(1)}, bf16[512,512]{1,0:T(8,128)(2,1)S(1)}, u32[]{:S(2)}, u32[]{:S(2)}) %collective-permute-start.1) | collective-permute-done | bytes 524320 | tf_op jit(solution)/shard_map/ppermute | solution.py:197
  41.4 2.1 %collective-permute-start.3 = (bf16[512,512]{1,0:T(8,128)(2,1)S(1)}, bf16[512,512]{1,0:T(8,128)(2,1)S(1)}, u32[]{:S(2)}, u32[]{:S(2)}) collective-permute-start(bf16[512,512]{1,0:T(8,128)(2,1)S(1)} %collective-permute-done.1.refs_0_), channel_id=1, source_target_pairs={{0,1},{1,0},{2,3},{3,2},{4,5},{5,4},{6,7},{7,6},{8,9},{9,8},{10,11... | collective-permute-start | bytes 1572872 | tf_op jit(solution)/shard_map/ppermute | solution.py:197
  43.5 6.2 %collective-permute-done.4.refs_1_ = bf16[512,512]{1,0:T(8,128)(2,1)S(1)} collective-permute-done((bf16[512,512]{1,0:T(8,128)(2,1)S(1)}, bf16[512,512]{1,0:T(8,128)(2,1)S(1)}, u32[]{:S(2)}, u32[]{:S(2)}) %collective-permute-start.4) | collective-permute-done | bytes 524320 | tf_op jit(solution)/shard_map/ppermute | solution.py:197
  49.7 1.9 %collective-permute-start.5 = (bf16[512,512]{1,0:T(8,128)(2,1)S(1)}, bf16[512,512]{1,0:T(8,128)(2,1)S(1)}, u32[]{:S(2)}, u32[]{:S(2)}) collective-permute-start(bf16[512,512]{1,0:T(8,128)(2,1)S(1)} %collective-permute-done.4.refs_1_), channel_id=1, source_target_pairs={{0,1},{1,0},{2,3},{3,2},{4,5},{5,4},{6,7},{7,6},{8,9},{9,8},{10,11... | collective-permute-start | bytes 1572872 | tf_op jit(solution)/shard_map/ppermute | solution.py:197
  51.6 1.2 shard_map.50.before_ref
  53.5 1.8 %shard_map.51 = (f32[512,512]{1,0:T(8,128)S(1)}, f32[192,512]{1,0:T(8,128)S(1)}, f32[192,512]{1,0:T(8,128)S(1)}) custom-call(s32[11]{0:T(128)S(1)} %stack.56.where_ref, bf16[512,4096]{1,0:T(8,128)(2,1)S(1)} %bitcast.26, bf16[512,512]{1,0:T(8,128)(2,1)S(1)} %collective-permute-done.3.next_near_ref, bf16[512,512]{1,0:T(8,128)(2,1)S(1)} %collective-permute-done.5.far_ref, ...), custom_call_target="tpu_custom_call" | custom-call | flops 1000000000 | bytes 10000000 | tf_op jit(solution)/shard_map/pallas_call | solution.py:172
  55.3 2.0 %collective-permute-start.7 = (f32[192,512]{1,0:T(8,128)S(1)}, f32[192,512]{1,0:T(8,128)S(1)}, u32[]{:S(2)}, u32[]{:S(2)}) collective-permute-start(f32[192,512]{1,0:T(8,128)S(1)} %get-tuple-element.23), channel_id=1, source_target_pairs={{0,1},{1,0},{2,3},{3,2},{4,5},{5,4},{6,7},{7,6},{8,9},{9,8},{10,11... | collective-permute-start | bytes 1179656 | tf_op jit(solution)/shard_map/ppermute | solution.py:197
  57.4 1.6 %collective-permute-done.7 = f32[192,512]{1,0:T(8,128)S(1)} collective-permute-done((f32[192,512]{1,0:T(8,128)S(1)}, f32[192,512]{1,0:T(8,128)S(1)}, u32[]{:S(2)}, u32[]{:S(2)}) %collective-permute-start.7) | collective-permute-done | bytes 393248 | tf_op jit(solution)/shard_map/ppermute | solution.py:197
  59.0 19.2 %all_to_all.5 = f32[4,48,512]{2,1,0:T(8,128)S(1)} all-to-all(f32[4,48,512]{2,1,0:T(8,128)S(1)} %bitcast.31), channel_id=1, replica_groups={{0,2,4,6},{1,3,5,7},{8,10,12,14},{9,11,13,15},{16,18,20,22},{17,19,21,2..., dimensions={0} | all-to-all | bytes 786432 | tf_op jit(solution)/shard_map/all_to_all | solution.py:232
  78.3 2.8 %collective-permute-start.8 = (f32[48,512]{1,0:T(8,128)S(1)}, f32[48,512]{1,0:T(8,128)S(1)}, u32[]{:S(2)}, u32[]{:S(2)}) collective-permute-start(f32[48,512]{1,0:T(8,128)S(1)} %reduce_sum.9), channel_id=1, source_target_pairs={{0,8},{8,0},{16,24},{24,16},{32,40},{40,32},{48,56},{56,48},{64,72... | collective-permute-start | bytes 294920 | tf_op jit(solution)/shard_map/ppermute | solution.py:234
  81.1 3.7 %collective-permute-done.8 = f32[48,512]{1,0:T(8,128)S(1)} collective-permute-done((f32[48,512]{1,0:T(8,128)S(1)}, f32[48,512]{1,0:T(8,128)S(1)}, u32[]{:S(2)}, u32[]{:S(2)}) %collective-permute-start.8) | collective-permute-done | bytes 98336 | tf_op jit(solution)/shard_map/ppermute | solution.py:234
  84.8 16.8 %all_gather.15.own_ref = f32[2,192,512]{2,1,0:T(8,128)S(1)} all-gather(f32[2,48,512]{2,1,0:T(8,128)S(1)} %pad_maximum_fusion.1), channel_id=1, replica_groups={{0,2,4,6},{1,3,5,7},{8,10,12,14},{9,11,13,15},{16,18,20,22},{17,19,21,2..., dimensions={1}, use_global_device_ids=true | all-gather | bytes 983040 | tf_op jit(solution)/shard_map/all_gather | solution.py:236
  101.6 2.2 %all-gather = f32[4,64,512]{2,1,0:T(8,128)S(1)} all-gather(f32[2,64,512]{2,1,0:T(8,128)S(1)} %slice.4), channel_id=2, replica_groups={{0,1},{2,3},{4,5},{6,7},{8,9},{10,11},{12,13},{14,15},{16,17},{18,19},{..., dimensions={0}, use_global_device_ids=true | all-gather | bytes 786432 | tf_op jit(solution)/shard_map/all_gather | solution.py:239
  103.8 2.1 %shard_map.52 = (f32[128,384]{1,0:T(8,128)S(1)}, f32[128,384]{1,0:T(8,128)S(1)}) custom-call(f32[2,192,512]{2,1,0:T(8,128)S(1)} %all_gather.15.own_ref, f32[2,2,64,512]{3,2,1,0:T(8,128)S(1)} %bitcast.29), custom_call_target="tpu_custom_call" | custom-call | flops 1000000000 | bytes 10000000 | tf_op jit(solution)/shard_map/pallas_call | solution.py:172
  106.0 14.3 %all-gather.1 = f32[512,384]{1,0:T(8,128)S(1)} all-gather(f32[128,384]{1,0:T(8,128)S(1)} %get-tuple-element.24), channel_id=3, replica_groups={{0,16,32,48},{8,24,40,56},{64,80,96,112},{72,88,104,120},{128,144,160,1..., dimensions={0}, use_global_device_ids=true | all-gather | bytes 983040 | tf_op jit(solution)/shard_map/all_gather | solution.py:247
  120.3 1.9 %collective-permute-start.9 = (f32[4,128,384]{2,1,0:T(8,128)S(1)}, f32[4,128,384]{2,1,0:T(8,128)S(1)}, u32[]{:S(2)}, u32[]{:S(2)}) collective-permute-start(f32[4,128,384]{2,1,0:T(8,128)S(1)} %bitcast.27), channel_id=1, source_target_pairs={{0,1},{1,0},{2,3},{3,2},{4,5},{5,4},{6,7},{7,6},{8,9},{9,8},{10,11... | collective-permute-start | bytes 2359304 | tf_op jit(solution)/shard_map/ppermute | solution.py:197
  122.2 2.3 %collective-permute-done.9.other_ref = f32[4,128,384]{2,1,0:T(8,128)S(1)} collective-permute-done((f32[4,128,384]{2,1,0:T(8,128)S(1)}, f32[4,128,384]{2,1,0:T(8,128)S(1)}, u32[]{:S(2)}, u32[]{:S(2)}) %collective-permute-start.9) | collective-permute-done | bytes 786464 | tf_op jit(solution)/shard_map/ppermute | solution.py:197
  124.5 7.5 %shard_map.53 = bf16[512,128]{1,0:T(8,128)(2,1)} custom-call(s32[11]{0:T(128)S(1)} %stack.56.where_ref, f32[4,128,384]{2,1,0:T(8,128)S(1)} %bitcast.28, f32[4,128,384]{2,1,0:T(8,128)S(1)} %collective-permute-done.9.other_ref, f32[128,384]{1,0:T(8,128)S(1)} %get-tuple-element.25.refs_0_, f32[512,512]{1,0:T(8,128)S(1)} %get-tuple-element.26.refs_1_), custom_call_target="tpu_custom_call" | custom-call | flops 1000000000 | bytes 10000000 | tf_op jit(solution)/shard_map/pallas_call | solution.py:172
  (18 shorter events, 6.3 us)
Async XLA Ops:
  1.1 11.4 %collective-permute-start = (bf16[512,512]{1,0:T(8,128)(2,1)S(1)}, bf16[512,512]{1,0:T(8,128)(2,1)S(1)}, u32[]{:S(2)}, u32[]{:S(2)}) collective-permute-start(bf16[512,512]{1,0:T(8,128)(2,1)S(1)} %pad_maximum_fusion.own_ref), channel_id=1, source_target_pairs={{0,1},{1,0},{2,3},{3,2},{4,5},{5,4},{6,7},{7,6},{8,9},{9,8},{10,11... | collective-permute-start | bytes 1572872 | tf_op jit(solution)/shard_map/ppermute | solution.py:197
  3.0 18.2 %collective-permute-start.2 = (bf16[512,512]{1,0:T(8,128)(2,1)S(1)}, bf16[512,512]{1,0:T(8,128)(2,1)S(1)}, u32[]{:S(2)}, u32[]{:S(2)}) collective-permute-start(bf16[512,512]{1,0:T(8,128)(2,1)S(1)} %pad_maximum_fusion.own_ref), channel_id=1, source_target_pairs={{0,2},{1,7},{2,4},{3,1},{4,6},{5,3},{6,0},{7,5},{8,10},{9,15},{10,... | collective-permute-start | bytes 1572872 | tf_op jit(solution)/shard_map/ppermute | solution.py:197
  9.3 2.2 %copy-start = (bf16[1,512,4096]{2,1,0:T(8,128)(2,1)S(1)}, bf16[1,512,4096]{2,1,0:T(8,128)(2,1)}, u32[]{:S(2)}) copy-start(bf16[1,512,4096]{2,1,0:T(8,128)(2,1)} %param.4) | copy-start | bytes 12582916
  13.5 26.9 %collective-permute-start.1 = (bf16[512,512]{1,0:T(8,128)(2,1)S(1)}, bf16[512,512]{1,0:T(8,128)(2,1)S(1)}, u32[]{:S(2)}, u32[]{:S(2)}) collective-permute-start(bf16[512,512]{1,0:T(8,128)(2,1)S(1)} %collective-permute-done.refs_0_), channel_id=1, source_target_pairs={{0,2},{1,7},{2,4},{3,1},{4,6},{5,3},{6,0},{7,5},{8,10},{9,15},{10,... | collective-permute-start | bytes 1572872 | tf_op jit(solution)/shard_map/ppermute | solution.py:197
  21.3 28.4 %collective-permute-start.4 = (bf16[512,512]{1,0:T(8,128)(2,1)S(1)}, bf16[512,512]{1,0:T(8,128)(2,1)S(1)}, u32[]{:S(2)}, u32[]{:S(2)}) collective-permute-start(bf16[512,512]{1,0:T(8,128)(2,1)S(1)} %collective-permute-done.2.refs_0_), channel_id=1, source_target_pairs={{0,2},{1,7},{2,4},{3,1},{4,6},{5,3},{6,0},{7,5},{8,10},{9,15},{10,... | collective-permute-start | bytes 1572872 | tf_op jit(solution)/shard_map/ppermute | solution.py:197
  35.3 16.4 %collective-permute-start.6 = (bf16[512,512]{1,0:T(8,128)(2,1)S(1)}, bf16[512,512]{1,0:T(8,128)(2,1)S(1)}, u32[]{:S(2)}, u32[]{:S(2)}) collective-permute-start(bf16[512,512]{1,0:T(8,128)(2,1)S(1)} %collective-permute-done.2.refs_0_), channel_id=1, source_target_pairs={{0,1},{1,0},{2,3},{3,2},{4,5},{5,4},{6,7},{7,6},{8,9},{9,8},{10,11... | collective-permute-start | bytes 1572872 | tf_op jit(solution)/shard_map/ppermute | solution.py:197
  41.4 12.1 %copy-start.1 = (bf16[1,512,384]{2,1,0:T(8,128)(2,1)S(1)}, bf16[1,512,384]{2,1,0:T(8,128)(2,1)}, u32[]{:S(2)}) copy-start(bf16[1,512,384]{2,1,0:T(8,128)(2,1)} %param.7) | copy-start | bytes 1179652
  41.4 11.5 %collective-permute-start.3 = (bf16[512,512]{1,0:T(8,128)(2,1)S(1)}, bf16[512,512]{1,0:T(8,128)(2,1)S(1)}, u32[]{:S(2)}, u32[]{:S(2)}) collective-permute-start(bf16[512,512]{1,0:T(8,128)(2,1)S(1)} %collective-permute-done.1.refs_0_), channel_id=1, source_target_pairs={{0,1},{1,0},{2,3},{3,2},{4,5},{5,4},{6,7},{7,6},{8,9},{9,8},{10,11... | collective-permute-start | bytes 1572872 | tf_op jit(solution)/shard_map/ppermute | solution.py:197
  49.7 3.8 %collective-permute-start.5 = (bf16[512,512]{1,0:T(8,128)(2,1)S(1)}, bf16[512,512]{1,0:T(8,128)(2,1)S(1)}, u32[]{:S(2)}, u32[]{:S(2)}) collective-permute-start(bf16[512,512]{1,0:T(8,128)(2,1)S(1)} %collective-permute-done.4.refs_1_), channel_id=1, source_target_pairs={{0,1},{1,0},{2,3},{3,2},{4,5},{5,4},{6,7},{7,6},{8,9},{9,8},{10,11... | collective-permute-start | bytes 1572872 | tf_op jit(solution)/shard_map/ppermute | solution.py:197
  55.3 3.6 %collective-permute-start.7 = (f32[192,512]{1,0:T(8,128)S(1)}, f32[192,512]{1,0:T(8,128)S(1)}, u32[]{:S(2)}, u32[]{:S(2)}) collective-permute-start(f32[192,512]{1,0:T(8,128)S(1)} %get-tuple-element.23), channel_id=1, source_target_pairs={{0,1},{1,0},{2,3},{3,2},{4,5},{5,4},{6,7},{7,6},{8,9},{9,8},{10,11... | collective-permute-start | bytes 1179656 | tf_op jit(solution)/shard_map/ppermute | solution.py:197
  78.3 6.5 %collective-permute-start.8 = (f32[48,512]{1,0:T(8,128)S(1)}, f32[48,512]{1,0:T(8,128)S(1)}, u32[]{:S(2)}, u32[]{:S(2)}) collective-permute-start(f32[48,512]{1,0:T(8,128)S(1)} %reduce_sum.9), channel_id=1, source_target_pairs={{0,8},{8,0},{16,24},{24,16},{32,40},{40,32},{48,56},{56,48},{64,72... | collective-permute-start | bytes 294920 | tf_op jit(solution)/shard_map/ppermute | solution.py:234
  120.3 4.2 %collective-permute-start.9 = (f32[4,128,384]{2,1,0:T(8,128)S(1)}, f32[4,128,384]{2,1,0:T(8,128)S(1)}, u32[]{:S(2)}, u32[]{:S(2)}) collective-permute-start(f32[4,128,384]{2,1,0:T(8,128)S(1)} %bitcast.27), channel_id=1, source_target_pairs={{0,1},{1,0},{2,3},{3,2},{4,5},{5,4},{6,7},{7,6},{8,9},{9,8},{10,11... | collective-permute-start | bytes 2359304 | tf_op jit(solution)/shard_map/ppermute | solution.py:197

commit v5 on v4

--- a/solution.py
+++ b/solution.py
@@ -136,7 +136,7 @@
         last_body(where_ref, other_ref, own_ref, *refs)
 
 
-def last_body(where_ref, v1_ref, v2_ref, coef_ref, y_ref, out_ref, c_ref, d_ref, p_ref):
+def last_body(where_ref, v1_ref, v2_ref, y_ref, out_ref, c_ref, d_ref, p_ref, z_ref):
     node = where_ref[2]
     pairs = ((node, node ^ 1), (node ^ 2, node ^ 3))
     systems = []
@@ -155,15 +155,14 @@
             total = part if total is None else total + part
         sums.append(total)
     own, other = sums
+    z_ref[...] = y_ref[:, R:] - dot(y_ref[:, :R], c_ref[0])
     product = dot(other[:, :R], own)
     solve([(product[:, :R], other[:, R:] - product[:, R:], d_ref, p_ref.at[0])])
-    x2 = d_ref[...]
-    c1 = c_ref[0]
-    c0 = coef_ref[...]
-    x1 = c1[:, R:] - dot(c1[:, :R], x2)
-    x0 = c0[:, 2 * R :] - dot(c0[:, :R], x1) - dot(c0[:, R : 2 * R], x2)
-    x = jnp.concatenate([x0, x1, x2], axis=0)
-    out_ref[...] = (y_ref[:, 3 * R :] - dot(y_ref[:, : 3 * R], x)).astype(BF16)
+    out_ref[...] = (z_ref[:, R:] - dot(z_ref[:, :R], d_ref[...])).astype(BF16)
+
+
+def lift_kernel(coef_ref, y_ref, out_ref):
+    out_ref[...] = y_ref[:, R:] - dot(y_ref[:, :R], coef_ref[...])
 
 
 def whole(kernel, outs, scratch, operands):
@@ -246,6 +245,7 @@
     window = [[8 * g + 2 * n + low for n in range(4)] for g in range(leaves // 8) for low in range(2)]
     nodes = lax.all_gather(part, "leaf", axis=0, axis_index_groups=window)
     others = move(nodes, swap)
+    y = whole(lift_kernel, [jax.ShapeDtypeStruct((BLOCK, width - R), F32)], [], (coef, y))
     out = whole(
         last_levels,
         [jax.ShapeDtypeStruct((y.shape[0], R), BF16)],
@@ -253,8 +253,9 @@
             pltpu.VMEM((2, R, 2 * R), F32),
             pltpu.VMEM((R, R), F32),
             pltpu.VMEM((2, R, R), F32),
+            pltpu.VMEM((BLOCK, 2 * R), F32),
         ],
-        (where, nodes, others, coef, y),
+        (where, nodes, others, y),
     )
     return out[None]
 

time: 134 us -> 132 us (0.985)
    pallas_call x8 -> x9, Pallas kernels: 16.6 us -> 16.6 us  [whole(): pl.pallas_call(kernel, in_specs=[smem if x.ndim == 1 else vmem for x in o...]
  transfers between devices with their start and end apart: 10 -> 10, of which waited for: 7 -> 7; matrix products, arithmetic and copies ran while one was open for 0% -> 0% of each run, Pallas kernels for 4% -> 5%
where the time goes in v5:
time: 132 us; the launch traced here: 131 us
  blocking collectives  52.6 us (40%)
  starting transfers between devices  41 us (31%)
  waiting for transfers between devices  17.2 us (13%)
  Pallas kernels  16.6 us (13%)
  local copies, waits for them, and re-layouts  2.3 us (2%)
    ppermute x9, starting transfers between devices, move(): return lax.ppermute(value, 'row', way)  38.1 us
    all_to_all x1, blocking collectives, local(): lax.all_to_all(keep.reshape(4, quarter, width), 'row', 0, 0, tiled=True,...  19.2 us
    all_gather x1, blocking collectives, local(): lax.all_gather(both, 'row', axis=1, tiled=True, axis_index_groups=same_core)  16.8 us
    pallas_call x9, Pallas kernels, whole(): pl.pallas_call(kernel, in_specs=[smem if x.ndim == 1 else vmem for x in o...  16.6 us
    all_gather x1, blocking collectives, local(): nodes = lax.all_gather(part, 'leaf', axis=0, axis_index_groups=window)  14.3 us
    ppermute x9, waiting for transfers between devices, move(): return lax.ppermute(value, 'row', way)  13.5 us
    ppermute x1, waiting for transfers between devices, local(): sibling = lax.ppermute(piece, 'leaf', [(i, i ^ 1) for i in range(leaves)])  3.66 us
    ppermute x1, starting transfers between devices, local(): sibling = lax.ppermute(piece, 'leaf', [(i, i ^ 1) for i in range(leaves)])  2.85 us
  transfers between devices with their start and end apart: 10, of which 7 were waited for; matrix products, arithmetic and copies ran while one was open for 0% of the time, Pallas kernels for 5%

profile of v5, /device:TPU:6, one launch (start us, length us, event | category | flops | bytes accessed | tf_op | source)
XLA Modules:
  0.0 131.2 jit_solution(6899762357499285127)
XLA Ops:
  1.1 1.9 %collective-permute-start = (bf16[512,512]{1,0:T(8,128)(2,1)S(1)}, bf16[512,512]{1,0:T(8,128)(2,1)S(1)}, u32[]{:S(2)}, u32[]{:S(2)}) collective-permute-start(bf16[512,512]{1,0:T(8,128)(2,1)S(1)} %pad_maximum_fusion.own_ref), channel_id=1, source_target_pairs={{0,1},{1,0},{2,3},{3,2},{4,5},{5,4},{6,7},{7,6},{8,9},{9,8},{10,11... | collective-permute-start | bytes 1572872 | tf_op jit(solution)/shard_map/ppermute | solution.py:196
  3.0 6.1 %collective-permute-start.2 = (bf16[512,512]{1,0:T(8,128)(2,1)S(1)}, bf16[512,512]{1,0:T(8,128)(2,1)S(1)}, u32[]{:S(2)}, u32[]{:S(2)}) collective-permute-start(bf16[512,512]{1,0:T(8,128)(2,1)S(1)} %pad_maximum_fusion.own_ref), channel_id=1, source_target_pairs={{0,2},{1,7},{2,4},{3,1},{4,6},{5,3},{6,0},{7,5},{8,10},{9,15},{10,... | collective-permute-start | bytes 1572872 | tf_op jit(solution)/shard_map/ppermute | solution.py:196
  9.3 2.2 %copy-done = bf16[1,512,4096]{2,1,0:T(8,128)(2,1)S(1)} copy-done((bf16[1,512,4096]{2,1,0:T(8,128)(2,1)S(1)}, bf16[1,512,4096]{2,1,0:T(8,128)(2,1)}, u32[]{:S(2)}) %copy-start) | copy-done | bytes 4194328
  13.5 7.3 %collective-permute-start.1 = (bf16[512,512]{1,0:T(8,128)(2,1)S(1)}, bf16[512,512]{1,0:T(8,128)(2,1)S(1)}, u32[]{:S(2)}, u32[]{:S(2)}) collective-permute-start(bf16[512,512]{1,0:T(8,128)(2,1)S(1)} %collective-permute-done.refs_0_), channel_id=1, source_target_pairs={{0,2},{1,7},{2,4},{3,1},{4,6},{5,3},{6,0},{7,5},{8,10},{9,15},{10,... | collective-permute-start | bytes 1572872 | tf_op jit(solution)/shard_map/ppermute | solution.py:196
  21.3 13.0 %collective-permute-start.4 = (bf16[512,512]{1,0:T(8,128)(2,1)S(1)}, bf16[512,512]{1,0:T(8,128)(2,1)S(1)}, u32[]{:S(2)}, u32[]{:S(2)}) collective-permute-start(bf16[512,512]{1,0:T(8,128)(2,1)S(1)} %collective-permute-done.2.refs_0_), channel_id=1, source_target_pairs={{0,2},{1,7},{2,4},{3,1},{4,6},{5,3},{6,0},{7,5},{8,10},{9,15},{10,... | collective-permute-start | bytes 1572872 | tf_op jit(solution)/shard_map/ppermute | solution.py:196
  35.3 1.9 %collective-permute-start.6 = (bf16[512,512]{1,0:T(8,128)(2,1)S(1)}, bf16[512,512]{1,0:T(8,128)(2,1)S(1)}, u32[]{:S(2)}, u32[]{:S(2)}) collective-permute-start(bf16[512,512]{1,0:T(8,128)(2,1)S(1)} %collective-permute-done.2.refs_0_), channel_id=1, source_target_pairs={{0,1},{1,0},{2,3},{3,2},{4,5},{5,4},{6,7},{7,6},{8,9},{9,8},{10,11... | collective-permute-start | bytes 1572872 | tf_op jit(solution)/shard_map/ppermute | solution.py:196
  37.2 3.2 %collective-permute-done.1.refs_0_ = bf16[512,512]{1,0:T(8,128)(2,1)S(1)} collective-permute-done((bf16[512,512]{1,0:T(8,128)(2,1)S(1)}, bf16[512,512]{1,0:T(8,128)(2,1)S(1)}, u32[]{:S(2)}, u32[]{:S(2)}) %collective-permute-start.1) | collective-permute-done | bytes 524320 | tf_op jit(solution)/shard_map/ppermute | solution.py:196
  41.4 2.1 %collective-permute-start.3 = (bf16[512,512]{1,0:T(8,128)(2,1)S(1)}, bf16[512,512]{1,0:T(8,128)(2,1)S(1)}, u32[]{:S(2)}, u32[]{:S(2)}) collective-permute-start(bf16[512,512]{1,0:T(8,128)(2,1)S(1)} %collective-permute-done.1.refs_0_), channel_id=1, source_target_pairs={{0,1},{1,0},{2,3},{3,2},{4,5},{5,4},{6,7},{7,6},{8,9},{9,8},{10,11... | collective-permute-start | bytes 1572872 | tf_op jit(solution)/shard_map/ppermute | solution.py:196
  43.5 6.2 %collective-permute-done.4.refs_1_ = bf16[512,512]{1,0:T(8,128)(2,1)S(1)} collective-permute-done((bf16[512,512]{1,0:T(8,128)(2,1)S(1)}, bf16[512,512]{1,0:T(8,128)(2,1)S(1)}, u32[]{:S(2)}, u32[]{:S(2)}) %collective-permute-start.4) | collective-permute-done | bytes 524320 | tf_op jit(solution)/shard_map/ppermute | solution.py:196
  49.7 1.9 %collective-permute-start.5 = (bf16[512,512]{1,0:T(8,128)(2,1)S(1)}, bf16[512,512]{1,0:T(8,128)(2,1)S(1)}, u32[]{:S(2)}, u32[]{:S(2)}) collective-permute-start(bf16[512,512]{1,0:T(8,128)(2,1)S(1)} %collective-permute-done.4.refs_1_), channel_id=1, source_target_pairs={{0,1},{1,0},{2,3},{3,2},{4,5},{5,4},{6,7},{7,6},{8,9},{9,8},{10,11... | collective-permute-start | bytes 1572872 | tf_op jit(solution)/shard_map/ppermute | solution.py:196
  51.6 1.2 shard_map.50.before_ref
  53.5 1.8 %shard_map.51 = (f32[512,512]{1,0:T(8,128)S(1)}, f32[192,512]{1,0:T(8,128)S(1)}, f32[192,512]{1,0:T(8,128)S(1)}) custom-call(s32[11]{0:T(128)S(1)} %stack.56.where_ref, bf16[512,4096]{1,0:T(8,128)(2,1)S(1)} %bitcast.26, bf16[512,512]{1,0:T(8,128)(2,1)S(1)} %collective-permute-done.3.next_near_ref, bf16[512,512]{1,0:T(8,128)(2,1)S(1)} %collective-permute-done.5.far_ref, ...), custom_call_target="tpu_custom_call" | custom-call | flops 1000000000 | bytes 10000000 | tf_op jit(solution)/shard_map/pallas_call | solution.py:171
  55.3 2.0 %collective-permute-start.7 = (f32[192,512]{1,0:T(8,128)S(1)}, f32[192,512]{1,0:T(8,128)S(1)}, u32[]{:S(2)}, u32[]{:S(2)}) collective-permute-start(f32[192,512]{1,0:T(8,128)S(1)} %get-tuple-element.23), channel_id=1, source_target_pairs={{0,1},{1,0},{2,3},{3,2},{4,5},{5,4},{6,7},{7,6},{8,9},{9,8},{10,11... | collective-permute-start | bytes 1179656 | tf_op jit(solution)/shard_map/ppermute | solution.py:196
  57.4 1.6 %collective-permute-done.7 = f32[192,512]{1,0:T(8,128)S(1)} collective-permute-done((f32[192,512]{1,0:T(8,128)S(1)}, f32[192,512]{1,0:T(8,128)S(1)}, u32[]{:S(2)}, u32[]{:S(2)}) %collective-permute-start.7) | collective-permute-done | bytes 393248 | tf_op jit(solution)/shard_map/ppermute | solution.py:196
  59.0 19.2 %all_to_all.5 = f32[4,48,512]{2,1,0:T(8,128)S(1)} all-to-all(f32[4,48,512]{2,1,0:T(8,128)S(1)} %bitcast.31), channel_id=1, replica_groups={{0,2,4,6},{1,3,5,7},{8,10,12,14},{9,11,13,15},{16,18,20,22},{17,19,21,2..., dimensions={0} | all-to-all | bytes 786432 | tf_op jit(solution)/shard_map/all_to_all | solution.py:231
  78.3 2.8 %collective-permute-start.8 = (f32[48,512]{1,0:T(8,128)S(1)}, f32[48,512]{1,0:T(8,128)S(1)}, u32[]{:S(2)}, u32[]{:S(2)}) collective-permute-start(f32[48,512]{1,0:T(8,128)S(1)} %reduce_sum.9), channel_id=1, source_target_pairs={{0,8},{8,0},{16,24},{24,16},{32,40},{40,32},{48,56},{56,48},{64,72... | collective-permute-start | bytes 294920 | tf_op jit(solution)/shard_map/ppermute | solution.py:233
  81.1 3.7 %collective-permute-done.8 = f32[48,512]{1,0:T(8,128)S(1)} collective-permute-done((f32[48,512]{1,0:T(8,128)S(1)}, f32[48,512]{1,0:T(8,128)S(1)}, u32[]{:S(2)}, u32[]{:S(2)}) %collective-permute-start.8) | collective-permute-done | bytes 98336 | tf_op jit(solution)/shard_map/ppermute | solution.py:233
  84.8 16.8 %all_gather.15.own_ref = f32[2,192,512]{2,1,0:T(8,128)S(1)} all-gather(f32[2,48,512]{2,1,0:T(8,128)S(1)} %pad_maximum_fusion.1), channel_id=1, replica_groups={{0,2,4,6},{1,3,5,7},{8,10,12,14},{9,11,13,15},{16,18,20,22},{17,19,21,2..., dimensions={1}, use_global_device_ids=true | all-gather | bytes 983040 | tf_op jit(solution)/shard_map/all_gather | solution.py:235
  101.6 2.2 %all-gather = f32[4,64,512]{2,1,0:T(8,128)S(1)} all-gather(f32[2,64,512]{2,1,0:T(8,128)S(1)} %slice.4), channel_id=2, replica_groups={{0,1},{2,3},{4,5},{6,7},{8,9},{10,11},{12,13},{14,15},{16,17},{18,19},{..., dimensions={0}, use_global_device_ids=true | all-gather | bytes 786432 | tf_op jit(solution)/shard_map/all_gather | solution.py:238
  103.8 2.1 %shard_map.52 = (f32[128,384]{1,0:T(8,128)S(1)}, f32[128,384]{1,0:T(8,128)S(1)}) custom-call(f32[2,192,512]{2,1,0:T(8,128)S(1)} %all_gather.15.own_ref, f32[2,2,64,512]{3,2,1,0:T(8,128)S(1)} %bitcast.29), custom_call_target="tpu_custom_call" | custom-call | flops 1000000000 | bytes 10000000 | tf_op jit(solution)/shard_map/pallas_call | solution.py:171
  106.0 14.3 %all-gather.1 = f32[512,384]{1,0:T(8,128)S(1)} all-gather(f32[128,384]{1,0:T(8,128)S(1)} %get-tuple-element.24), channel_id=3, replica_groups={{0,16,32,48},{8,24,40,56},{64,80,96,112},{72,88,104,120},{128,144,160,1..., dimensions={0}, use_global_device_ids=true | all-gather | bytes 983040 | tf_op jit(solution)/shard_map/all_gather | solution.py:246
  120.3 1.9 %collective-permute-start.9 = (f32[4,128,384]{2,1,0:T(8,128)S(1)}, f32[4,128,384]{2,1,0:T(8,128)S(1)}, u32[]{:S(2)}, u32[]{:S(2)}) collective-permute-start(f32[4,128,384]{2,1,0:T(8,128)S(1)} %bitcast.27), channel_id=1, source_target_pairs={{0,1},{1,0},{2,3},{3,2},{4,5},{5,4},{6,7},{7,6},{8,9},{9,8},{10,11... | collective-permute-start | bytes 2359304 | tf_op jit(solution)/shard_map/ppermute | solution.py:196
  123.0 1.5 %collective-permute-done.9.other_ref = f32[4,128,384]{2,1,0:T(8,128)S(1)} collective-permute-done((f32[4,128,384]{2,1,0:T(8,128)S(1)}, f32[4,128,384]{2,1,0:T(8,128)S(1)}, u32[]{:S(2)}, u32[]{:S(2)}) %collective-permute-start.9) | collective-permute-done | bytes 786464 | tf_op jit(solution)/shard_map/ppermute | solution.py:196
  124.5 6.7 %shard_map.54 = bf16[512,128]{1,0:T(8,128)(2,1)} custom-call(s32[11]{0:T(128)S(1)} %stack.56.where_ref, f32[4,128,384]{2,1,0:T(8,128)S(1)} %bitcast.28, f32[4,128,384]{2,1,0:T(8,128)S(1)} %collective-permute-done.9.other_ref, f32[512,384]{1,0:T(8,128)S(1)} %shard_map.53.refs_0_), custom_call_target="tpu_custom_call" | custom-call | flops 1000000000 | bytes 10000000 | tf_op jit(solution)/shard_map/pallas_call | solution.py:171
  (19 shorter events, 7.1 us)
Async XLA Ops:
  1.1 11.4 %collective-permute-start = (bf16[512,512]{1,0:T(8,128)(2,1)S(1)}, bf16[512,512]{1,0:T(8,128)(2,1)S(1)}, u32[]{:S(2)}, u32[]{:S(2)}) collective-permute-start(bf16[512,512]{1,0:T(8,128)(2,1)S(1)} %pad_maximum_fusion.own_ref), channel_id=1, source_target_pairs={{0,1},{1,0},{2,3},{3,2},{4,5},{5,4},{6,7},{7,6},{8,9},{9,8},{10,11... | collective-permute-start | bytes 1572872 | tf_op jit(solution)/shard_map/ppermute | solution.py:196
  3.0 18.2 %collective-permute-start.2 = (bf16[512,512]{1,0:T(8,128)(2,1)S(1)}, bf16[512,512]{1,0:T(8,128)(2,1)S(1)}, u32[]{:S(2)}, u32[]{:S(2)}) collective-permute-start(bf16[512,512]{1,0:T(8,128)(2,1)S(1)} %pad_maximum_fusion.own_ref), channel_id=1, source_target_pairs={{0,2},{1,7},{2,4},{3,1},{4,6},{5,3},{6,0},{7,5},{8,10},{9,15},{10,... | collective-permute-start | bytes 1572872 | tf_op jit(solution)/shard_map/ppermute | solution.py:196
  9.3 2.2 %copy-start = (bf16[1,512,4096]{2,1,0:T(8,128)(2,1)S(1)}, bf16[1,512,4096]{2,1,0:T(8,128)(2,1)}, u32[]{:S(2)}) copy-start(bf16[1,512,4096]{2,1,0:T(8,128)(2,1)} %param.4) | copy-start | bytes 12582916
  13.5 26.9 %collective-permute-start.1 = (bf16[512,512]{1,0:T(8,128)(2,1)S(1)}, bf16[512,512]{1,0:T(8,128)(2,1)S(1)}, u32[]{:S(2)}, u32[]{:S(2)}) collective-permute-start(bf16[512,512]{1,0:T(8,128)(2,1)S(1)} %collective-permute-done.refs_0_), channel_id=1, source_target_pairs={{0,2},{1,7},{2,4},{3,1},{4,6},{5,3},{6,0},{7,5},{8,10},{9,15},{10,... | collective-permute-start | bytes 1572872 | tf_op jit(solution)/shard_map/ppermute | solution.py:196
  21.3 28.4 %collective-permute-start.4 = (bf16[512,512]{1,0:T(8,128)(2,1)S(1)}, bf16[512,512]{1,0:T(8,128)(2,1)S(1)}, u32[]{:S(2)}, u32[]{:S(2)}) collective-permute-start(bf16[512,512]{1,0:T(8,128)(2,1)S(1)} %collective-permute-done.2.refs_0_), channel_id=1, source_target_pairs={{0,2},{1,7},{2,4},{3,1},{4,6},{5,3},{6,0},{7,5},{8,10},{9,15},{10,... | collective-permute-start | bytes 1572872 | tf_op jit(solution)/shard_map/ppermute | solution.py:196
  35.3 16.4 %collective-permute-start.6 = (bf16[512,512]{1,0:T(8,128)(2,1)S(1)}, bf16[512,512]{1,0:T(8,128)(2,1)S(1)}, u32[]{:S(2)}, u32[]{:S(2)}) collective-permute-start(bf16[512,512]{1,0:T(8,128)(2,1)S(1)} %collective-permute-done.2.refs_0_), channel_id=1, source_target_pairs={{0,1},{1,0},{2,3},{3,2},{4,5},{5,4},{6,7},{7,6},{8,9},{9,8},{10,11... | collective-permute-start | bytes 1572872 | tf_op jit(solution)/shard_map/ppermute | solution.py:196
  41.4 12.1 %copy-start.1 = (bf16[1,512,384]{2,1,0:T(8,128)(2,1)S(1)}, bf16[1,512,384]{2,1,0:T(8,128)(2,1)}, u32[]{:S(2)}) copy-start(bf16[1,512,384]{2,1,0:T(8,128)(2,1)} %param.7) | copy-start | bytes 1179652
  41.4 11.5 %collective-permute-start.3 = (bf16[512,512]{1,0:T(8,128)(2,1)S(1)}, bf16[512,512]{1,0:T(8,128)(2,1)S(1)}, u32[]{:S(2)}, u32[]{:S(2)}) collective-permute-start(bf16[512,512]{1,0:T(8,128)(2,1)S(1)} %collective-permute-done.1.refs_0_), channel_id=1, source_target_pairs={{0,1},{1,0},{2,3},{3,2},{4,5},{5,4},{6,7},{7,6},{8,9},{9,8},{10,11... | collective-permute-start | bytes 1572872 | tf_op jit(solution)/shard_map/ppermute | solution.py:196
  49.7 3.8 %collective-permute-start.5 = (bf16[512,512]{1,0:T(8,128)(2,1)S(1)}, bf16[512,512]{1,0:T(8,128)(2,1)S(1)}, u32[]{:S(2)}, u32[]{:S(2)}) collective-permute-start(bf16[512,512]{1,0:T(8,128)(2,1)S(1)} %collective-permute-done.4.refs_1_), channel_id=1, source_target_pairs={{0,1},{1,0},{2,3},{3,2},{4,5},{5,4},{6,7},{7,6},{8,9},{9,8},{10,11... | collective-permute-start | bytes 1572872 | tf_op jit(solution)/shard_map/ppermute | solution.py:196
  55.3 3.6 %collective-permute-start.7 = (f32[192,512]{1,0:T(8,128)S(1)}, f32[192,512]{1,0:T(8,128)S(1)}, u32[]{:S(2)}, u32[]{:S(2)}) collective-permute-start(f32[192,512]{1,0:T(8,128)S(1)} %get-tuple-element.23), channel_id=1, source_target_pairs={{0,1},{1,0},{2,3},{3,2},{4,5},{5,4},{6,7},{7,6},{8,9},{9,8},{10,11... | collective-permute-start | bytes 1179656 | tf_op jit(solution)/shard_map/ppermute | solution.py:196
  78.3 6.5 %collective-permute-start.8 = (f32[48,512]{1,0:T(8,128)S(1)}, f32[48,512]{1,0:T(8,128)S(1)}, u32[]{:S(2)}, u32[]{:S(2)}) collective-permute-start(f32[48,512]{1,0:T(8,128)S(1)} %reduce_sum.9), channel_id=1, source_target_pairs={{0,8},{8,0},{16,24},{24,16},{32,40},{40,32},{48,56},{56,48},{64,72... | collective-permute-start | bytes 294920 | tf_op jit(solution)/shard_map/ppermute | solution.py:233
  120.3 4.2 %collective-permute-start.9 = (f32[4,128,384]{2,1,0:T(8,128)S(1)}, f32[4,128,384]{2,1,0:T(8,128)S(1)}, u32[]{:S(2)}, u32[]{:S(2)}) collective-permute-start(f32[4,128,384]{2,1,0:T(8,128)S(1)} %bitcast.27), channel_id=1, source_target_pairs={{0,1},{1,0},{2,3},{3,2},{4,5},{5,4},{6,7},{7,6},{8,9},{9,8},{10,11... | collective-permute-start | bytes 2359304 | tf_op jit(solution)/shard_map/ppermute | solution.py:196

commit v6 on v5

--- a/solution.py
+++ b/solution.py
@@ -43,13 +43,13 @@
         c_ref[...] = c_ref[...] + dot(x, right - dot(a, c_ref[...]))
 
 
-def solve(systems):
+def solve(systems, rounds=2):
     left = jnp.float32(0)
     grown = jnp.float32(0)
     for s, right, c_ref, p_ref in systems:
         c = right + dot(s, right)
         p = dot(s, s)
-        for _ in range(2):
+        for _ in range(rounds):
             c = c + dot(p, c)
             p = dot(p, p)
         c_ref[...] = c
@@ -157,7 +157,7 @@
     own, other = sums
     z_ref[...] = y_ref[:, R:] - dot(y_ref[:, :R], c_ref[0])
     product = dot(other[:, :R], own)
-    solve([(product[:, :R], other[:, R:] - product[:, R:], d_ref, p_ref.at[0])])
+    solve([(product[:, :R], other[:, R:] - product[:, R:], d_ref, p_ref.at[0])], rounds=3)
     out_ref[...] = (z_ref[:, R:] - dot(z_ref[:, :R], d_ref[...])).astype(BF16)
 
 

time: 132 us -> 132 us (level)
  no operation moved by 1% of the time
where the time goes in v6:
time: 132 us; the launch traced here: 131 us
  blocking collectives  52.6 us (40%)
  starting transfers between devices  41 us (31%)
  waiting for transfers between devices  17.2 us (13%)
  Pallas kernels  16.5 us (12%)
  local copies, waits for them, and re-layouts  2.3 us (2%)
    ppermute x9, starting transfers between devices, move(): return lax.ppermute(value, 'row', way)  38.1 us
    all_to_all x1, blocking collectives, local(): lax.all_to_all(keep.reshape(4, quarter, width), 'row', 0, 0, tiled=True,...  19.2 us
    all_gather x1, blocking collectives, local(): lax.all_gather(both, 'row', axis=1, tiled=True, axis_index_groups=same_core)  16.8 us
    pallas_call x9, Pallas kernels, whole(): pl.pallas_call(kernel, in_specs=[smem if x.ndim == 1 else vmem for x in o...  16.5 us
    all_gather x1, blocking collectives, local(): nodes = lax.all_gather(part, 'leaf', axis=0, axis_index_groups=window)  14.3 us
    ppermute x9, waiting for transfers between devices, move(): return lax.ppermute(value, 'row', way)  13.5 us
    ppermute x1, waiting for transfers between devices, local(): sibling = lax.ppermute(piece, 'leaf', [(i, i ^ 1) for i in range(leaves)])  3.66 us
    ppermute x1, starting transfers between devices, local(): sibling = lax.ppermute(piece, 'leaf', [(i, i ^ 1) for i in range(leaves)])  2.85 us
  transfers between devices with their start and end apart: 10, of which 7 were waited for; matrix products, arithmetic and copies ran while one was open for 0% of the time, Pallas kernels for 5%

profile of v6, /device:TPU:6, one launch (start us, length us, event | category | flops | bytes accessed | tf_op | source)
XLA Modules:
  0.0 131.0 jit_solution(13740385544829454158)
XLA Ops:
  1.1 1.9 %collective-permute-start = (bf16[512,512]{1,0:T(8,128)(2,1)S(1)}, bf16[512,512]{1,0:T(8,128)(2,1)S(1)}, u32[]{:S(2)}, u32[]{:S(2)}) collective-permute-start(bf16[512,512]{1,0:T(8,128)(2,1)S(1)} %pad_maximum_fusion.own_ref), channel_id=1, source_target_pairs={{0,1},{1,0},{2,3},{3,2},{4,5},{5,4},{6,7},{7,6},{8,9},{9,8},{10,11... | collective-permute-start | bytes 1572872 | tf_op jit(solution)/shard_map/ppermute | solution.py:196
  3.0 6.1 %collective-permute-start.2 = (bf16[512,512]{1,0:T(8,128)(2,1)S(1)}, bf16[512,512]{1,0:T(8,128)(2,1)S(1)}, u32[]{:S(2)}, u32[]{:S(2)}) collective-permute-start(bf16[512,512]{1,0:T(8,128)(2,1)S(1)} %pad_maximum_fusion.own_ref), channel_id=1, source_target_pairs={{0,2},{1,7},{2,4},{3,1},{4,6},{5,3},{6,0},{7,5},{8,10},{9,15},{10,... | collective-permute-start | bytes 1572872 | tf_op jit(solution)/shard_map/ppermute | solution.py:196
  9.3 2.2 %copy-done = bf16[1,512,4096]{2,1,0:T(8,128)(2,1)S(1)} copy-done((bf16[1,512,4096]{2,1,0:T(8,128)(2,1)S(1)}, bf16[1,512,4096]{2,1,0:T(8,128)(2,1)}, u32[]{:S(2)}) %copy-start) | copy-done | bytes 4194328
  13.5 7.3 %collective-permute-start.1 = (bf16[512,512]{1,0:T(8,128)(2,1)S(1)}, bf16[512,512]{1,0:T(8,128)(2,1)S(1)}, u32[]{:S(2)}, u32[]{:S(2)}) collective-permute-start(bf16[512,512]{1,0:T(8,128)(2,1)S(1)} %collective-permute-done.refs_0_), channel_id=1, source_target_pairs={{0,2},{1,7},{2,4},{3,1},{4,6},{5,3},{6,0},{7,5},{8,10},{9,15},{10,... | collective-permute-start | bytes 1572872 | tf_op jit(solution)/shard_map/ppermute | solution.py:196
  21.3 13.0 %collective-permute-start.4 = (bf16[512,512]{1,0:T(8,128)(2,1)S(1)}, bf16[512,512]{1,0:T(8,128)(2,1)S(1)}, u32[]{:S(2)}, u32[]{:S(2)}) collective-permute-start(bf16[512,512]{1,0:T(8,128)(2,1)S(1)} %collective-permute-done.2.refs_0_), channel_id=1, source_target_pairs={{0,2},{1,7},{2,4},{3,1},{4,6},{5,3},{6,0},{7,5},{8,10},{9,15},{10,... | collective-permute-start | bytes 1572872 | tf_op jit(solution)/shard_map/ppermute | solution.py:196
  35.3 1.9 %collective-permute-start.6 = (bf16[512,512]{1,0:T(8,128)(2,1)S(1)}, bf16[512,512]{1,0:T(8,128)(2,1)S(1)}, u32[]{:S(2)}, u32[]{:S(2)}) collective-permute-start(bf16[512,512]{1,0:T(8,128)(2,1)S(1)} %collective-permute-done.2.refs_0_), channel_id=1, source_target_pairs={{0,1},{1,0},{2,3},{3,2},{4,5},{5,4},{6,7},{7,6},{8,9},{9,8},{10,11... | collective-permute-start | bytes 1572872 | tf_op jit(solution)/shard_map/ppermute | solution.py:196
  37.2 3.2 %collective-permute-done.1.refs_0_ = bf16[512,512]{1,0:T(8,128)(2,1)S(1)} collective-permute-done((bf16[512,512]{1,0:T(8,128)(2,1)S(1)}, bf16[512,512]{1,0:T(8,128)(2,1)S(1)}, u32[]{:S(2)}, u32[]{:S(2)}) %collective-permute-start.1) | collective-permute-done | bytes 524320 | tf_op jit(solution)/shard_map/ppermute | solution.py:196
  41.4 2.1 %collective-permute-start.3 = (bf16[512,512]{1,0:T(8,128)(2,1)S(1)}, bf16[512,512]{1,0:T(8,128)(2,1)S(1)}, u32[]{:S(2)}, u32[]{:S(2)}) collective-permute-start(bf16[512,512]{1,0:T(8,128)(2,1)S(1)} %collective-permute-done.1.refs_0_), channel_id=1, source_target_pairs={{0,1},{1,0},{2,3},{3,2},{4,5},{5,4},{6,7},{7,6},{8,9},{9,8},{10,11... | collective-permute-start | bytes 1572872 | tf_op jit(solution)/shard_map/ppermute | solution.py:196
  43.5 6.2 %collective-permute-done.4.refs_1_ = bf16[512,512]{1,0:T(8,128)(2,1)S(1)} collective-permute-done((bf16[512,512]{1,0:T(8,128)(2,1)S(1)}, bf16[512,512]{1,0:T(8,128)(2,1)S(1)}, u32[]{:S(2)}, u32[]{:S(2)}) %collective-permute-start.4) | collective-permute-done | bytes 524320 | tf_op jit(solution)/shard_map/ppermute | solution.py:196
  49.7 1.9 %collective-permute-start.5 = (bf16[512,512]{1,0:T(8,128)(2,1)S(1)}, bf16[512,512]{1,0:T(8,128)(2,1)S(1)}, u32[]{:S(2)}, u32[]{:S(2)}) collective-permute-start(bf16[512,512]{1,0:T(8,128)(2,1)S(1)} %collective-permute-done.4.refs_1_), channel_id=1, source_target_pairs={{0,1},{1,0},{2,3},{3,2},{4,5},{5,4},{6,7},{7,6},{8,9},{9,8},{10,11... | collective-permute-start | bytes 1572872 | tf_op jit(solution)/shard_map/ppermute | solution.py:196
  51.6 1.2 shard_map.50.before_ref
  53.5 1.8 %shard_map.51 = (f32[512,512]{1,0:T(8,128)S(1)}, f32[192,512]{1,0:T(8,128)S(1)}, f32[192,512]{1,0:T(8,128)S(1)}) custom-call(s32[11]{0:T(128)S(1)} %stack.56.where_ref, bf16[512,4096]{1,0:T(8,128)(2,1)S(1)} %bitcast.26, bf16[512,512]{1,0:T(8,128)(2,1)S(1)} %collective-permute-done.3.next_near_ref, bf16[512,512]{1,0:T(8,128)(2,1)S(1)} %collective-permute-done.5.far_ref, ...), custom_call_target="tpu_custom_call" | custom-call | flops 1000000000 | bytes 10000000 | tf_op jit(solution)/shard_map/pallas_call | solution.py:171
  55.3 2.0 %collective-permute-start.7 = (f32[192,512]{1,0:T(8,128)S(1)}, f32[192,512]{1,0:T(8,128)S(1)}, u32[]{:S(2)}, u32[]{:S(2)}) collective-permute-start(f32[192,512]{1,0:T(8,128)S(1)} %get-tuple-element.23), channel_id=1, source_target_pairs={{0,1},{1,0},{2,3},{3,2},{4,5},{5,4},{6,7},{7,6},{8,9},{9,8},{10,11... | collective-permute-start | bytes 1179656 | tf_op jit(solution)/shard_map/ppermute | solution.py:196
  57.4 1.6 %collective-permute-done.7 = f32[192,512]{1,0:T(8,128)S(1)} collective-permute-done((f32[192,512]{1,0:T(8,128)S(1)}, f32[192,512]{1,0:T(8,128)S(1)}, u32[]{:S(2)}, u32[]{:S(2)}) %collective-permute-start.7) | collective-permute-done | bytes 393248 | tf_op jit(solution)/shard_map/ppermute | solution.py:196
  59.0 19.2 %all_to_all.5 = f32[4,48,512]{2,1,0:T(8,128)S(1)} all-to-all(f32[4,48,512]{2,1,0:T(8,128)S(1)} %bitcast.31), channel_id=1, replica_groups={{0,2,4,6},{1,3,5,7},{8,10,12,14},{9,11,13,15},{16,18,20,22},{17,19,21,2..., dimensions={0} | all-to-all | bytes 786432 | tf_op jit(solution)/shard_map/all_to_all | solution.py:231
  78.3 2.8 %collective-permute-start.8 = (f32[48,512]{1,0:T(8,128)S(1)}, f32[48,512]{1,0:T(8,128)S(1)}, u32[]{:S(2)}, u32[]{:S(2)}) collective-permute-start(f32[48,512]{1,0:T(8,128)S(1)} %reduce_sum.9), channel_id=1, source_target_pairs={{0,8},{8,0},{16,24},{24,16},{32,40},{40,32},{48,56},{56,48},{64,72... | collective-permute-start | bytes 294920 | tf_op jit(solution)/shard_map/ppermute | solution.py:233
  81.1 3.7 %collective-permute-done.8 = f32[48,512]{1,0:T(8,128)S(1)} collective-permute-done((f32[48,512]{1,0:T(8,128)S(1)}, f32[48,512]{1,0:T(8,128)S(1)}, u32[]{:S(2)}, u32[]{:S(2)}) %collective-permute-start.8) | collective-permute-done | bytes 98336 | tf_op jit(solution)/shard_map/ppermute | solution.py:233
  84.8 16.8 %all_gather.15.own_ref = f32[2,192,512]{2,1,0:T(8,128)S(1)} all-gather(f32[2,48,512]{2,1,0:T(8,128)S(1)} %pad_maximum_fusion.1), channel_id=1, replica_groups={{0,2,4,6},{1,3,5,7},{8,10,12,14},{9,11,13,15},{16,18,20,22},{17,19,21,2..., dimensions={1}, use_global_device_ids=true | all-gather | bytes 983040 | tf_op jit(solution)/shard_map/all_gather | solution.py:235
  101.6 2.2 %all-gather = f32[4,64,512]{2,1,0:T(8,128)S(1)} all-gather(f32[2,64,512]{2,1,0:T(8,128)S(1)} %slice.4), channel_id=2, replica_groups={{0,1},{2,3},{4,5},{6,7},{8,9},{10,11},{12,13},{14,15},{16,17},{18,19},{..., dimensions={0}, use_global_device_ids=true | all-gather | bytes 786432 | tf_op jit(solution)/shard_map/all_gather | solution.py:238
  103.8 2.1 %shard_map.52 = (f32[128,384]{1,0:T(8,128)S(1)}, f32[128,384]{1,0:T(8,128)S(1)}) custom-call(f32[2,192,512]{2,1,0:T(8,128)S(1)} %all_gather.15.own_ref, f32[2,2,64,512]{3,2,1,0:T(8,128)S(1)} %bitcast.29), custom_call_target="tpu_custom_call" | custom-call | flops 1000000000 | bytes 10000000 | tf_op jit(solution)/shard_map/pallas_call | solution.py:171
  106.0 14.3 %all-gather.1 = f32[512,384]{1,0:T(8,128)S(1)} all-gather(f32[128,384]{1,0:T(8,128)S(1)} %get-tuple-element.24), channel_id=3, replica_groups={{0,16,32,48},{8,24,40,56},{64,80,96,112},{72,88,104,120},{128,144,160,1..., dimensions={0}, use_global_device_ids=true | all-gather | bytes 983040 | tf_op jit(solution)/shard_map/all_gather | solution.py:246
  120.3 1.9 %collective-permute-start.9 = (f32[4,128,384]{2,1,0:T(8,128)S(1)}, f32[4,128,384]{2,1,0:T(8,128)S(1)}, u32[]{:S(2)}, u32[]{:S(2)}) collective-permute-start(f32[4,128,384]{2,1,0:T(8,128)S(1)} %bitcast.27), channel_id=1, source_target_pairs={{0,1},{1,0},{2,3},{3,2},{4,5},{5,4},{6,7},{7,6},{8,9},{9,8},{10,11... | collective-permute-start | bytes 2359304 | tf_op jit(solution)/shard_map/ppermute | solution.py:196
  123.0 1.5 %collective-permute-done.9.other_ref = f32[4,128,384]{2,1,0:T(8,128)S(1)} collective-permute-done((f32[4,128,384]{2,1,0:T(8,128)S(1)}, f32[4,128,384]{2,1,0:T(8,128)S(1)}, u32[]{:S(2)}, u32[]{:S(2)}) %collective-permute-start.9) | collective-permute-done | bytes 786464 | tf_op jit(solution)/shard_map/ppermute | solution.py:196
  124.5 6.6 %shard_map.54 = bf16[512,128]{1,0:T(8,128)(2,1)} custom-call(s32[11]{0:T(128)S(1)} %stack.56.where_ref, f32[4,128,384]{2,1,0:T(8,128)S(1)} %bitcast.28, f32[4,128,384]{2,1,0:T(8,128)S(1)} %collective-permute-done.9.other_ref, f32[512,384]{1,0:T(8,128)S(1)} %shard_map.53.refs_0_), custom_call_target="tpu_custom_call" | custom-call | flops 1000000000 | bytes 10000000 | tf_op jit(solution)/shard_map/pallas_call | solution.py:171
  (19 shorter events, 7.1 us)
Async XLA Ops:
  1.1 11.4 %collective-permute-start = (bf16[512,512]{1,0:T(8,128)(2,1)S(1)}, bf16[512,512]{1,0:T(8,128)(2,1)S(1)}, u32[]{:S(2)}, u32[]{:S(2)}) collective-permute-start(bf16[512,512]{1,0:T(8,128)(2,1)S(1)} %pad_maximum_fusion.own_ref), channel_id=1, source_target_pairs={{0,1},{1,0},{2,3},{3,2},{4,5},{5,4},{6,7},{7,6},{8,9},{9,8},{10,11... | collective-permute-start | bytes 1572872 | tf_op jit(solution)/shard_map/ppermute | solution.py:196
  3.0 18.2 %collective-permute-start.2 = (bf16[512,512]{1,0:T(8,128)(2,1)S(1)}, bf16[512,512]{1,0:T(8,128)(2,1)S(1)}, u32[]{:S(2)}, u32[]{:S(2)}) collective-permute-start(bf16[512,512]{1,0:T(8,128)(2,1)S(1)} %pad_maximum_fusion.own_ref), channel_id=1, source_target_pairs={{0,2},{1,7},{2,4},{3,1},{4,6},{5,3},{6,0},{7,5},{8,10},{9,15},{10,... | collective-permute-start | bytes 1572872 | tf_op jit(solution)/shard_map/ppermute | solution.py:196
  9.3 2.2 %copy-start = (bf16[1,512,4096]{2,1,0:T(8,128)(2,1)S(1)}, bf16[1,512,4096]{2,1,0:T(8,128)(2,1)}, u32[]{:S(2)}) copy-start(bf16[1,512,4096]{2,1,0:T(8,128)(2,1)} %param.4) | copy-start | bytes 12582916
  13.5 26.9 %collective-permute-start.1 = (bf16[512,512]{1,0:T(8,128)(2,1)S(1)}, bf16[512,512]{1,0:T(8,128)(2,1)S(1)}, u32[]{:S(2)}, u32[]{:S(2)}) collective-permute-start(bf16[512,512]{1,0:T(8,128)(2,1)S(1)} %collective-permute-done.refs_0_), channel_id=1, source_target_pairs={{0,2},{1,7},{2,4},{3,1},{4,6},{5,3},{6,0},{7,5},{8,10},{9,15},{10,... | collective-permute-start | bytes 1572872 | tf_op jit(solution)/shard_map/ppermute | solution.py:196
  21.3 28.4 %collective-permute-start.4 = (bf16[512,512]{1,0:T(8,128)(2,1)S(1)}, bf16[512,512]{1,0:T(8,128)(2,1)S(1)}, u32[]{:S(2)}, u32[]{:S(2)}) collective-permute-start(bf16[512,512]{1,0:T(8,128)(2,1)S(1)} %collective-permute-done.2.refs_0_), channel_id=1, source_target_pairs={{0,2},{1,7},{2,4},{3,1},{4,6},{5,3},{6,0},{7,5},{8,10},{9,15},{10,... | collective-permute-start | bytes 1572872 | tf_op jit(solution)/shard_map/ppermute | solution.py:196
  35.3 16.4 %collective-permute-start.6 = (bf16[512,512]{1,0:T(8,128)(2,1)S(1)}, bf16[512,512]{1,0:T(8,128)(2,1)S(1)}, u32[]{:S(2)}, u32[]{:S(2)}) collective-permute-start(bf16[512,512]{1,0:T(8,128)(2,1)S(1)} %collective-permute-done.2.refs_0_), channel_id=1, source_target_pairs={{0,1},{1,0},{2,3},{3,2},{4,5},{5,4},{6,7},{7,6},{8,9},{9,8},{10,11... | collective-permute-start | bytes 1572872 | tf_op jit(solution)/shard_map/ppermute | solution.py:196
  41.4 12.1 %copy-start.1 = (bf16[1,512,384]{2,1,0:T(8,128)(2,1)S(1)}, bf16[1,512,384]{2,1,0:T(8,128)(2,1)}, u32[]{:S(2)}) copy-start(bf16[1,512,384]{2,1,0:T(8,128)(2,1)} %param.7) | copy-start | bytes 1179652
  41.4 11.5 %collective-permute-start.3 = (bf16[512,512]{1,0:T(8,128)(2,1)S(1)}, bf16[512,512]{1,0:T(8,128)(2,1)S(1)}, u32[]{:S(2)}, u32[]{:S(2)}) collective-permute-start(bf16[512,512]{1,0:T(8,128)(2,1)S(1)} %collective-permute-done.1.refs_0_), channel_id=1, source_target_pairs={{0,1},{1,0},{2,3},{3,2},{4,5},{5,4},{6,7},{7,6},{8,9},{9,8},{10,11... | collective-permute-start | bytes 1572872 | tf_op jit(solution)/shard_map/ppermute | solution.py:196
  49.7 3.8 %collective-permute-start.5 = (bf16[512,512]{1,0:T(8,128)(2,1)S(1)}, bf16[512,512]{1,0:T(8,128)(2,1)S(1)}, u32[]{:S(2)}, u32[]{:S(2)}) collective-permute-start(bf16[512,512]{1,0:T(8,128)(2,1)S(1)} %collective-permute-done.4.refs_1_), channel_id=1, source_target_pairs={{0,1},{1,0},{2,3},{3,2},{4,5},{5,4},{6,7},{7,6},{8,9},{9,8},{10,11... | collective-permute-start | bytes 1572872 | tf_op jit(solution)/shard_map/ppermute | solution.py:196
  55.3 3.6 %collective-permute-start.7 = (f32[192,512]{1,0:T(8,128)S(1)}, f32[192,512]{1,0:T(8,128)S(1)}, u32[]{:S(2)}, u32[]{:S(2)}) collective-permute-start(f32[192,512]{1,0:T(8,128)S(1)} %get-tuple-element.23), channel_id=1, source_target_pairs={{0,1},{1,0},{2,3},{3,2},{4,5},{5,4},{6,7},{7,6},{8,9},{9,8},{10,11... | collective-permute-start | bytes 1179656 | tf_op jit(solution)/shard_map/ppermute | solution.py:196
  78.3 6.5 %collective-permute-start.8 = (f32[48,512]{1,0:T(8,128)S(1)}, f32[48,512]{1,0:T(8,128)S(1)}, u32[]{:S(2)}, u32[]{:S(2)}) collective-permute-start(f32[48,512]{1,0:T(8,128)S(1)} %reduce_sum.9), channel_id=1, source_target_pairs={{0,8},{8,0},{16,24},{24,16},{32,40},{40,32},{48,56},{56,48},{64,72... | collective-permute-start | bytes 294920 | tf_op jit(solution)/shard_map/ppermute | solution.py:233
  120.3 4.2 %collective-permute-start.9 = (f32[4,128,384]{2,1,0:T(8,128)S(1)}, f32[4,128,384]{2,1,0:T(8,128)S(1)}, u32[]{:S(2)}, u32[]{:S(2)}) collective-permute-start(f32[4,128,384]{2,1,0:T(8,128)S(1)} %bitcast.27), channel_id=1, source_target_pairs={{0,1},{1,0},{2,3},{3,2},{4,5},{5,4},{6,7},{7,6},{8,9},{9,8},{10,11... | collective-permute-start | bytes 2359304 | tf_op jit(solution)/shard_map/ppermute | solution.py:196

commit v7 on v6

--- a/solution.py
+++ b/solution.py
@@ -44,8 +44,8 @@
 
 
 def solve(systems, rounds=2):
-    left = jnp.float32(0)
-    grown = jnp.float32(0)
+    left = jnp.zeros((R, R), F32)
+    grown = jnp.zeros((R, R), F32)
     for s, right, c_ref, p_ref in systems:
         c = right + dot(s, right)
         p = dot(s, s)
@@ -54,21 +54,22 @@
             p = dot(p, p)
         c_ref[...] = c
         p_ref[...] = p
-        left = jnp.maximum(left, jnp.sum(p * p))
-        grown = jnp.maximum(grown, jnp.sum(s * s))
-    good = jnp.logical_and(left < 0.25, grown < 64.0)
+        left = left + p * p
+        grown = grown + s * s
+    left = jnp.sum(left)
+    good = jnp.logical_and(left < 0.25, jnp.sum(grown) < 64.0)
 
     @pl.when(good)
     def _():
         def more(_):
-            size = jnp.float32(0)
+            size = jnp.zeros((R, R), F32)
             for _, _, c_ref, p_ref in systems:
                 q = p_ref[...]
                 c_ref[...] = c_ref[...] + dot(q, c_ref[...])
                 q = dot(q, q)
                 p_ref[...] = q
-                size = jnp.maximum(size, jnp.sum(q * q))
-            return size
+                size = size + q * q
+            return jnp.sum(size)
 
         lax.while_loop(lambda size: size > 1e-13, more, left)
 

time: 132 us -> 132 us (level)
  no operation moved by 1% of the time
where the time goes in v7:
time: 132 us; the launch traced here: 131 us
  blocking collectives  52.6 us (40%)
  starting transfers between devices  41 us (31%)
  waiting for transfers between devices  17.2 us (13%)
  Pallas kernels  16.4 us (12%)
  local copies, waits for them, and re-layouts  2.3 us (2%)
    ppermute x9, starting transfers between devices, move(): return lax.ppermute(value, 'row', way)  38.1 us
    all_to_all x1, blocking collectives, local(): lax.all_to_all(keep.reshape(4, quarter, width), 'row', 0, 0, tiled=True,...  19.2 us
    all_gather x1, blocking collectives, local(): lax.all_gather(both, 'row', axis=1, tiled=True, axis_index_groups=same_core)  16.8 us
    pallas_call x9, Pallas kernels, whole(): pl.pallas_call(kernel, in_specs=[smem if x.ndim == 1 else vmem for x in o...  16.4 us
    all_gather x1, blocking collectives, local(): nodes = lax.all_gather(part, 'leaf', axis=0, axis_index_groups=window)  14.3 us
    ppermute x9, waiting for transfers between devices, move(): return lax.ppermute(value, 'row', way)  13.5 us
    ppermute x1, waiting for transfers between devices, local(): sibling = lax.ppermute(piece, 'leaf', [(i, i ^ 1) for i in range(leaves)])  3.66 us
    ppermute x1, starting transfers between devices, local(): sibling = lax.ppermute(piece, 'leaf', [(i, i ^ 1) for i in range(leaves)])  2.85 us
  transfers between devices with their start and end apart: 10, of which 7 were waited for; matrix products, arithmetic and copies ran while one was open for 0% of the time, Pallas kernels for 5%

profile of v7, /device:TPU:6, one launch (start us, length us, event | category | flops | bytes accessed | tf_op | source)
XLA Modules:
  0.0 131.0 jit_solution(7892569593292014862)
XLA Ops:
  1.1 1.9 %collective-permute-start = (bf16[512,512]{1,0:T(8,128)(2,1)S(1)}, bf16[512,512]{1,0:T(8,128)(2,1)S(1)}, u32[]{:S(2)}, u32[]{:S(2)}) collective-permute-start(bf16[512,512]{1,0:T(8,128)(2,1)S(1)} %pad_maximum_fusion.own_ref), channel_id=1, source_target_pairs={{0,1},{1,0},{2,3},{3,2},{4,5},{5,4},{6,7},{7,6},{8,9},{9,8},{10,11... | collective-permute-start | bytes 1572872 | tf_op jit(solution)/shard_map/ppermute | solution.py:197
  3.0 6.1 %collective-permute-start.2 = (bf16[512,512]{1,0:T(8,128)(2,1)S(1)}, bf16[512,512]{1,0:T(8,128)(2,1)S(1)}, u32[]{:S(2)}, u32[]{:S(2)}) collective-permute-start(bf16[512,512]{1,0:T(8,128)(2,1)S(1)} %pad_maximum_fusion.own_ref), channel_id=1, source_target_pairs={{0,2},{1,7},{2,4},{3,1},{4,6},{5,3},{6,0},{7,5},{8,10},{9,15},{10,... | collective-permute-start | bytes 1572872 | tf_op jit(solution)/shard_map/ppermute | solution.py:197
  9.3 2.2 %copy-done = bf16[1,512,4096]{2,1,0:T(8,128)(2,1)S(1)} copy-done((bf16[1,512,4096]{2,1,0:T(8,128)(2,1)S(1)}, bf16[1,512,4096]{2,1,0:T(8,128)(2,1)}, u32[]{:S(2)}) %copy-start) | copy-done | bytes 4194328
  13.5 7.3 %collective-permute-start.1 = (bf16[512,512]{1,0:T(8,128)(2,1)S(1)}, bf16[512,512]{1,0:T(8,128)(2,1)S(1)}, u32[]{:S(2)}, u32[]{:S(2)}) collective-permute-start(bf16[512,512]{1,0:T(8,128)(2,1)S(1)} %collective-permute-done.refs_0_), channel_id=1, source_target_pairs={{0,2},{1,7},{2,4},{3,1},{4,6},{5,3},{6,0},{7,5},{8,10},{9,15},{10,... | collective-permute-start | bytes 1572872 | tf_op jit(solution)/shard_map/ppermute | solution.py:197
  21.3 13.0 %collective-permute-start.4 = (bf16[512,512]{1,0:T(8,128)(2,1)S(1)}, bf16[512,512]{1,0:T(8,128)(2,1)S(1)}, u32[]{:S(2)}, u32[]{:S(2)}) collective-permute-start(bf16[512,512]{1,0:T(8,128)(2,1)S(1)} %collective-permute-done.2.refs_0_), channel_id=1, source_target_pairs={{0,2},{1,7},{2,4},{3,1},{4,6},{5,3},{6,0},{7,5},{8,10},{9,15},{10,... | collective-permute-start | bytes 1572872 | tf_op jit(solution)/shard_map/ppermute | solution.py:197
  35.3 1.9 %collective-permute-start.6 = (bf16[512,512]{1,0:T(8,128)(2,1)S(1)}, bf16[512,512]{1,0:T(8,128)(2,1)S(1)}, u32[]{:S(2)}, u32[]{:S(2)}) collective-permute-start(bf16[512,512]{1,0:T(8,128)(2,1)S(1)} %collective-permute-done.2.refs_0_), channel_id=1, source_target_pairs={{0,1},{1,0},{2,3},{3,2},{4,5},{5,4},{6,7},{7,6},{8,9},{9,8},{10,11... | collective-permute-start | bytes 1572872 | tf_op jit(solution)/shard_map/ppermute | solution.py:197
  37.2 3.2 %collective-permute-done.1.refs_0_ = bf16[512,512]{1,0:T(8,128)(2,1)S(1)} collective-permute-done((bf16[512,512]{1,0:T(8,128)(2,1)S(1)}, bf16[512,512]{1,0:T(8,128)(2,1)S(1)}, u32[]{:S(2)}, u32[]{:S(2)}) %collective-permute-start.1) | collective-permute-done | bytes 524320 | tf_op jit(solution)/shard_map/ppermute | solution.py:197
  41.4 2.1 %collective-permute-start.3 = (bf16[512,512]{1,0:T(8,128)(2,1)S(1)}, bf16[512,512]{1,0:T(8,128)(2,1)S(1)}, u32[]{:S(2)}, u32[]{:S(2)}) collective-permute-start(bf16[512,512]{1,0:T(8,128)(2,1)S(1)} %collective-permute-done.1.refs_0_), channel_id=1, source_target_pairs={{0,1},{1,0},{2,3},{3,2},{4,5},{5,4},{6,7},{7,6},{8,9},{9,8},{10,11... | collective-permute-start | bytes 1572872 | tf_op jit(solution)/shard_map/ppermute | solution.py:197
  43.5 6.2 %collective-permute-done.4.refs_1_ = bf16[512,512]{1,0:T(8,128)(2,1)S(1)} collective-permute-done((bf16[512,512]{1,0:T(8,128)(2,1)S(1)}, bf16[512,512]{1,0:T(8,128)(2,1)S(1)}, u32[]{:S(2)}, u32[]{:S(2)}) %collective-permute-start.4) | collective-permute-done | bytes 524320 | tf_op jit(solution)/shard_map/ppermute | solution.py:197
  49.7 1.9 %collective-permute-start.5 = (bf16[512,512]{1,0:T(8,128)(2,1)S(1)}, bf16[512,512]{1,0:T(8,128)(2,1)S(1)}, u32[]{:S(2)}, u32[]{:S(2)}) collective-permute-start(bf16[512,512]{1,0:T(8,128)(2,1)S(1)} %collective-permute-done.4.refs_1_), channel_id=1, source_target_pairs={{0,1},{1,0},{2,3},{3,2},{4,5},{5,4},{6,7},{7,6},{8,9},{9,8},{10,11... | collective-permute-start | bytes 1572872 | tf_op jit(solution)/shard_map/ppermute | solution.py:197
  51.6 1.2 shard_map.50.before_ref
  53.5 1.8 %shard_map.51 = (f32[512,512]{1,0:T(8,128)S(1)}, f32[192,512]{1,0:T(8,128)S(1)}, f32[192,512]{1,0:T(8,128)S(1)}) custom-call(s32[11]{0:T(128)S(1)} %stack.56.where_ref, bf16[512,4096]{1,0:T(8,128)(2,1)S(1)} %bitcast.26, bf16[512,512]{1,0:T(8,128)(2,1)S(1)} %collective-permute-done.3.next_near_ref, bf16[512,512]{1,0:T(8,128)(2,1)S(1)} %collective-permute-done.5.far_ref, ...), custom_call_target="tpu_custom_call" | custom-call | flops 1000000000 | bytes 10000000 | tf_op jit(solution)/shard_map/pallas_call | solution.py:172
  55.3 2.0 %collective-permute-start.7 = (f32[192,512]{1,0:T(8,128)S(1)}, f32[192,512]{1,0:T(8,128)S(1)}, u32[]{:S(2)}, u32[]{:S(2)}) collective-permute-start(f32[192,512]{1,0:T(8,128)S(1)} %get-tuple-element.23), channel_id=1, source_target_pairs={{0,1},{1,0},{2,3},{3,2},{4,5},{5,4},{6,7},{7,6},{8,9},{9,8},{10,11... | collective-permute-start | bytes 1179656 | tf_op jit(solution)/shard_map/ppermute | solution.py:197
  57.4 1.6 %collective-permute-done.7 = f32[192,512]{1,0:T(8,128)S(1)} collective-permute-done((f32[192,512]{1,0:T(8,128)S(1)}, f32[192,512]{1,0:T(8,128)S(1)}, u32[]{:S(2)}, u32[]{:S(2)}) %collective-permute-start.7) | collective-permute-done | bytes 393248 | tf_op jit(solution)/shard_map/ppermute | solution.py:197
  59.0 19.2 %all_to_all.5 = f32[4,48,512]{2,1,0:T(8,128)S(1)} all-to-all(f32[4,48,512]{2,1,0:T(8,128)S(1)} %bitcast.31), channel_id=1, replica_groups={{0,2,4,6},{1,3,5,7},{8,10,12,14},{9,11,13,15},{16,18,20,22},{17,19,21,2..., dimensions={0} | all-to-all | bytes 786432 | tf_op jit(solution)/shard_map/all_to_all | solution.py:232
  78.3 2.8 %collective-permute-start.8 = (f32[48,512]{1,0:T(8,128)S(1)}, f32[48,512]{1,0:T(8,128)S(1)}, u32[]{:S(2)}, u32[]{:S(2)}) collective-permute-start(f32[48,512]{1,0:T(8,128)S(1)} %reduce_sum.9), channel_id=1, source_target_pairs={{0,8},{8,0},{16,24},{24,16},{32,40},{40,32},{48,56},{56,48},{64,72... | collective-permute-start | bytes 294920 | tf_op jit(solution)/shard_map/ppermute | solution.py:234
  81.1 3.7 %collective-permute-done.8 = f32[48,512]{1,0:T(8,128)S(1)} collective-permute-done((f32[48,512]{1,0:T(8,128)S(1)}, f32[48,512]{1,0:T(8,128)S(1)}, u32[]{:S(2)}, u32[]{:S(2)}) %collective-permute-start.8) | collective-permute-done | bytes 98336 | tf_op jit(solution)/shard_map/ppermute | solution.py:234
  84.8 16.8 %all_gather.15.own_ref = f32[2,192,512]{2,1,0:T(8,128)S(1)} all-gather(f32[2,48,512]{2,1,0:T(8,128)S(1)} %pad_maximum_fusion.1), channel_id=1, replica_groups={{0,2,4,6},{1,3,5,7},{8,10,12,14},{9,11,13,15},{16,18,20,22},{17,19,21,2..., dimensions={1}, use_global_device_ids=true | all-gather | bytes 983040 | tf_op jit(solution)/shard_map/all_gather | solution.py:236
  101.6 2.2 %all-gather = f32[4,64,512]{2,1,0:T(8,128)S(1)} all-gather(f32[2,64,512]{2,1,0:T(8,128)S(1)} %slice.4), channel_id=2, replica_groups={{0,1},{2,3},{4,5},{6,7},{8,9},{10,11},{12,13},{14,15},{16,17},{18,19},{..., dimensions={0}, use_global_device_ids=true | all-gather | bytes 786432 | tf_op jit(solution)/shard_map/all_gather | solution.py:239
  103.8 2.1 %shard_map.52 = (f32[128,384]{1,0:T(8,128)S(1)}, f32[128,384]{1,0:T(8,128)S(1)}) custom-call(f32[2,192,512]{2,1,0:T(8,128)S(1)} %all_gather.15.own_ref, f32[2,2,64,512]{3,2,1,0:T(8,128)S(1)} %bitcast.29), custom_call_target="tpu_custom_call" | custom-call | flops 1000000000 | bytes 10000000 | tf_op jit(solution)/shard_map/pallas_call | solution.py:172
  106.0 14.3 %all-gather.1 = f32[512,384]{1,0:T(8,128)S(1)} all-gather(f32[128,384]{1,0:T(8,128)S(1)} %get-tuple-element.24), channel_id=3, replica_groups={{0,16,32,48},{8,24,40,56},{64,80,96,112},{72,88,104,120},{128,144,160,1..., dimensions={0}, use_global_device_ids=true | all-gather | bytes 983040 | tf_op jit(solution)/shard_map/all_gather | solution.py:247
  120.3 1.9 %collective-permute-start.9 = (f32[4,128,384]{2,1,0:T(8,128)S(1)}, f32[4,128,384]{2,1,0:T(8,128)S(1)}, u32[]{:S(2)}, u32[]{:S(2)}) collective-permute-start(f32[4,128,384]{2,1,0:T(8,128)S(1)} %bitcast.27), channel_id=1, source_target_pairs={{0,1},{1,0},{2,3},{3,2},{4,5},{5,4},{6,7},{7,6},{8,9},{9,8},{10,11... | collective-permute-start | bytes 2359304 | tf_op jit(solution)/shard_map/ppermute | solution.py:197
  123.0 1.5 %collective-permute-done.9.other_ref = f32[4,128,384]{2,1,0:T(8,128)S(1)} collective-permute-done((f32[4,128,384]{2,1,0:T(8,128)S(1)}, f32[4,128,384]{2,1,0:T(8,128)S(1)}, u32[]{:S(2)}, u32[]{:S(2)}) %collective-permute-start.9) | collective-permute-done | bytes 786464 | tf_op jit(solution)/shard_map/ppermute | solution.py:197
  124.5 6.6 %shard_map.54 = bf16[512,128]{1,0:T(8,128)(2,1)} custom-call(s32[11]{0:T(128)S(1)} %stack.56.where_ref, f32[4,128,384]{2,1,0:T(8,128)S(1)} %bitcast.28, f32[4,128,384]{2,1,0:T(8,128)S(1)} %collective-permute-done.9.other_ref, f32[512,384]{1,0:T(8,128)S(1)} %shard_map.53.refs_0_), custom_call_target="tpu_custom_call" | custom-call | flops 1000000000 | bytes 10000000 | tf_op jit(solution)/shard_map/pallas_call | solution.py:172
  (19 shorter events, 7.1 us)
Async XLA Ops:
  1.1 11.4 %collective-permute-start = (bf16[512,512]{1,0:T(8,128)(2,1)S(1)}, bf16[512,512]{1,0:T(8,128)(2,1)S(1)}, u32[]{:S(2)}, u32[]{:S(2)}) collective-permute-start(bf16[512,512]{1,0:T(8,128)(2,1)S(1)} %pad_maximum_fusion.own_ref), channel_id=1, source_target_pairs={{0,1},{1,0},{2,3},{3,2},{4,5},{5,4},{6,7},{7,6},{8,9},{9,8},{10,11... | collective-permute-start | bytes 1572872 | tf_op jit(solution)/shard_map/ppermute | solution.py:197
  3.0 18.2 %collective-permute-start.2 = (bf16[512,512]{1,0:T(8,128)(2,1)S(1)}, bf16[512,512]{1,0:T(8,128)(2,1)S(1)}, u32[]{:S(2)}, u32[]{:S(2)}) collective-permute-start(bf16[512,512]{1,0:T(8,128)(2,1)S(1)} %pad_maximum_fusion.own_ref), channel_id=1, source_target_pairs={{0,2},{1,7},{2,4},{3,1},{4,6},{5,3},{6,0},{7,5},{8,10},{9,15},{10,... | collective-permute-start | bytes 1572872 | tf_op jit(solution)/shard_map/ppermute | solution.py:197
  9.3 2.2 %copy-start = (bf16[1,512,4096]{2,1,0:T(8,128)(2,1)S(1)}, bf16[1,512,4096]{2,1,0:T(8,128)(2,1)}, u32[]{:S(2)}) copy-start(bf16[1,512,4096]{2,1,0:T(8,128)(2,1)} %param.4) | copy-start | bytes 12582916
  13.5 26.9 %collective-permute-start.1 = (bf16[512,512]{1,0:T(8,128)(2,1)S(1)}, bf16[512,512]{1,0:T(8,128)(2,1)S(1)}, u32[]{:S(2)}, u32[]{:S(2)}) collective-permute-start(bf16[512,512]{1,0:T(8,128)(2,1)S(1)} %collective-permute-done.refs_0_), channel_id=1, source_target_pairs={{0,2},{1,7},{2,4},{3,1},{4,6},{5,3},{6,0},{7,5},{8,10},{9,15},{10,... | collective-permute-start | bytes 1572872 | tf_op jit(solution)/shard_map/ppermute | solution.py:197
  21.3 28.4 %collective-permute-start.4 = (bf16[512,512]{1,0:T(8,128)(2,1)S(1)}, bf16[512,512]{1,0:T(8,128)(2,1)S(1)}, u32[]{:S(2)}, u32[]{:S(2)}) collective-permute-start(bf16[512,512]{1,0:T(8,128)(2,1)S(1)} %collective-permute-done.2.refs_0_), channel_id=1, source_target_pairs={{0,2},{1,7},{2,4},{3,1},{4,6},{5,3},{6,0},{7,5},{8,10},{9,15},{10,... | collective-permute-start | bytes 1572872 | tf_op jit(solution)/shard_map/ppermute | solution.py:197
  35.3 16.4 %collective-permute-start.6 = (bf16[512,512]{1,0:T(8,128)(2,1)S(1)}, bf16[512,512]{1,0:T(8,128)(2,1)S(1)}, u32[]{:S(2)}, u32[]{:S(2)}) collective-permute-start(bf16[512,512]{1,0:T(8,128)(2,1)S(1)} %collective-permute-done.2.refs_0_), channel_id=1, source_target_pairs={{0,1},{1,0},{2,3},{3,2},{4,5},{5,4},{6,7},{7,6},{8,9},{9,8},{10,11... | collective-permute-start | bytes 1572872 | tf_op jit(solution)/shard_map/ppermute | solution.py:197
  41.4 12.1 %copy-start.1 = (bf16[1,512,384]{2,1,0:T(8,128)(2,1)S(1)}, bf16[1,512,384]{2,1,0:T(8,128)(2,1)}, u32[]{:S(2)}) copy-start(bf16[1,512,384]{2,1,0:T(8,128)(2,1)} %param.7) | copy-start | bytes 1179652
  41.4 11.5 %collective-permute-start.3 = (bf16[512,512]{1,0:T(8,128)(2,1)S(1)}, bf16[512,512]{1,0:T(8,128)(2,1)S(1)}, u32[]{:S(2)}, u32[]{:S(2)}) collective-permute-start(bf16[512,512]{1,0:T(8,128)(2,1)S(1)} %collective-permute-done.1.refs_0_), channel_id=1, source_target_pairs={{0,1},{1,0},{2,3},{3,2},{4,5},{5,4},{6,7},{7,6},{8,9},{9,8},{10,11... | collective-permute-start | bytes 1572872 | tf_op jit(solution)/shard_map/ppermute | solution.py:197
  49.7 3.8 %collective-permute-start.5 = (bf16[512,512]{1,0:T(8,128)(2,1)S(1)}, bf16[512,512]{1,0:T(8,128)(2,1)S(1)}, u32[]{:S(2)}, u32[]{:S(2)}) collective-permute-start(bf16[512,512]{1,0:T(8,128)(2,1)S(1)} %collective-permute-done.4.refs_1_), channel_id=1, source_target_pairs={{0,1},{1,0},{2,3},{3,2},{4,5},{5,4},{6,7},{7,6},{8,9},{9,8},{10,11... | collective-permute-start | bytes 1572872 | tf_op jit(solution)/shard_map/ppermute | solution.py:197
  55.3 3.6 %collective-permute-start.7 = (f32[192,512]{1,0:T(8,128)S(1)}, f32[192,512]{1,0:T(8,128)S(1)}, u32[]{:S(2)}, u32[]{:S(2)}) collective-permute-start(f32[192,512]{1,0:T(8,128)S(1)} %get-tuple-element.23), channel_id=1, source_target_pairs={{0,1},{1,0},{2,3},{3,2},{4,5},{5,4},{6,7},{7,6},{8,9},{9,8},{10,11... | collective-permute-start | bytes 1179656 | tf_op jit(solution)/shard_map/ppermute | solution.py:197
  78.3 6.5 %collective-permute-start.8 = (f32[48,512]{1,0:T(8,128)S(1)}, f32[48,512]{1,0:T(8,128)S(1)}, u32[]{:S(2)}, u32[]{:S(2)}) collective-permute-start(f32[48,512]{1,0:T(8,128)S(1)} %reduce_sum.9), channel_id=1, source_target_pairs={{0,8},{8,0},{16,24},{24,16},{32,40},{40,32},{48,56},{56,48},{64,72... | collective-permute-start | bytes 294920 | tf_op jit(solution)/shard_map/ppermute | solution.py:234
  120.3 4.2 %collective-permute-start.9 = (f32[4,128,384]{2,1,0:T(8,128)S(1)}, f32[4,128,384]{2,1,0:T(8,128)S(1)}, u32[]{:S(2)}, u32[]{:S(2)}) collective-permute-start(f32[4,128,384]{2,1,0:T(8,128)S(1)} %bitcast.27), channel_id=1, source_target_pairs={{0,1},{1,0},{2,3},{3,2},{4,5},{5,4},{6,7},{7,6},{8,9},{9,8},{10,11... | collective-permute-start | bytes 2359304 | tf_op jit(solution)/shard_map/ppermute | solution.py:197
